TPU v7x, 32 devices: a whole 2x2x4 slice. The times are simulated.
32 devices in a mesh: groups: 2 (over x), inst: 16 (over z, y, core).
Axes of the slice: x: 2, y: 2, z: 4, core: 2. Of those that a mesh axis runs over, the one named last changes fastest.
Arguments:
- hidden: bfloat16 [1024, 8192], P('groups', 'inst'), parts along dimension 0, may hold values from -64 to 64
- gain: float32 [8192], replicated, may hold values from 0.1 to 1.9
- w_query: bfloat16 [8192, 2048], P(None, 'inst'), may hold values from -0.0625 to 0.0625
- w_key: bfloat16 [8192, 256], P(None, 'inst'), may hold values from -0.0625 to 0.0625
- w_value: bfloat16 [8192, 256], P(None, 'inst'), may hold values from -0.0625 to 0.0625
- cache_pool: bfloat16 [1024, 64, 2, 256], P(('groups', 'inst')), parts along dimension 0, may hold values from -70 to 70
- prefix_len: int32 [4], P('groups'), parts along dimension 0, may hold values from 1024 to 4096, as said below
- hit_page: int32 [4, 64], P('groups'), parts along dimension 0, may hold values from -1 to 511, as said below
- decode_owner: int32 [32], P('groups'), parts along dimension 0, may hold values from 0 to 15, as said below
Outputs:
- attn_out: bfloat16 [1024, 2048], P('groups', 'inst'), parts along dimension 0
- decode_pages: bfloat16 [64, 64, 2, 128], P(('groups', 'inst')), parts along dimension 0
There are 2 independent parts, one for each index of `groups`. A program takes and returns all parts, laid end to end along the dimension named above; an argument that names none is the same for every part. Nothing has to cross between parts.
Inputs may be any that keep to these rules, and one draw needn't show every extreme that they name: `prefix_len`: the largest length is exactly 4096. `hit_page`: an entry is -1 exactly for page entries p >= ceil(prefix_len[r] / 64); other entries are distinct pool pages, held by holder id // 32. No holder holds more than 16 entries of the list, and some holder holds exactly 16. `decode_owner`: no device owns more than 2 rows, and some device owns exactly 2.
All inputs are finite; a program needn't handle non-finite values.
Results may differ from a plain program's by a relative error of at most 0.007.
The roundings to bfloat16 on the way count: a program that leaves them out, or rounds other values in their place, can miss the bound.
Values may be sent and summed in bfloat16 or wider, within the bound.
No kernel may reach another device: no remote copies, remote signals or barrier semaphores. Data moves between devices by JAX's collectives and lax.ppermute only.
A program may use at most 128 MiB of HBM per device.

v0:
```python
import jax
import jax.numpy as jnp
from jax import lax
from jax.sharding import PartitionSpec as P

OWN = 2


EPS = 1e-05
ROPE_BASE = 500000.0


def rotary_tables(positions, head_dim):
    half_dim = head_dim // 2
    freqs = ROPE_BASE ** (-(jnp.arange(half_dim, dtype=jnp.float32) * 2.0 / head_dim))
    angles = positions[:, None] * freqs[None, :]
    return (jnp.cos(angles), jnp.sin(angles))


def rotate_rows(values, cos_table, sin_table):
    half_dim = values.shape[-1] // 2
    first_half = values[..., :half_dim]
    second_half = values[..., half_dim:]
    return jnp.concatenate(
        [
            first_half * cos_table - second_half * sin_table,
            second_half * cos_table + first_half * sin_table,
        ],
        axis=-1,
    )


def rotate_cols(values, cos_table, sin_table):
    half_dim = values.shape[-2] // 2
    first_half = values[..., :half_dim, :]
    second_half = values[..., half_dim:, :]
    return jnp.concatenate(
        [
            first_half * cos_table - second_half * sin_table,
            second_half * cos_table + first_half * sin_table,
        ],
        axis=-2,
    )


def contract_last(left, right):
    return lax.dot_general(
        left, right, (((1,), (1,)), ((), ())), preferred_element_type=jnp.float32
    )


def contract_first(weights, rows):
    return lax.dot_general(
        weights, rows, (((0,), (1,)), ((), ())), preferred_element_type=jnp.float32
    )


def on_device(
    hidden, gain, w_query, w_key, w_value, cache_pool, prefix_len, hit_page, decode_owner
):
    my_index = lax.axis_index("inst")
    devices = lax.axis_size("inst")
    tok_count = hidden.shape[0]
    head_dim = w_query.shape[1]
    requests = prefix_len.shape[0]
    new_len = tok_count // requests
    gathered = lax.all_gather(hidden, "inst", axis=1, tiled=True)
    wide_vals = gathered.astype(jnp.float32)
    inverse_rms = lax.rsqrt(jnp.mean(wide_vals * wide_vals, axis=-1, keepdims=True) + EPS)
    normed = (wide_vals * inverse_rms * gain).astype(jnp.bfloat16)
    query = jnp.dot(normed, w_query, preferred_element_type=jnp.float32)
    key_cols = contract_first(w_key, normed)
    value_cols = contract_first(w_value, normed)
    new_kv = jnp.stack([key_cols.astype(jnp.bfloat16), value_cols.astype(jnp.bfloat16)])
    all_kv = lax.all_gather(new_kv, "inst", axis=1, tiled=True)
    kv_dim = all_kv.shape[1]
    kv_heads = kv_dim // head_dim
    group_size = devices // kv_heads
    my_group = my_index // group_size
    positions = (
        jnp.repeat(prefix_len, new_len) + jnp.tile(jnp.arange(new_len, dtype=jnp.int32), requests)
    ).astype(jnp.float32)
    cos_table, sin_table = rotary_tables(positions, head_dim)
    q_rot = rotate_rows(query, cos_table, sin_table).astype(jnp.bfloat16)
    k_rot = rotate_cols(
        all_kv[0].astype(jnp.float32).reshape(kv_heads, head_dim, tok_count),
        cos_table.T,
        sin_table.T,
    ).astype(jnp.bfloat16)
    v_heads = all_kv[1].reshape(kv_heads, head_dim, tok_count)
    my_keys = lax.dynamic_index_in_dim(k_rot, my_group, 0, keepdims=False)
    my_values = lax.dynamic_index_in_dim(v_heads, my_group, 0, keepdims=False)
    pool_dev = cache_pool.shape[0]
    page_len = cache_pool.shape[1]
    hit_slots = pool_dev // 2
    flat_hits = hit_page.reshape(-1)
    entries = flat_hits.shape[0]
    is_valid = flat_hits >= 0
    holder = jnp.where(is_valid, flat_hits // pool_dev, -1)
    pool_slot = jnp.where(is_valid, flat_hits % pool_dev, 0)
    entry_ids = jnp.arange(entries, dtype=jnp.int32)
    earlier = (
        (holder[None, :] == holder[:, None])
        & (entry_ids[None, :] < entry_ids[:, None])
        & is_valid[None, :]
    )
    ranking = jnp.sum(earlier.astype(jnp.int32), axis=1)
    mine = is_valid & (holder == my_index)
    chosen = mine[None, :] & (ranking[None, :] == jnp.arange(hit_slots, dtype=jnp.int32)[:, None])
    pool_index = jnp.sum(jnp.where(chosen, pool_slot[None, :], 0), axis=1)
    present = jnp.any(chosen, axis=1)
    picked = cache_pool[pool_index]
    picked = jnp.where(present[:, None, None, None], picked, jnp.zeros_like(picked))
    inv_scale = head_dim ** (-0.5)
    per_head = picked.reshape(hit_slots, page_len, 2, kv_heads, head_dim).transpose(3, 0, 1, 2, 4)
    outgoing = jnp.repeat(per_head, group_size, axis=0)
    incoming = lax.all_to_all(outgoing, "inst", split_axis=0, concat_axis=0, tiled=True)
    stacked = incoming.reshape(devices * hit_slots, page_len, 2, head_dim)
    where_from = jnp.where(is_valid, holder * hit_slots + ranking, 0)
    prefix_rows = stacked[where_from]
    prefix_keys = prefix_rows[:, :, 0].reshape(requests, -1, head_dim)
    prefix_values = prefix_rows[:, :, 1].reshape(requests, -1, head_dim)
    prefix_span = prefix_keys.shape[1]
    causal_ok = (
        jnp.arange(new_len, dtype=jnp.int32)[None, :]
        <= jnp.arange(new_len, dtype=jnp.int32)[:, None]
    )
    pieces = []
    for request in range(requests):
        lower = request * new_len
        q_part = q_rot[lower : lower + new_len]
        pre_scores = contract_last(q_part, prefix_keys[request]) * inv_scale
        new_scores = (
            jnp.dot(q_part, my_keys[:, lower : lower + new_len], preferred_element_type=jnp.float32)
            * inv_scale
        )
        prefix_ok = jnp.arange(prefix_span, dtype=jnp.int32)[None, :] < prefix_len[request]
        row_max = jnp.maximum(
            jnp.max(jnp.where(prefix_ok, pre_scores, -jnp.inf), axis=1),
            jnp.max(jnp.where(causal_ok, new_scores, -jnp.inf), axis=1),
        )[:, None]
        pre_exps = jnp.where(prefix_ok, jnp.exp(pre_scores - row_max), 0.0)
        new_exps = jnp.where(causal_ok, jnp.exp(new_scores - row_max), 0.0)
        row_sum = jnp.sum(pre_exps, axis=1, keepdims=True) + jnp.sum(
            new_exps, axis=1, keepdims=True
        )
        mixture = jnp.dot(
            pre_exps.astype(jnp.bfloat16),
            prefix_values[request],
            preferred_element_type=jnp.float32,
        )
        mixture = mixture + contract_last(
            new_exps.astype(jnp.bfloat16), my_values[:, lower : lower + new_len]
        )
        pieces.append((mixture / row_sum).astype(jnp.bfloat16))
    attn_out = jnp.concatenate(pieces, axis=0)
    pages_new = new_len // page_len
    rows_new = decode_owner.shape[0]
    k_pages = (
        k_rot.reshape(kv_heads, head_dim, requests, pages_new, page_len)
        .transpose(2, 3, 0, 4, 1)
        .reshape(rows_new, page_len, head_dim)
    )
    v_pages = (
        v_heads.reshape(kv_heads, head_dim, requests, pages_new, page_len)
        .transpose(2, 3, 0, 4, 1)
        .reshape(rows_new, page_len, head_dim)
    )
    row_ids = jnp.arange(rows_new, dtype=jnp.int32)
    before_rows = (decode_owner[None, :] == decode_owner[:, None]) & (
        row_ids[None, :] < row_ids[:, None]
    )
    slot_num = jnp.sum(before_rows.astype(jnp.int32), axis=1)
    owned = (decode_owner[None, :] == my_index) & (
        slot_num[None, :] == jnp.arange(OWN, dtype=jnp.int32)[:, None]
    )
    pick_row = jnp.sum(jnp.where(owned, row_ids[None, :], 0), axis=1)
    has_row = jnp.any(owned, axis=1)
    page_pair = jnp.stack([k_pages[pick_row], v_pages[pick_row]], axis=2)
    decode_pages = jnp.where(has_row[:, None, None, None], page_pair, jnp.zeros_like(page_pair))
    return (attn_out, decode_pages)


def solution(mesh):
    return jax.shard_map(
        on_device,
        mesh=mesh,
        in_specs=(
            P("groups", "inst"),
            P(),
            P(None, "inst"),
            P(None, "inst"),
            P(None, "inst"),
            P(("groups", "inst"), None, None, None),
            P("groups"),
            P("groups", None),
            P("groups"),
        ),
        out_specs=(P("groups", "inst"), P(("groups", "inst"), None, None, None)),
        check_vma=False,
    )
```

profile of v0, /device:TPU:0, one launch (start us, length us, event | category | flops | bytes accessed | tf_op | source)
XLA Modules:
  0.0 309.4 jit_solution(16417389585315109285)
XLA Ops:
  7.9 0.8 reshape.375
  9.0 3.6 %gather_fusion = bf16[16,64,2,256]{3,2,1,0:T(2,128)(2,1)} fusion(bf16[32,64,2,256]{3,2,1,0:T(2,128)(2,1)S(1)} %copy-done, s32[1024]{0:T(1024)S(1)} %pad_clamp_fusion.2), kind=kCustom, calls=%fused_computation | custom fusion | bytes 2097216 | tf_op jit(solution)/shard_map/gather | solution.py:112
  12.6 3.5 %gather.15 = bf16[16,64,2,2,128]{4,3,2,1,0:T(2,128)(2,1)S(1)} reshape(bf16[16,64,2,256]{3,2,1,0:T(2,128)(2,1)} %gather_fusion) | data formatting | bytes 2097152 | tf_op jit(solution)/shard_map/gather | solution.py:112
  16.3 0.9 fusion.23
  17.5 5.4 %broadcast_in_dim.140 = bf16[2,8,16,64,2,128]{5,3,4,2,1,0:T(8,128)(2,1)} broadcast(bf16[2,16,64,2,128]{4,2,3,1,0:T(8,128)(2,1)S(1)} %copy.21), dimensions={0,2,3,4,5} | broadcast | bytes 9437184 | tf_op jit(solution)/shard_map/broadcast_in_dim | solution.py:116
  22.8 7.6 %all-to-all-start = ((bf16[16,16,64,2,128]{4,2,3,1,0:T(8,128)(2,1)}), bf16[16,16,64,2,128]{4,2,3,1,0:T(8,128)(2,1)}, u32[]{:S(2)}, u32[]{:S(2)}) async-start(bf16[16,16,64,2,128]{4,2,3,1,0:T(8,128)(2,1)} %bitcast.61), calls=%async_computation | async-start | bytes 16777216 | tf_op jit(solution)/shard_map/all_to_all | solution.py:117
  33.6 172.3 %all-gather.2.cloned.1.call-done = bf16[512,8192]{1,0:T(8,128)(2,1)} async-done(((bf16[512,512]{1,0:T(8,128)(2,1)}), bf16[512,8192]{1,0:T(8,128)(2,1)}) %all-gather.2.cloned.1.call-update) | async-done | bytes 8388624 | tf_op jit(solution)/shard_map/all_gather | solution.py:67
  205.8 5.1 %fusion = f32[512]{0:T(512)S(1)} fusion(bf16[512,8192]{1,0:T(8,128)(2,1)} %all-gather.2.cloned.1.call-done), kind=kLoop, calls=%fused_computation.6 | loop fusion | flops 12582400 | bytes 8390656 | tf_op jit(solution)/shard_map/reduce_sum | solution.py:69
  211.0 9.9 %fusion.2 = bf16[512,8192]{1,0:T(8,128)(2,1)} fusion(bf16[512,8192]{1,0:T(8,128)(2,1)} %all-gather.2.cloned.1.call-done, f32[8192]{0:T(1024)S(1)} %copy-done.4, f32[512]{0:T(512)S(1)} %add_rsqrt_fusion), kind=kLoop, calls=%fused_computation.8 | loop fusion | flops 16777216 | bytes 16812032 | tf_op jit(solution)/shard_map/convert_element_type | solution.py:70
  220.9 5.8 %fusion.22 = bf16[1,16,512]{2,1,0:T(8,128)(2,1)S(1)} fusion(bf16[512,8192]{1,0:T(8,128)(2,1)} %fusion.2, bf16[8192,16]{0,1:T(8,128)(2,1)S(1)} %copy-done.2), kind=kOutput, calls=%fused_computation.39 | convolution fusion | flops 134225920 | bytes 8667136 | tf_op jit(solution)/shard_map/dot_general | solution.py:53
  226.7 2.3 fusion.21
  228.9 44.3 %all_gather.7 = bf16[2,256,512]{2,1,0:T(8,128)(2,1)S(1)} all-gather(bf16[2,16,512]{2,1,0:T(8,128)(2,1)S(1)} %pad_maximum_fusion.2), channel_id=1, replica_groups=mesh['groups'=2,'inst'=16] {'inst'}, dimensions={1}, use_global_device_ids=true | all-gather | bytes 557056 | tf_op jit(solution)/shard_map/all_gather | solution.py:75
  273.7 0.9 concatenate.22
  274.6 1.4 maximum_bitcast_fusion
  277.7 0.7 copy.25
  278.5 6.9 %fusion.74 = f32[512,128]{0,1:T(8,128)S(1)} fusion(bf16[512,8192]{1,0:T(8,128)(2,1)} %fusion.2, bf16[8192,128]{1,0:T(8,128)(2,1)} %param.11), kind=kOutput, calls=%fused_computation.140 | convolution fusion | flops 1073741824 | bytes 10747904 | tf_op jit(solution)/shard_map/dot_general | solution.py:71
  286.4 6.4 %gather_fusion.1 = bf16[128,64,2,128]{3,1,2,0:T(8,128)(2,1)} fusion(bf16[256,64,2,128]{3,1,2,0:T(8,128)(2,1)} %bitcast.5, s32[1024]{0:T(1024)S(1)} %pad_clamp_fusion.1), kind=kCustom, calls=%fused_computation.1 | custom fusion | bytes 8389120 | tf_op jit(solution)/shard_map/gather | solution.py:120
  292.8 3.2 %fusion.71 = (bf16[64,64,1,128]{3,1,2,0:T(8,128)(2,1)S(1)}, bf16[64,64,1,128]{3,1,2,0:T(8,128)(2,1)S(1)}, bf16[64,64,1,128]{3,1,2,0:T(8,128)(2,1)S(1)}, bf16[64,64,1,128]{3,1,2,0:T(8,128)(2,1)S(1)}) fusion(bf16[128,64,2,128]{3,1,2,0:T(8,128)(2,1)} %gather_fusion.1), kind=kLoop, calls=%fused_computation.137 | loop fusion | bytes 8388608 | tf_op jit(solution)/shard_map/slice | solution.py:132
  296.0 0.8 select_reduce_fusion
  296.8 0.9 fusion.5
  297.7 0.9 fusion.7
  298.7 0.8 select_reduce_fusion.1
  299.5 0.9 fusion.3
  300.4 0.9 fusion.9
  (69 shorter events, 9.1 us)
Async XLA Ops:
  7.2 1.9 copy-start
  7.2 198.7 %all-gather.2.cloned.1.call-start = ((), (), s32[]{:S(2)}) async-start(), calls=%async_computation.1 | async-start | bytes 8912896 | tf_op jit(solution)/shard_map/all_gather | solution.py:67
  22.8 7.6 %copy-start.6 = (s32[2,64]{1,0:T(2,128)S(1)}, s32[2,64]{1,0:T(2,128)}, u32[]{:S(2)}) copy-start(s32[2,64]{1,0:T(2,128)} %param.16) | copy-start | bytes 1540
  22.8 7.7 %copy-start.5 = (s32[2]{0:T(128)S(1)}, s32[2]{0:T(128)}, u32[]{:S(2)}) copy-start(s32[2]{0:T(128)} %param.15) | copy-start | bytes 28
  22.8 9.0 %copy-start.7 = (s32[16]{0:T(128)S(1)}, s32[16]{0:T(128)}, u32[]{:S(2)}) copy-start(s32[16]{0:T(128)} %param.17) | copy-start | bytes 196
  22.8 263.5 %all-to-all-start = ((bf16[16,16,64,2,128]{4,2,3,1,0:T(8,128)(2,1)}), bf16[16,16,64,2,128]{4,2,3,1,0:T(8,128)(2,1)}, u32[]{:S(2)}, u32[]{:S(2)}) async-start(bf16[16,16,64,2,128]{4,2,3,1,0:T(8,128)(2,1)} %bitcast.61), calls=%async_computation | async-start | bytes 16777216 | tf_op jit(solution)/shard_map/all_to_all | solution.py:117
  33.6 177.4 %copy-start.4 = (f32[8192]{0:T(1024)S(1)}, f32[8192]{0:T(1024)}, u32[]{:S(2)}) copy-start(f32[8192]{0:T(1024)} %param.10) | copy-start | bytes 98308
  211.0 9.9 %copy-start.2 = (bf16[8192,16]{0,1:T(8,128)(2,1)S(1)}, bf16[8192,16]{0,1:T(8,128)(2,1)}, u32[]{:S(2)}) copy-start(bf16[8192,16]{0,1:T(8,128)(2,1)} %param.13) | copy-start | bytes 786436
  220.8 5.8 %copy-start.1 = (bf16[512,8192]{1,0:T(8,128)(2,1)S(1)}, bf16[512,8192]{1,0:T(8,128)(2,1)}, u32[]{:S(2)}) copy-start(bf16[512,8192]{1,0:T(8,128)(2,1)} %fusion.2) | copy-start | bytes 25165828
  220.8 5.8 %copy-start.3 = (bf16[8192,16]{0,1:T(8,128)(2,1)S(1)}, bf16[8192,16]{0,1:T(8,128)(2,1)}, u32[]{:S(2)}) copy-start(bf16[8192,16]{0,1:T(8,128)(2,1)} %param.12) | copy-start | bytes 786436
Sparse Core Ops, SparseCore 0:
  10.2 195.6 all-gather.1
where the time goes:
time: 310 us; the launch traced here: 309 us
  waiting for transfers between devices  173 us (56%)
  blocking collectives  44.3 us (14%)
  local copies, waits for them, and re-layouts  27.3 us (9%)
  other arithmetic  23.5 us (8%)
  matrix products  19.3 us (6%)
  between operations  14.3 us (5%)
  starting transfers between devices  7.62 us (2%)
    all_gather x1, waiting for transfers between devices, on_device(): gathered = lax.all_gather(hidden, 'inst', axis=1, tiled=True)  172 us
    all_gather x1, blocking collectives, on_device(): all_kv = lax.all_gather(new_kv, 'inst', axis=1, tiled=True)  44.3 us
    convert_element_type x1, other arithmetic, on_device(): normed = (wide_vals * inverse_rms * gain).astype(jnp.bfloat16)  9.87 us
    dot_general x2, matrix products, contract_first(): lax.dot_general(weights, rows, (((0,), (1,)), ((), ())), preferred_elemen...  8.05 us
    all_to_all x1, starting transfers between devices, on_device(): lax.all_to_all(outgoing, 'inst', split_axis=0, concat_axis=0, tiled=True)  7.58 us
    gather x2, local copies, waits for them, and re-layouts, on_device(): picked = cache_pool[pool_index]  7.11 us
    dot_general x1, matrix products, on_device(): query = jnp.dot(normed, w_query, preferred_element_type=jnp.float32)  6.85 us
    gather x1, local copies, waits for them, and re-layouts, on_device(): prefix_rows = stacked[where_from]  6.44 us
  transfers between devices with their start and end apart: 2, of which 1 were waited for; matrix products, arithmetic and copies ran while one was open for 17% of the time, Pallas kernels for 0%

commit v1 on v0

--- a/solution.py
+++ b/solution.py
@@ -1,6 +1,10 @@
+import functools
+
 import jax
 import jax.numpy as jnp
 from jax import lax
+from jax.experimental import pallas as pl
+from jax.experimental.pallas import tpu as pltpu
 from jax.sharding import PartitionSpec as P
 
 OWN = 2
@@ -181,9 +185,508 @@
     return (attn_out, decode_pages)
 
 
+VMEM_LIMIT = 48 * 1024 * 1024
+
+
+def in_vmem(count):
+    return [pl.BlockSpec(memory_space=pltpu.VMEM)] * count
+
+
+def in_smem(count):
+    return [pl.BlockSpec(memory_space=pltpu.SMEM)] * count
+
+
+def params():
+    return pltpu.CompilerParams(vmem_limit_bytes=VMEM_LIMIT)
+
+
+def cost(flops, nbytes):
+    return pl.CostEstimate(flops=flops, bytes_accessed=nbytes, transcendentals=0)
+
+
+def nt_dot(left, right):
+    return lax.dot_general(
+        left, right, (((1,), (1,)), ((), ())), preferred_element_type=jnp.float32
+    )
+
+
+def pick_pages_kernel(slots, place_ref, hits_ref, pool_ref, mine_ref, other_ref):
+    me, head = place_ref[0], place_ref[1]
+    pool_dev, page_len = pool_ref.shape[0], pool_ref.shape[1]
+    rows = 2 * page_len
+    out_row = lax.broadcasted_iota(jnp.int32, (rows, rows), 0)
+    in_row = lax.broadcasted_iota(jnp.int32, (rows, rows), 1)
+    wanted = jnp.where(out_row < page_len, 2 * out_row, 2 * (out_row - page_len) + 1)
+    unweave = (in_row == wanted).astype(jnp.bfloat16)
+
+    def entry(e, count):
+        page = hits_ref[e]
+        is_mine = (page >= 0) & (page // pool_dev == me)
+
+        @pl.when(is_mine)
+        def _():
+            at = pl.ds(pl.multiple_of(count * rows, rows), rows)
+            slab = pool_ref[page - me * pool_dev]
+            first = slab[:, :, :128].reshape(rows, 128)
+            second = slab[:, :, 128:].reshape(rows, 128)
+            both = jnp.concatenate([first, second], axis=1)
+            both = jnp.dot(unweave, both, preferred_element_type=jnp.float32)
+            both = both.astype(jnp.bfloat16)
+            mine_ref[at, :] = jnp.where(head == 0, both[:, :128], both[:, 128:])
+            other_ref[at, :] = jnp.where(head == 0, both[:, 128:], both[:, :128])
+
+        return count + is_mine.astype(jnp.int32)
+
+    lax.fori_loop(0, hits_ref.shape[0], entry, jnp.int32(0))
+
+
+def pick_pages(place, hits, pool, slots):
+    rows = slots * 2 * pool.shape[1]
+    block = jax.ShapeDtypeStruct((rows, 128), jnp.bfloat16)
+    return pl.pallas_call(
+        functools.partial(pick_pages_kernel, slots),
+        out_shape=(block, block),
+        in_specs=in_smem(2) + in_vmem(1),
+        out_specs=tuple(in_vmem(2)),
+        compiler_params=params(),
+        cost_estimate=cost(0, 4 * pool.size),
+        name="pick_pages",
+    )(place, hits, pool)
+
+
+def pack_weights_kernel(place_ref, wq_ref, wk_ref, wv_ref, *out_refs):
+    plane, lane = place_ref[2], place_ref[3]
+    feats = wk_ref.shape[0]
+    block = wq_ref.shape[0] // 16
+    for r, out_ref in enumerate(out_refs):
+        for k in range(4):
+            start = (lax.rem(plane + k, 4) * 4 + (lane ^ r)) * block
+            start = pl.multiple_of(start, block)
+            out_ref[k * block : (k + 1) * block, :] = wq_ref[pl.ds(start, block), :]
+            for j in range(block // 128):
+                at = 4 * block + (k * (block // 128) + j) * 2 * feats
+                columns = pl.ds(pl.multiple_of(start + j * 128, 128), 128)
+                out_ref[at : at + feats, :] = wk_ref[:, columns]
+                out_ref[at + feats : at + 2 * feats, :] = wv_ref[:, columns]
+
+
+def pack_weights(place, wq, wk_t, wv_t):
+    rows = wq.shape[0] // 4 + 2 * wk_t.shape[0] * wk_t.shape[1] // 4 // 128
+    block = jax.ShapeDtypeStruct((rows, 128), jnp.bfloat16)
+    return pl.pallas_call(
+        pack_weights_kernel,
+        out_shape=(block,) * 4,
+        in_specs=in_smem(1) + in_vmem(3),
+        out_specs=tuple(in_vmem(4)),
+        compiler_params=params(),
+        cost_estimate=cost(0, 4 * wq.size),
+        name="pack_weights",
+    )(place, wq, wk_t, wv_t)
+
+
+def project_kernel(place_ref, inv_ref, gain_ref, *refs):
+    plane = place_ref[2]
+    own_ref, downs, ups = refs[0], refs[1:4], refs[4:7]
+    weights, (near_ref, far_ref) = refs[7:11], refs[11:13]
+    toks, block = own_ref.shape
+    chunks = block // 128
+    inv = inv_ref[...]
+    totals = [None] * 4
+    kv_total = None
+    for k in range(4):
+        if k == 0:
+            raw = own_ref[...]
+        else:
+            raw = jnp.where(plane + k <= 3, downs[k - 1][...], ups[3 - k][...])
+        normed = (raw.astype(jnp.float32) * inv * gain_ref[k : k + 1, :]).astype(jnp.bfloat16)
+        kv_rows = []
+        for r in range(4):
+            part = jnp.dot(
+                normed,
+                weights[r][k * block : (k + 1) * block, :],
+                preferred_element_type=jnp.float32,
+            )
+            totals[r] = part if k == 0 else totals[r] + part
+            pieces = []
+            for j in range(chunks):
+                at = 4 * block + (k * chunks + j) * 32
+                pieces.append(weights[r][at : at + 32, :])
+            kv_rows.append(jnp.concatenate(pieces, axis=1))
+        kv_part = nt_dot(jnp.concatenate(kv_rows, axis=0), normed)
+        kv_total = kv_part if k == 0 else kv_total + kv_part
+    for out_ref, lanes in ((near_ref, (0, 2)), (far_ref, (1, 3))):
+        for n, r in enumerate(lanes):
+            base = n * (toks + 128)
+            out_ref[base : base + toks, :] = totals[r]
+            for t in range(toks // 128):
+                out_ref[base + toks + t * 32 : base + toks + (t + 1) * 32, :] = kv_total[
+                    r * 32 : (r + 1) * 32, t * 128 : (t + 1) * 128
+                ]
+
+
+def project(place, inv, gain, own, downs, ups, weights):
+    toks = own.shape[0]
+    out = jax.ShapeDtypeStruct((2 * (toks + 128), 128), jnp.float32)
+    return pl.pallas_call(
+        project_kernel,
+        out_shape=(out, out),
+        in_specs=in_smem(1) + in_vmem(2 + 7 + 4),
+        out_specs=tuple(in_vmem(2)),
+        compiler_params=params(),
+        cost_estimate=cost(2 * toks * 2048 * 640, 6 << 20),
+        name="project",
+    )(place, inv, gain, own, *downs, *ups, *weights)
+
+
+def finish_kernel(left_ref, middle_ref, right_ref, cos_ref, sin_ref, out_ref):
+    toks = cos_ref.shape[0]
+    total = left_ref[: toks + 128, :] + middle_ref[: toks + 128, :] + right_ref[...]
+    query = total[:toks]
+    swapped = jnp.concatenate([query[:, 64:], query[:, :64]], axis=1)
+    out_ref[:toks, :] = (query * cos_ref[...] + swapped * sin_ref[...]).astype(jnp.bfloat16)
+    out_ref[toks:, :] = total[toks:].astype(jnp.bfloat16)
+
+
+def finish(near, got, far_sum, cos_wide, sin_wide):
+    toks = cos_wide.shape[0]
+    return pl.pallas_call(
+        finish_kernel,
+        out_shape=jax.ShapeDtypeStruct((toks + 128, 128), jnp.bfloat16),
+        in_specs=in_vmem(5),
+        out_specs=in_vmem(1)[0],
+        compiler_params=params(),
+        cost_estimate=cost(0, 2 << 20),
+        name="finish_projection",
+    )(near, got, far_sum, cos_wide, sin_wide)
+
+
+def sort_pages_kernel(place_ref, hits_ref, lens_ref, *refs):
+    blocks, (keys_ref, values_ref, count_ref) = refs[:8], refs[8:11]
+    held, seen, sems = refs[11:]
+    me = place_ref[0]
+    pool_dev = place_ref[4]
+    copies = [
+        pltpu.make_async_copy(block, held.at[n], sems.at[n]) for n, block in enumerate(blocks)
+    ]
+    for copy in copies:
+        copy.start()
+    requests, keys_max = keys_ref.shape[0], keys_ref.shape[1]
+    entries = hits_ref.shape[0]
+    per_request = entries // requests
+    page_len = keys_max // per_request
+    values_ref[...] = jnp.zeros_like(values_ref)
+    keys_ref[...] = jnp.zeros_like(keys_ref)
+    for h in range(16):
+        seen[h] = 0
+    for copy in copies:
+        copy.wait()
+    for request in range(requests):
+
+        def entry(p, carry, request=request):
+            pages, tokens = carry
+            page = hits_ref[request * per_request + p]
+            valid = page >= 0
+            holder = jnp.maximum(page, 0) // pool_dev
+            rel = holder ^ me
+            taken = valid & ((rel & 4) == 0)
+            slot = seen[holder]
+            seen[holder] = slot + valid.astype(jnp.int32)
+
+            @pl.when(taken)
+            def _():
+                which = ((rel >> 3) & 1) * 4 + (rel & 3)
+                source = pl.multiple_of(slot * 2 * page_len, 2 * page_len)
+                target = pl.multiple_of(pages * page_len, page_len)
+                keys_ref[request, pl.ds(target, page_len), :] = held[
+                    which, pl.ds(source, page_len), :
+                ]
+                values_ref[request, pl.ds(target, page_len), :] = held[
+                    which, pl.ds(source + page_len, page_len), :
+                ]
+
+            here = taken.astype(jnp.int32)
+            filled = jnp.minimum(page_len, lens_ref[request] - p * page_len)
+            return pages + here, tokens + here * filled
+
+        _, tokens = lax.fori_loop(0, per_request, entry, (jnp.int32(0), jnp.int32(0)))
+        count_ref[request] = tokens
+
+
+def sort_pages(place, hits, lens, blocks, page_len):
+    requests = lens.shape[0]
+    span = hits.shape[0] // requests * page_len
+    side = jax.ShapeDtypeStruct((requests, span, 128), jnp.bfloat16)
+    return pl.pallas_call(
+        sort_pages_kernel,
+        out_shape=(side, side, jax.ShapeDtypeStruct((requests,), jnp.int32)),
+        in_specs=in_smem(3) + [pl.BlockSpec(memory_space=pl.ANY)] * 8,
+        out_specs=tuple(in_vmem(2) + in_smem(1)),
+        scratch_shapes=[
+            pltpu.VMEM((8,) + blocks[0].shape, jnp.bfloat16),
+            pltpu.SMEM((16,), jnp.int32),
+            pltpu.SemaphoreType.DMA((8,)),
+        ],
+        compiler_params=params(),
+        cost_estimate=cost(0, 8 << 20),
+        name="sort_pages",
+    )(place, hits, lens, *blocks)
+
+
+def column_to_row(column):
+    return jnp.transpose(jnp.broadcast_to(column, (128, 128)))[0:1]
+
+
+def row_to_column(row):
+    return jnp.transpose(jnp.broadcast_to(row, (128, 128)))[:, 0:1]
+
+
+def attend_kernel(chunk, count_ref, query_ref, keys_ref, values_ref, out_ref, acc, top, total):
+    requests = keys_ref.shape[0]
+    toks = out_ref.shape[0] - 8
+    new_len = toks // requests
+    for request in range(requests):
+        query = query_ref[request * new_len : (request + 1) * new_len, :]
+        keys_here = count_ref[request]
+        acc[...] = jnp.zeros_like(acc)
+        top[...] = jnp.full_like(top, -jnp.inf)
+        total[...] = jnp.zeros_like(total)
+
+        def step(n, carry, request=request, query=query, keys_here=keys_here):
+            at = pl.ds(pl.multiple_of(n * chunk, chunk), chunk)
+            scores = nt_dot(query, keys_ref[request, at, :]) * 128**-0.5
+            column = lax.broadcasted_iota(jnp.int32, scores.shape, 1)
+            scores = jnp.where(column < keys_here - n * chunk, scores, -jnp.inf)
+            old = top[:, 0:1]
+            new = jnp.maximum(old, jnp.max(scores, axis=1, keepdims=True))
+            exps = jnp.exp(scores - new)
+            fade = jnp.exp(old - new)
+            total[...] = total[...] * fade + jnp.sum(exps, axis=1, keepdims=True)
+            acc[...] = acc[...] * fade + jnp.dot(
+                exps.astype(jnp.bfloat16),
+                values_ref[request, at, :],
+                preferred_element_type=jnp.float32,
+            )
+            top[...] = jnp.broadcast_to(new, top.shape)
+            return carry
+
+        lax.fori_loop(0, (keys_here + chunk - 1) // chunk, step, 0)
+        out_ref[request * new_len : (request + 1) * new_len, :] = acc[...]
+        for b in range(new_len // 128):
+            row = request * (new_len // 128) + b
+            part = slice(b * 128, (b + 1) * 128)
+            out_ref[toks + row : toks + row + 1, :] = column_to_row(top[part, 0:1])
+            out_ref[toks + 4 + row : toks + 5 + row, :] = column_to_row(total[part, 0:1])
+
+
+def attend(count, query_kv, keys, values, toks):
+    new_len = toks // keys.shape[0]
+    return pl.pallas_call(
+        functools.partial(attend_kernel, 512),
+        out_shape=jax.ShapeDtypeStruct((toks + 8, 128), jnp.float32),
+        in_specs=in_smem(1) + in_vmem(3),
+        out_specs=in_vmem(1)[0],
+        scratch_shapes=[pltpu.VMEM((new_len, 128), jnp.float32)] * 3,
+        compiler_params=params(),
+        cost_estimate=cost(4 * new_len * 4096 * 128, 16 << 20),
+        name="attend_prefix",
+    )(count, query_kv, keys, values)
+
+
+def new_tokens_kernel(
+    place_ref, near_ref, side_ref, core_ref, cos_ref, sin_ref, key_ref, value_ref, page_ref, held, kt, vt
+):
+    me, head = place_ref[0], place_ref[1]
+    toks = key_ref.shape[1]
+    for n in range(4):
+        held[n] = near_ref[n]
+        held[4 + n] = side_ref[n]
+    for n in range(8):
+        held[8 + n] = core_ref[n]
+    for device in range(16):
+        rel = device ^ me
+        block = held[(rel & 1) * 8 + ((rel >> 1) & 1) * 4 + (rel >> 2)]
+        rows = slice((device % 8) * 16, (device % 8) * 16 + 16)
+        for t in range(toks // 128):
+            columns = slice(t * 128, (t + 1) * 128)
+            kt[device // 8, rows, columns] = block[t * 32 : t * 32 + 16]
+            vt[device // 8, rows, columns] = block[t * 32 + 16 : t * 32 + 32]
+    cos, sin = cos_ref[...], sin_ref[...]
+    for g in range(2):
+        first = kt[g, :64, :].astype(jnp.float32)
+        second = kt[g, 64:, :].astype(jnp.float32)
+        kt[g, :64, :] = (first * cos - second * sin).astype(jnp.bfloat16)
+        kt[g, 64:, :] = (second * cos + first * sin).astype(jnp.bfloat16)
+    key_ref[...] = kt[head]
+    value_ref[...] = vt[head]
+    page_len = page_ref.shape[1]
+    out_row = lax.broadcasted_iota(jnp.int32, (2 * page_len, 128), 0)
+    token = lax.broadcasted_iota(jnp.int32, (2 * page_len, 128), 1)
+    for slot in range(page_ref.shape[0]):
+        row, has = place_ref[5 + 2 * slot], place_ref[6 + 2 * slot]
+        start = (row // 8) * (toks // 2) + ((row // 2) % 4) * page_len
+        columns = pl.ds(pl.multiple_of(start // 128 * 128, 128), 128)
+        inside = token - start % 128
+        inside = jnp.where(has > 0, inside, -1)
+        take_k = ((out_row % 2 == 0) & (inside == out_row // 2)).astype(jnp.bfloat16)
+        take_v = ((out_row % 2 == 1) & (inside == out_row // 2)).astype(jnp.bfloat16)
+        woven = nt_dot(take_k, kt[row % 2, :, columns]) + nt_dot(take_v, vt[row % 2, :, columns])
+        page_ref[slot] = woven.astype(jnp.bfloat16).reshape(page_len, 2, 128)
+
+
+def new_tokens(place, near, side, core, cos_t, sin_t, page_len):
+    toks = cos_t.shape[1]
+    half = jax.ShapeDtypeStruct((128, toks), jnp.bfloat16)
+    return pl.pallas_call(
+        new_tokens_kernel,
+        out_shape=(half, half, jax.ShapeDtypeStruct((OWN, page_len, 2, 128), jnp.bfloat16)),
+        in_specs=in_smem(1) + in_vmem(5),
+        out_specs=tuple(in_vmem(3)),
+        scratch_shapes=[
+            pltpu.VMEM((16, 128, 128), jnp.bfloat16),
+            pltpu.VMEM((2, 128, toks), jnp.bfloat16),
+            pltpu.VMEM((2, 128, toks), jnp.bfloat16),
+        ],
+        compiler_params=params(),
+        cost_estimate=cost(0, 2 << 20),
+        name="new_tokens",
+    )(place, near, side, core, cos_t, sin_t)
+
+
+def combine_kernel(own_ref, far_ref, query_ref, key_ref, value_ref, out_ref):
+    toks = out_ref.shape[0]
+    new_len = toks // 2
+    query_at = lax.broadcasted_iota(jnp.int32, (128, new_len), 0)
+    key_at = lax.broadcasted_iota(jnp.int32, (128, new_len), 1)
+    for b in range(toks // 128):
+        rows = slice(b * 128, (b + 1) * 128)
+        request = b * 128 // new_len
+        columns = slice(request * new_len, (request + 1) * new_len)
+        scores = jnp.dot(query_ref[rows, :], key_ref[:, columns], preferred_element_type=jnp.float32)
+        allowed = key_at <= query_at + (b * 128 - request * new_len)
+        scores = jnp.where(allowed, scores * 128**-0.5, -jnp.inf)
+        tops = [row_to_column(ref[toks + b : toks + b + 1, :]) for ref in (own_ref, far_ref)]
+        sums = [row_to_column(ref[toks + 4 + b : toks + 5 + b, :]) for ref in (own_ref, far_ref)]
+        top = jnp.maximum(jnp.maximum(tops[0], tops[1]), jnp.max(scores, axis=1, keepdims=True))
+        exps = jnp.exp(scores - top)
+        mixture = nt_dot(exps.astype(jnp.bfloat16), value_ref[:, columns])
+        total = jnp.sum(exps, axis=1, keepdims=True)
+        for ref, peak, row_sum in zip((own_ref, far_ref), tops, sums):
+            fade = jnp.exp(peak - top)
+            total = total + row_sum * fade
+            mixture = mixture + ref[rows, :] * fade
+        out_ref[rows, :] = (mixture / total).astype(jnp.bfloat16)
+
+
+def combine(own, far, query_kv, key_t, value_t):
+    toks = key_t.shape[1]
+    return pl.pallas_call(
+        combine_kernel,
+        out_shape=jax.ShapeDtypeStruct((toks, 128), jnp.bfloat16),
+        in_specs=in_vmem(5),
+        out_specs=in_vmem(1)[0],
+        compiler_params=params(),
+        cost_estimate=cost(0, 1 << 20),
+        name="combine",
+    )(own, far, query_kv, key_t, value_t)
+
+
+def swap(values, bits):
+    return lax.ppermute(values, "inst", [(i, i ^ bits) for i in range(16)])
+
+
+def hop(values, step, step_count):
+    pairs = []
+    for i in range(16):
+        plane = i // 4
+        sends = plane >= step_count - 1 if step > 0 else plane <= 4 - step_count
+        if sends and 0 <= plane + step <= 3:
+            pairs.append((i, i + 4 * step))
+    return lax.ppermute(values, "inst", pairs)
+
+
+def on_16_devices(
+    hidden, gain, w_query, w_key, w_value, cache_pool, prefix_len, hit_page, decode_owner
+):
+    me = lax.axis_index("inst")
+    plane, lane = me // 4, me % 4
+    toks, block = hidden.shape
+    pool_dev, page_len = cache_pool.shape[0], cache_pool.shape[1]
+    requests = prefix_len.shape[0]
+    new_len = toks // requests
+    slots = pool_dev // 2
+    head = me // 8
+    rows_new = decode_owner.shape[0]
+    row_ids = jnp.arange(rows_new, dtype=jnp.int32)
+    before_rows = (decode_owner[None, :] == decode_owner[:, None]) & (
+        row_ids[None, :] < row_ids[:, None]
+    )
+    slot_num = jnp.sum(before_rows.astype(jnp.int32), axis=1)
+    owned = (decode_owner[None, :] == me) & (
+        slot_num[None, :] == jnp.arange(OWN, dtype=jnp.int32)[:, None]
+    )
+    pick_row = jnp.sum(jnp.where(owned, row_ids[None, :], 0), axis=1)
+    has_row = jnp.any(owned, axis=1).astype(jnp.int32)
+    place = jnp.stack([me, head, plane, lane]).astype(jnp.int32)
+    page_place = jnp.concatenate(
+        [place, jnp.full((1,), pool_dev, jnp.int32), jnp.stack([pick_row, has_row], 1).reshape(-1)]
+    )
+    sort_place = jnp.concatenate([place, jnp.full((1,), pool_dev, jnp.int32)])
+    hits = hit_page.reshape(-1)
+
+    wide = hidden.astype(jnp.float32)
+    squares = jnp.sum(wide * wide, axis=1)
+    squares = squares + swap(squares, 1)
+    squares = squares + swap(squares, 2)
+    squares = squares + swap(squares, 4) + (swap(squares, 8) + swap(squares, 12))
+    inv = lax.rsqrt(squares / (block * 16) + EPS)[:, None]
+
+    downs, ups = [hidden], [hidden]
+    for k in (1, 2, 3):
+        downs.append(hop(downs[-1], -1, k))
+        ups.append(hop(ups[-1], 1, k))
+
+    packed = pack_weights(place, w_query, w_key.T, w_value.T)
+    weights = [packed[0]] + [swap(packed[r], r) for r in (1, 2, 3)]
+
+    mine, other = pick_pages(place, hits, cache_pool, slots)
+    pages = [mine, swap(other, 8)]
+    pages = [pages[0], swap(pages[0], 2), pages[1], swap(pages[1], 2)]
+    pages = [each for page in pages for each in (page, swap(page, 1))]
+    keys, values, count = sort_pages(sort_place, hits, prefix_len, pages, page_len)
+
+    positions = (
+        jnp.repeat(prefix_len, new_len) + jnp.tile(jnp.arange(new_len, dtype=jnp.int32), requests)
+    ).astype(jnp.float32)
+    cos_table, sin_table = rotary_tables(positions, 128)
+    cos_wide = jnp.concatenate([cos_table, cos_table], axis=1)
+    sin_wide = jnp.concatenate([-sin_table, sin_table], axis=1)
+
+    gain_blocks = lax.dynamic_index_in_dim(gain.reshape(4, 4, block), lane, 1, keepdims=False)
+    gain_blocks = jnp.concatenate([gain_blocks, gain_blocks], axis=0)
+    gain_blocks = lax.dynamic_slice_in_dim(gain_blocks, plane, 4, 0)
+    near, far = project(place, inv, gain_blocks, hidden, downs[1:], ups[1:], weights)
+    got = swap(far, 1)
+    far_sum = swap(near[toks + 128 :] + got[toks + 128 :], 2)
+    query_kv = finish(near, got, far_sum, cos_wide, sin_wide)
+
+    from_plane = swap(query_kv, 4)
+    kv = query_kv[toks:]
+    near_kv = jnp.stack([kv, from_plane[toks:], swap(kv, 8), swap(kv, 12)])
+    side_kv = swap(near_kv, 2)
+    core_kv = swap(jnp.concatenate([near_kv, side_kv], axis=0), 1)
+
+    partner_part = swap(attend(count, from_plane, keys, values, toks), 4)
+    own_part = attend(count, query_kv, keys, values, toks)
+    key_t, value_t, decode_pages = new_tokens(
+        page_place, near_kv, side_kv, core_kv, cos_table.T, sin_table.T, page_len
+    )
+    attn_out = combine(own_part, partner_part, query_kv, key_t, value_t)
+    return (attn_out, decode_pages)
+
+
 def solution(mesh):
     return jax.shard_map(
-        on_device,
+        on_16_devices if mesh.shape["inst"] == 16 else on_device,
         mesh=mesh,
         in_specs=(
             P("groups", "inst"),

time: 310 us -> 135 us (0.44)
  waiting for transfers between devices: 173 us -> 48.8 us
  blocking collectives: 44.3 us -> 0 us
  Pallas kernels: 0 us -> 37.9 us
  starting transfers between devices: 7.62 us -> 36.8 us
  local copies, waits for them, and re-layouts: 27.3 us -> 6.6 us
  other arithmetic: 23.5 us -> 3.63 us
  matrix products: 19.3 us -> 0 us
  between operations: 14.3 us -> 1.03 us
    all_gather x1 -> x0, waiting for transfers between devices: 172 us -> none  [on_device(): gathered = lax.all_gather(hidden, 'inst', axis=1, tiled=True)]
    ppermute x0 -> x29, waiting for transfers between devices: none -> 48.8 us  [the longest x23 43.7 us: swap(): return lax.ppermute(values, 'inst', [(i, i ^ bits) for i in range(16)])]
    all_gather x1 -> x0, blocking collectives: 44.3 us -> none  [on_device(): all_kv = lax.all_gather(new_kv, 'inst', axis=1, tiled=True)]
    pallas_call x0 -> x9, Pallas kernels: none -> 37.9 us  [the longest x2 11.4 us: attend(): pl.pallas_call(functools.partial(attend_kernel, 512), out_shape=jax.Shape...]
    ppermute x0 -> x29, starting transfers between devices: none -> 36.8 us  [the longest x23 24.3 us: swap(): return lax.ppermute(values, 'inst', [(i, i ^ bits) for i in range(16)])]
    dot_general x11 -> x0, matrix products: 19.3 us -> none  [the longest x2 8.05 us: contract_first(): lax.dot_general(weights, rows, (((0,), (1,)), ((), ())), preferred_elemen...]
    gather x5 -> x0, local copies, waits for them, and re-layouts: 14.7 us -> none  [the longest x2 7.11 us: on_device(): picked = cache_pool[pool_index]]
    convert_element_type x2 -> x1, other arithmetic: 9.92 us -> 0.01 us  [on_16_devices(): has_row = jnp.any(owned, axis=1).astype(jnp.int32)]
  transfers between devices with their start and end apart: 2 -> 29, of which waited for: 1 -> 10; matrix products, arithmetic and copies ran while one was open for 17% -> 3% of each run, Pallas kernels for 0% -> 26%
where the time goes in v1:
time: 135 us
  waiting for transfers between devices  48.8 us (36%)
  Pallas kernels  37.9 us (28%)
  starting transfers between devices  36.8 us (27%)
  local copies, waits for them, and re-layouts  6.6 us (5%)
  other arithmetic  3.63 us (3%)
    ppermute x23, waiting for transfers between devices, swap(): return lax.ppermute(values, 'inst', [(i, i ^ bits) for i in range(16)])  43.7 us
    ppermute x23, starting transfers between devices, swap(): return lax.ppermute(values, 'inst', [(i, i ^ bits) for i in range(16)])  24.3 us
    ppermute x6, starting transfers between devices, hop(): return lax.ppermute(values, 'inst', pairs)  12.5 us
    pallas_call x2, Pallas kernels, attend(): pl.pallas_call(functools.partial(attend_kernel, 512), out_shape=jax.Shape...  11.4 us
    pallas_call x1, Pallas kernels, sort_pages(): pl.pallas_call(sort_pages_kernel, out_shape=(side, side, jax.ShapeDtypeSt...  7.88 us
    pallas_call x1, Pallas kernels, pick_pages(): pl.pallas_call(functools.partial(pick_pages_kernel, slots), out_shape=(bl...  6.76 us
    unnamed x34, local copies, waits for them, and re-layouts  5.97 us
    pallas_call x1, Pallas kernels, project(): pl.pallas_call(project_kernel, out_shape=(out, out), in_specs=in_smem(1)...  5.91 us
  transfers between devices with their start and end apart: 29, of which 10 were waited for; matrix products, arithmetic and copies ran while one was open for 3% of the time, Pallas kernels for 26%

profile of v1, /device:TPU:0, one launch (start us, length us, event | category | flops | bytes accessed | tf_op | source)
XLA Modules:
  0.0 134.7 jit_solution(13826787104614721031)
XLA Ops:
  2.1 6.4 %collective-permute-start.15 = (bf16[512,512]{1,0:T(8,128)(2,1)}, bf16[512,512]{1,0:T(8,128)(2,1)}, u32[]{:S(2)}, u32[]{:S(2)}) collective-permute-start(bf16[512,512]{1,0:T(8,128)(2,1)} %refs_0_.1), channel_id=1, source_target_pairs={{0,4},{1,5},{2,6},{3,7},{4,8},{5,9},{6,10},{7,11},{8,12},{9,13},{1... | collective-permute-start | bytes 1572872 | tf_op jit(solution)/shard_map/ppermute | solution.py:604
  10.9 2.0 %collective-permute-start.8 = (f32[512]{0:T(512)S(1)}, f32[512]{0:T(512)S(1)}, u32[]{:S(2)}, u32[]{:S(2)}) collective-permute-start(f32[512]{0:T(512)S(1)} %add.46), channel_id=1, source_target_pairs={{0,2},{1,3},{2,0},{3,1},{4,6},{5,7},{6,4},{7,5},{8,10},{9,11},{10,... | collective-permute-start | bytes 6152 | tf_op jit(solution)/shard_map/ppermute | solution.py:594
  12.8 5.1 %collective-permute-done.12.refs_1_ = bf16[512,512]{1,0:T(8,128)(2,1)} collective-permute-done((bf16[512,512]{1,0:T(8,128)(2,1)}, bf16[512,512]{1,0:T(8,128)(2,1)}, u32[]{:S(2)}, u32[]{:S(2)}) %collective-permute-start.12) | collective-permute-done | bytes 524320 | tf_op jit(solution)/shard_map/ppermute | solution.py:604
  20.8 1.6 %copy-done.2 = bf16[8192,128]{1,0:T(8,128)(2,1)S(1)} copy-done((bf16[8192,128]{1,0:T(8,128)(2,1)S(1)}, bf16[8192,128]{1,0:T(8,128)(2,1)}, u32[]{:S(2)}) %copy-start.2) | copy-done | bytes 2097176
  24.3 2.0 %pack_weights.1 = (bf16[2560,128]{1,0:T(8,128)(2,1)S(1)}, bf16[2560,128]{1,0:T(8,128)(2,1)}, bf16[2560,128]{1,0:T(8,128)(2,1)}, bf16[2560,128]{1,0:T(8,128)(2,1)}) custom-call(s32[4]{0:T(128)S(1)} %pad_add_fusion.1.place_ref, bf16[8192,128]{1,0:T(8,128)(2,1)S(1)} %copy-done.2, bf16[16,8192]{1,0:T(8,128)(2,1)S(1)} %bitcast.27, bf16[16,8192]{1,0:T(8,128)(2,1)S(1)} %bitcast.28), custom_call_target="tpu_custom_call" | custom-call | bytes 4194304 | tf_op jit(solution)/shard_map/pack_weights/pallas_call | solution.py:276
  26.3 6.4 %collective-permute-start.10 = (f32[512]{0:T(512)S(1)}, f32[512]{0:T(512)S(1)}, u32[]{:S(2)}, u32[]{:S(2)}) collective-permute-start(f32[512]{0:T(512)S(1)} %add.47), channel_id=1, source_target_pairs={{0,8},{1,9},{2,10},{3,11},{4,12},{5,13},{6,14},{7,15},{8,0},{9,1},... | collective-permute-start | bytes 6152 | tf_op jit(solution)/shard_map/ppermute | solution.py:594
  32.9 2.5 %collective-permute-start.11 = (f32[512]{0:T(512)S(1)}, f32[512]{0:T(512)S(1)}, u32[]{:S(2)}, u32[]{:S(2)}) collective-permute-start(f32[512]{0:T(512)S(1)} %add.47), channel_id=1, source_target_pairs={{0,12},{1,13},{2,14},{3,15},{4,8},{5,9},{6,10},{7,11},{8,4},{9,5},... | collective-permute-start | bytes 6152 | tf_op jit(solution)/shard_map/ppermute | solution.py:594
  35.3 2.0 %collective-permute-start.9 = (f32[512]{0:T(512)S(1)}, f32[512]{0:T(512)S(1)}, u32[]{:S(2)}, u32[]{:S(2)}) collective-permute-start(f32[512]{0:T(512)S(1)} %add.47), channel_id=1, source_target_pairs={{0,4},{1,5},{2,6},{3,7},{4,0},{5,1},{6,2},{7,3},{8,12},{9,13},{10,... | collective-permute-start | bytes 6152 | tf_op jit(solution)/shard_map/ppermute | solution.py:594
  37.4 6.8 %pick_pages.1 = (bf16[2048,128]{1,0:T(8,128)(2,1)S(1)}, bf16[2048,128]{1,0:T(8,128)(2,1)}) custom-call(s32[4]{0:T(128)S(1)} %pad_add_fusion.1.place_ref, s32[128]{0:T(128)S(1)} %reshape.46.hits_ref, bf16[32,64,2,256]{3,2,1,0:T(2,128)(2,1)S(1)} %copy-done.3), custom_call_target="tpu_custom_call" | custom-call | bytes 4194304 | tf_op jit(solution)/shard_map/pick_pages/pallas_call | solution.py:246
  47.3 2.9 %collective-permute-start.3 = (bf16[2048,128]{1,0:T(8,128)(2,1)}, bf16[2048,128]{1,0:T(8,128)(2,1)}, u32[]{:S(2)}, u32[]{:S(2)}) collective-permute-start(bf16[2048,128]{1,0:T(8,128)(2,1)} %get-tuple-element.17), channel_id=1, source_target_pairs={{0,8},{1,9},{2,10},{3,11},{4,12},{5,13},{6,14},{7,15},{8,0},{9,1},... | collective-permute-start | bytes 1572872 | tf_op jit(solution)/shard_map/ppermute | solution.py:594
  50.4 12.5 %collective-permute-done.19.refs_9_ = bf16[2560,128]{1,0:T(8,128)(2,1)S(1)} collective-permute-done((bf16[2560,128]{1,0:T(8,128)(2,1)}, bf16[2560,128]{1,0:T(8,128)(2,1)S(1)}, u32[]{:S(2)}, u32[]{:S(2)}) %collective-permute-start.19) | collective-permute-done | bytes 655392 | tf_op jit(solution)/shard_map/ppermute | solution.py:594
  62.9 11.7 %collective-permute-done.20.refs_10_ = bf16[2560,128]{1,0:T(8,128)(2,1)} collective-permute-done((bf16[2560,128]{1,0:T(8,128)(2,1)}, bf16[2560,128]{1,0:T(8,128)(2,1)}, u32[]{:S(2)}, u32[]{:S(2)}) %collective-permute-start.20) | collective-permute-done | bytes 655392 | tf_op jit(solution)/shard_map/ppermute | solution.py:594
  74.5 2.3 %collective-permute-start = (bf16[2048,128]{1,0:T(8,128)(2,1)}, bf16[2048,128]{1,0:T(8,128)(2,1)}, u32[]{:S(2)}, u32[]{:S(2)}) collective-permute-start(bf16[2048,128]{1,0:T(8,128)(2,1)} %copy-done.5), channel_id=1, source_target_pairs={{0,1},{1,0},{2,3},{3,2},{4,5},{5,4},{6,7},{7,6},{8,9},{9,8},{10,11... | collective-permute-start | bytes 1572872 | tf_op jit(solution)/shard_map/ppermute | solution.py:594
  76.9 5.9 %project.1 = (f32[1280,128]{1,0:T(8,128)S(1)}, f32[1280,128]{1,0:T(8,128)}) custom-call(s32[4]{0:T(128)S(1)} %pad_add_fusion.1.place_ref, f32[512,1]{1,0:T(8,128)S(1)} %copy.14.inv_ref, f32[4,512]{1,0:T(4,128)S(1)} %fusion.1.gain_ref, bf16[512,512]{1,0:T(8,128)(2,1)S(1)} %copy-done.4, bf16[512,512]{1,0:T(8,128)(2,1)} %collective-permute-done.12.refs_1_, ...), custom_call_target="tpu_custom_call" | custom-call | flops 1342177280 | bytes 6291456 | tf_op jit(solution)/shard_map/project/pallas_call | solution.py:330
  84.4 13.1 %collective-permute-done.5.refs_6_ = bf16[2048,128]{1,0:T(8,128)(2,1)S(1)} collective-permute-done((bf16[2048,128]{1,0:T(8,128)(2,1)}, bf16[2048,128]{1,0:T(8,128)(2,1)S(1)}, u32[]{:S(2)}, u32[]{:S(2)}) %collective-permute-start.5) | collective-permute-done | bytes 524320 | tf_op jit(solution)/shard_map/ppermute | solution.py:594
  99.4 7.9 %sort_pages.1 = (bf16[2,4096,128]{2,1,0:T(8,128)(2,1)}, bf16[2,4096,128]{2,1,0:T(8,128)(2,1)}, s32[2]{0:T(128)S(1)}) custom-call(s32[5]{0:T(128)S(1)} %concatenate.21.place_ref, s32[128]{0:T(128)S(1)} %reshape.46.hits_ref, s32[2]{0:T(128)S(1)} %copy-done.9, bf16[2048,128]{1,0:T(8,128)(2,1)S(1)} %copy-done.6, bf16[2048,128]{1,0:T(8,128)(2,1)} %collective-permute-done.refs_1_, ...), custom_call_target="tpu_custom_call" | custom-call | bytes 8388608 | tf_op jit(solution)/shard_map/sort_pages/pallas_call | solution.py:419
  109.6 2.8 %collective-permute-start.26 = (bf16[128,128]{1,0:T(8,128)(2,1)S(1)}, bf16[128,128]{1,0:T(8,128)(2,1)S(1)}, u32[]{:S(2)}, u32[]{:S(2)}) collective-permute-start(bf16[128,128]{1,0:T(8,128)(2,1)S(1)} %get-tuple-element.31), channel_id=1, source_target_pairs={{0,12},{1,13},{2,14},{3,15},{4,8},{5,9},{6,10},{7,11},{8,4},{9,5},... | collective-permute-start | bytes 98312 | tf_op jit(solution)/shard_map/ppermute | solution.py:594
  112.4 2.1 %collective-permute-done.23.query_ref = bf16[640,128]{1,0:T(8,128)(2,1)S(1)} collective-permute-done((bf16[640,128]{1,0:T(8,128)(2,1)S(1)}, bf16[640,128]{1,0:T(8,128)(2,1)S(1)}, u32[]{:S(2)}, u32[]{:S(2)}) %collective-permute-start.23) | collective-permute-done | bytes 163872 | tf_op jit(solution)/shard_map/ppermute | solution.py:594
  114.5 2.1 %collective-permute-done.26 = bf16[128,128]{1,0:T(8,128)(2,1)S(1)} collective-permute-done((bf16[128,128]{1,0:T(8,128)(2,1)S(1)}, bf16[128,128]{1,0:T(8,128)(2,1)S(1)}, u32[]{:S(2)}, u32[]{:S(2)}) %collective-permute-start.26) | collective-permute-done | bytes 32800 | tf_op jit(solution)/shard_map/ppermute | solution.py:594
  117.2 1.6 %copy-done.1 = bf16[2,4096,128]{2,1,0:T(8,128)(2,1)S(1)} copy-done((bf16[2,4096,128]{2,1,0:T(8,128)(2,1)S(1)}, bf16[2,4096,128]{2,1,0:T(8,128)(2,1)}, u32[]{:S(2)}) %copy-start.1) | copy-done | bytes 2097176
  118.8 5.7 %attend_prefix.3 = f32[520,128]{1,0:T(8,128)S(1)} custom-call(s32[2]{0:T(128)S(1)} %get-tuple-element.18.count_ref, bf16[640,128]{1,0:T(8,128)(2,1)S(1)} %collective-permute-done.23.query_ref, bf16[2,4096,128]{2,1,0:T(8,128)(2,1)S(1)} %copy-done, bf16[2,4096,128]{2,1,0:T(8,128)(2,1)S(1)} %copy-done.1), custom_call_target="tpu_custom_call" | custom-call | flops 536870912 | bytes 16777216 | tf_op jit(solution)/shard_map/attend_prefix/pallas_call | solution.py:483
  125.3 5.7 %attend_prefix.2.own_ref = f32[520,128]{1,0:T(8,128)S(1)} custom-call(s32[2]{0:T(128)S(1)} %get-tuple-element.18.count_ref, bf16[640,128]{1,0:T(8,128)(2,1)S(1)} %finish_projection.1.query_ref, bf16[2,4096,128]{2,1,0:T(8,128)(2,1)S(1)} %copy-done, bf16[2,4096,128]{2,1,0:T(8,128)(2,1)S(1)} %copy-done.1), custom_call_target="tpu_custom_call" | custom-call | flops 536870912 | bytes 16777216 | tf_op jit(solution)/shard_map/attend_prefix/pallas_call | solution.py:483
  131.0 1.7 %new_tokens.1 = (bf16[128,512]{1,0:T(8,128)(2,1)S(1)}, bf16[128,512]{1,0:T(8,128)(2,1)S(1)}, bf16[2,64,2,128]{3,2,1,0:T(2,128)(2,1)}) custom-call(s32[9]{0:T(128)S(1)} %concatenate.25.place_ref, bf16[4,128,128]{2,1,0:T(8,128)(2,1)S(1)} %pad_maximum_fusion.2.near_ref, bf16[4,128,128]{2,1,0:T(8,128)(2,1)S(1)} %collective-permute-done.27.side_ref, ...), custom_call_target="tpu_custom_call" | custom-call | bytes 2097152 | tf_op jit(solution)/shard_map/new_tokens/pallas_call | solution.py:539
  132.7 2.0 %combine.1 = bf16[512,128]{1,0:T(8,128)(2,1)} custom-call(f32[520,128]{1,0:T(8,128)S(1)} %attend_prefix.2.own_ref, f32[520,128]{1,0:T(8,128)S(1)} %collective-permute-done.24.far_ref, bf16[640,128]{1,0:T(8,128)(2,1)S(1)} %finish_projection.1.query_ref, bf16[128,512]{1,0:T(8,128)(2,1)S(1)} %get-tuple-element.27.key_ref, ...), custom_call_target="tpu_custom_call" | custom-call | bytes 1048576 | tf_op jit(solution)/shard_map/combine/pallas_call | solution.py:582
  (107 shorter events, 19.0 us)
Async XLA Ops:
  0.7 17.3 %collective-permute-start.12 = (bf16[512,512]{1,0:T(8,128)(2,1)}, bf16[512,512]{1,0:T(8,128)(2,1)}, u32[]{:S(2)}, u32[]{:S(2)}) collective-permute-start(bf16[512,512]{1,0:T(8,128)(2,1)} %refs_0_.1), channel_id=1, source_target_pairs={{4,0},{5,1},{6,2},{7,3},{8,4},{9,5},{10,6},{11,7},{12,8},{13,9},{1... | collective-permute-start | bytes 1572872 | tf_op jit(solution)/shard_map/ppermute | solution.py:604
  2.1 17.2 %collective-permute-start.15 = (bf16[512,512]{1,0:T(8,128)(2,1)}, bf16[512,512]{1,0:T(8,128)(2,1)}, u32[]{:S(2)}, u32[]{:S(2)}) collective-permute-start(bf16[512,512]{1,0:T(8,128)(2,1)} %refs_0_.1), channel_id=1, source_target_pairs={{0,4},{1,5},{2,6},{3,7},{4,8},{5,9},{6,10},{7,11},{8,12},{9,13},{1... | collective-permute-start | bytes 1572872 | tf_op jit(solution)/shard_map/ppermute | solution.py:604
  10.9 15.4 %collective-permute-start.8 = (f32[512]{0:T(512)S(1)}, f32[512]{0:T(512)S(1)}, u32[]{:S(2)}, u32[]{:S(2)}) collective-permute-start(f32[512]{0:T(512)S(1)} %add.46), channel_id=1, source_target_pairs={{0,2},{1,3},{2,0},{3,1},{4,6},{5,7},{6,4},{7,5},{8,10},{9,11},{10,... | collective-permute-start | bytes 6152 | tf_op jit(solution)/shard_map/ppermute | solution.py:594
  18.0 27.3 %collective-permute-start.13 = (bf16[512,512]{1,0:T(8,128)(2,1)}, bf16[512,512]{1,0:T(8,128)(2,1)}, u32[]{:S(2)}, u32[]{:S(2)}) collective-permute-start(bf16[512,512]{1,0:T(8,128)(2,1)} %collective-permute-done.12.refs_1_), channel_id=1, source_target_pairs={{4,0},{5,1},{6,2},{7,3},{8,4},{9,5},{10,6},{11,7},{20,16},{21,17},... | collective-permute-start | bytes 1572872 | tf_op jit(solution)/shard_map/ppermute | solution.py:604
  19.3 27.3 %collective-permute-start.16 = (bf16[512,512]{1,0:T(8,128)(2,1)}, bf16[512,512]{1,0:T(8,128)(2,1)}, u32[]{:S(2)}, u32[]{:S(2)}) collective-permute-start(bf16[512,512]{1,0:T(8,128)(2,1)} %collective-permute-done.15.refs_4_), channel_id=1, source_target_pairs={{4,8},{5,9},{6,10},{7,11},{8,12},{9,13},{10,14},{11,15},{20,24},{2... | collective-permute-start | bytes 1572872 | tf_op jit(solution)/shard_map/ppermute | solution.py:604
  26.3 21.0 %collective-permute-start.18 = (bf16[2560,128]{1,0:T(8,128)(2,1)}, bf16[2560,128]{1,0:T(8,128)(2,1)}, u32[]{:S(2)}, u32[]{:S(2)}) collective-permute-start(bf16[2560,128]{1,0:T(8,128)(2,1)} %get-tuple-element.20), channel_id=1, source_target_pairs={{0,1},{1,0},{2,3},{3,2},{4,5},{5,4},{6,7},{7,6},{8,9},{9,8},{10,11... | collective-permute-start | bytes 1966088 | tf_op jit(solution)/shard_map/ppermute | solution.py:594
  26.3 9.0 %collective-permute-start.10 = (f32[512]{0:T(512)S(1)}, f32[512]{0:T(512)S(1)}, u32[]{:S(2)}, u32[]{:S(2)}) collective-permute-start(f32[512]{0:T(512)S(1)} %add.47), channel_id=1, source_target_pairs={{0,8},{1,9},{2,10},{3,11},{4,12},{5,13},{6,14},{7,15},{8,0},{9,1},... | collective-permute-start | bytes 6152 | tf_op jit(solution)/shard_map/ppermute | solution.py:594
  32.9 12.1 %collective-permute-start.11 = (f32[512]{0:T(512)S(1)}, f32[512]{0:T(512)S(1)}, u32[]{:S(2)}, u32[]{:S(2)}) collective-permute-start(f32[512]{0:T(512)S(1)} %add.47), channel_id=1, source_target_pairs={{0,12},{1,13},{2,14},{3,15},{4,8},{5,9},{6,10},{7,11},{8,4},{9,5},... | collective-permute-start | bytes 6152 | tf_op jit(solution)/shard_map/ppermute | solution.py:594
  35.3 9.7 %collective-permute-start.9 = (f32[512]{0:T(512)S(1)}, f32[512]{0:T(512)S(1)}, u32[]{:S(2)}, u32[]{:S(2)}) collective-permute-start(f32[512]{0:T(512)S(1)} %add.47), channel_id=1, source_target_pairs={{0,4},{1,5},{2,6},{3,7},{4,0},{5,1},{6,2},{7,3},{8,12},{9,13},{10,... | collective-permute-start | bytes 6152 | tf_op jit(solution)/shard_map/ppermute | solution.py:594
  45.0 17.9 %collective-permute-start.19 = (bf16[2560,128]{1,0:T(8,128)(2,1)}, bf16[2560,128]{1,0:T(8,128)(2,1)S(1)}, u32[]{:S(2)}, u32[]{:S(2)}) collective-permute-start(bf16[2560,128]{1,0:T(8,128)(2,1)} %get-tuple-element.21), channel_id=1, source_target_pairs={{0,2},{1,3},{2,0},{3,1},{4,6},{5,7},{6,4},{7,5},{8,10},{9,11},{10,... | collective-permute-start | bytes 1966088 | tf_op jit(solution)/shard_map/ppermute | solution.py:594
  45.0 29.5 %collective-permute-start.20 = (bf16[2560,128]{1,0:T(8,128)(2,1)}, bf16[2560,128]{1,0:T(8,128)(2,1)}, u32[]{:S(2)}, u32[]{:S(2)}) collective-permute-start(bf16[2560,128]{1,0:T(8,128)(2,1)} %get-tuple-element.22), channel_id=1, source_target_pairs={{0,3},{1,2},{2,1},{3,0},{4,7},{5,6},{6,5},{7,4},{8,11},{9,10},{10,... | collective-permute-start | bytes 1966088 | tf_op jit(solution)/shard_map/ppermute | solution.py:594
  45.3 31.6 %collective-permute-start.14 = (bf16[512,512]{1,0:T(8,128)(2,1)}, bf16[512,512]{1,0:T(8,128)(2,1)S(1)}, u32[]{:S(2)}, u32[]{:S(2)}) collective-permute-start(bf16[512,512]{1,0:T(8,128)(2,1)} %collective-permute-done.13.refs_2_), channel_id=1, source_target_pairs={{4,0},{5,1},{6,2},{7,3},{20,16},{21,17},{22,18},{23,19}} | collective-permute-start | bytes 1572872 | tf_op jit(solution)/shard_map/ppermute | solution.py:604
  46.6 30.3 %collective-permute-start.17 = (bf16[512,512]{1,0:T(8,128)(2,1)}, bf16[512,512]{1,0:T(8,128)(2,1)S(1)}, u32[]{:S(2)}, u32[]{:S(2)}) collective-permute-start(bf16[512,512]{1,0:T(8,128)(2,1)} %collective-permute-done.16.refs_5_), channel_id=1, source_target_pairs={{8,12},{9,13},{10,14},{11,15},{24,28},{25,29},{26,30},{27,31}} | collective-permute-start | bytes 1572872 | tf_op jit(solution)/shard_map/ppermute | solution.py:604
  47.3 35.6 %collective-permute-start.3 = (bf16[2048,128]{1,0:T(8,128)(2,1)}, bf16[2048,128]{1,0:T(8,128)(2,1)}, u32[]{:S(2)}, u32[]{:S(2)}) collective-permute-start(bf16[2048,128]{1,0:T(8,128)(2,1)} %get-tuple-element.17), channel_id=1, source_target_pairs={{0,8},{1,9},{2,10},{3,11},{4,12},{5,13},{6,14},{7,15},{8,0},{9,1},... | collective-permute-start | bytes 1572872 | tf_op jit(solution)/shard_map/ppermute | solution.py:594
  62.9 21.5 %collective-permute-start.1 = (bf16[2048,128]{1,0:T(8,128)(2,1)}, bf16[2048,128]{1,0:T(8,128)(2,1)}, u32[]{:S(2)}, u32[]{:S(2)}) collective-permute-start(bf16[2048,128]{1,0:T(8,128)(2,1)} %copy-done.5), channel_id=1, source_target_pairs={{0,2},{1,3},{2,0},{3,1},{4,6},{5,7},{6,4},{7,5},{8,10},{9,11},{10,... | collective-permute-start | bytes 1572872 | tf_op jit(solution)/shard_map/ppermute | solution.py:594
  74.5 24.6 %collective-permute-start = (bf16[2048,128]{1,0:T(8,128)(2,1)}, bf16[2048,128]{1,0:T(8,128)(2,1)}, u32[]{:S(2)}, u32[]{:S(2)}) collective-permute-start(bf16[2048,128]{1,0:T(8,128)(2,1)} %copy-done.5), channel_id=1, source_target_pairs={{0,1},{1,0},{2,3},{3,2},{4,5},{5,4},{6,7},{7,6},{8,9},{9,8},{10,11... | collective-permute-start | bytes 1572872 | tf_op jit(solution)/shard_map/ppermute | solution.py:594
  82.8 14.7 %collective-permute-start.21 = (f32[1280,128]{1,0:T(8,128)}, f32[1280,128]{1,0:T(8,128)S(1)}, u32[]{:S(2)}, u32[]{:S(2)}) collective-permute-start(f32[1280,128]{1,0:T(8,128)} %get-tuple-element.24), channel_id=1, source_target_pairs={{0,1},{1,0},{2,3},{3,2},{4,5},{5,4},{6,7},{7,6},{8,9},{9,8},{10,11... | collective-permute-start | bytes 1966088 | tf_op jit(solution)/shard_map/ppermute | solution.py:594
  82.9 14.6 %collective-permute-start.5 = (bf16[2048,128]{1,0:T(8,128)(2,1)}, bf16[2048,128]{1,0:T(8,128)(2,1)S(1)}, u32[]{:S(2)}, u32[]{:S(2)}) collective-permute-start(bf16[2048,128]{1,0:T(8,128)(2,1)} %collective-permute-done.3.refs_4_), channel_id=1, source_target_pairs={{0,2},{1,3},{2,0},{3,1},{4,6},{5,7},{6,4},{7,5},{8,10},{9,11},{10,... | collective-permute-start | bytes 1572872 | tf_op jit(solution)/shard_map/ppermute | solution.py:594
  83.7 15.4 %collective-permute-start.4 = (bf16[2048,128]{1,0:T(8,128)(2,1)}, bf16[2048,128]{1,0:T(8,128)(2,1)S(1)}, u32[]{:S(2)}, u32[]{:S(2)}) collective-permute-start(bf16[2048,128]{1,0:T(8,128)(2,1)} %collective-permute-done.3.refs_4_), channel_id=1, source_target_pairs={{0,1},{1,0},{2,3},{3,2},{4,5},{5,4},{6,7},{7,6},{8,9},{9,8},{10,11... | collective-permute-start | bytes 1572872 | tf_op jit(solution)/shard_map/ppermute | solution.py:594
  84.4 14.7 %collective-permute-start.2 = (bf16[2048,128]{1,0:T(8,128)(2,1)}, bf16[2048,128]{1,0:T(8,128)(2,1)S(1)}, u32[]{:S(2)}, u32[]{:S(2)}) collective-permute-start(bf16[2048,128]{1,0:T(8,128)(2,1)} %collective-permute-done.1.refs_2_), channel_id=1, source_target_pairs={{0,1},{1,0},{2,3},{3,2},{4,5},{5,4},{6,7},{7,6},{8,9},{9,8},{10,11... | collective-permute-start | bytes 1572872 | tf_op jit(solution)/shard_map/ppermute | solution.py:594
  97.6 10.2 %collective-permute-start.22 = (f32[640,128]{1,0:T(8,128)S(1)}, f32[640,128]{1,0:T(8,128)S(1)}, u32[]{:S(2)}, u32[]{:S(2)}) collective-permute-start(f32[640,128]{1,0:T(8,128)S(1)} %slice_add_fusion), channel_id=1, source_target_pairs={{0,2},{1,3},{2,0},{3,1},{4,6},{5,7},{6,4},{7,5},{8,10},{9,11},{10,... | collective-permute-start | bytes 983048 | tf_op jit(solution)/shard_map/ppermute | solution.py:594
  109.6 7.1 %collective-permute-start.26 = (bf16[128,128]{1,0:T(8,128)(2,1)S(1)}, bf16[128,128]{1,0:T(8,128)(2,1)S(1)}, u32[]{:S(2)}, u32[]{:S(2)}) collective-permute-start(bf16[128,128]{1,0:T(8,128)(2,1)S(1)} %get-tuple-element.31), channel_id=1, source_target_pairs={{0,12},{1,13},{2,14},{3,15},{4,8},{5,9},{6,10},{7,11},{8,4},{9,5},... | collective-permute-start | bytes 98312 | tf_op jit(solution)/shard_map/ppermute | solution.py:594
  116.7 8.0 %collective-permute-start.27 = (bf16[4,128,128]{2,1,0:T(8,128)(2,1)S(1)}, bf16[4,128,128]{2,1,0:T(8,128)(2,1)S(1)}, u32[]{:S(2)}, u32[]{:S(2)}) collective-permute-start(bf16[4,128,128]{2,1,0:T(8,128)(2,1)S(1)} %pad_maximum_fusion.2.near_ref), channel_id=1, source_target_pairs={{0,2},{1,3},{2,0},{3,1},{4,6},{5,7},{6,4},{7,5},{8,10},{9,11},{10,... | collective-permute-start | bytes 393224 | tf_op jit(solution)/shard_map/ppermute | solution.py:594
  124.5 8.2 %collective-permute-start.24 = (f32[520,128]{1,0:T(8,128)S(1)}, f32[520,128]{1,0:T(8,128)S(1)}, u32[]{:S(2)}, u32[]{:S(2)}) collective-permute-start(f32[520,128]{1,0:T(8,128)S(1)} %attend_prefix.3), channel_id=1, source_target_pairs={{0,4},{1,5},{2,6},{3,7},{4,0},{5,1},{6,2},{7,3},{8,12},{9,13},{10,... | collective-permute-start | bytes 798728 | tf_op jit(solution)/shard_map/ppermute | solution.py:594
  (19 other events, 256.5 us)

commit v2 on v0

--- a/solution.py
+++ b/solution.py
@@ -1,6 +1,10 @@
+import functools
+
 import jax
 import jax.numpy as jnp
 from jax import lax
+from jax.experimental import pallas as pl
+from jax.experimental.pallas import tpu as pltpu
 from jax.sharding import PartitionSpec as P
 
 OWN = 2
@@ -181,9 +185,636 @@
     return (attn_out, decode_pages)
 
 
+VMEM_LIMIT = 48 * 1024 * 1024
+CHUNK = 512
+SUM_ROWS = 16
+
+
+def in_vmem(count):
+    return [pl.BlockSpec(memory_space=pltpu.VMEM)] * count
+
+
+def in_smem(count):
+    return [pl.BlockSpec(memory_space=pltpu.SMEM)] * count
+
+
+def params():
+    return pltpu.CompilerParams(vmem_limit_bytes=VMEM_LIMIT)
+
+
+def cost(flops, nbytes):
+    return pl.CostEstimate(flops=flops, bytes_accessed=nbytes, transcendentals=0)
+
+
+def nt_dot(left, right):
+    return lax.dot_general(
+        left, right, (((1,), (1,)), ((), ())), preferred_element_type=jnp.float32
+    )
+
+
+def holder_of(page, pool_dev):
+    if pool_dev & (pool_dev - 1) == 0:
+        return jnp.right_shift(page, pool_dev.bit_length() - 1)
+    return page // pool_dev
+
+
+def pick_pages_kernel(place_ref, hits_ref, pool_ref, mine_ref, other_ref, held, sems):
+    me, head = place_ref[0], place_ref[1]
+    pool_dev, page_len = pool_ref.shape[0], pool_ref.shape[1]
+    slots = held.shape[0]
+    rows = 2 * page_len
+    out_row = lax.broadcasted_iota(jnp.int32, (rows, rows), 0)
+    in_row = lax.broadcasted_iota(jnp.int32, (rows, rows), 1)
+    wanted = jnp.where(out_row < page_len, 2 * out_row, 2 * (out_row - page_len) + 1)
+    unweave = (in_row == wanted).astype(jnp.bfloat16)
+
+    def fetch(page, slot):
+        return pltpu.make_async_copy(pool_ref.at[page], held.at[slot], sems.at[slot])
+
+    def entry(e, count):
+        page = hits_ref[e]
+        is_mine = (page >= 0) & (holder_of(page, pool_dev) == me)
+
+        @pl.when(is_mine)
+        def _():
+            fetch(page - me * pool_dev, count).start()
+
+        return count + is_mine.astype(jnp.int32)
+
+    count = lax.fori_loop(0, hits_ref.shape[0], entry, jnp.int32(0))
+
+    def arrive(slot, carry):
+        fetch(0, slot).wait()
+        return carry
+
+    lax.fori_loop(0, count, arrive, 0)
+    for slot in range(slots):
+        at = slice(slot * rows, (slot + 1) * rows)
+        slab = held[slot]
+        first = slab[:, :, :128].reshape(rows, 128)
+        second = slab[:, :, 128:].reshape(rows, 128)
+        both = jnp.concatenate([first, second], axis=1)
+        both = jnp.dot(unweave, both, preferred_element_type=jnp.float32)
+        both = both.astype(jnp.bfloat16)
+        mine_ref[at, :] = jnp.where(head == 0, both[:, :128], both[:, 128:])
+        other_ref[at, :] = jnp.where(head == 0, both[:, 128:], both[:, :128])
+
+
+def pick_pages(place, hits, pool, slots):
+    rows = slots * 2 * pool.shape[1]
+    block = jax.ShapeDtypeStruct((rows, 128), jnp.bfloat16)
+    return pl.pallas_call(
+        pick_pages_kernel,
+        out_shape=(block, block),
+        in_specs=in_smem(2) + [pl.BlockSpec(memory_space=pl.ANY)],
+        out_specs=tuple(in_vmem(2)),
+        scratch_shapes=[
+            pltpu.VMEM((slots,) + pool.shape[1:], jnp.bfloat16),
+            pltpu.SemaphoreType.DMA((slots,)),
+        ],
+        compiler_params=params(),
+        cost_estimate=cost(0, 4 * pool.size),
+        name="pick_pages",
+    )(place, hits, pool)
+
+
+def column_to_row(column):
+    return jnp.transpose(jnp.broadcast_to(column, (128, 128)))[0:1]
+
+
+def row_to_column(row):
+    return jnp.transpose(jnp.broadcast_to(row, (128, 128)))[:, 0:1]
+
+
+def plane_order(plane):
+    return [0, jnp.where(plane <= 2, 1, 3), 2, jnp.where(plane <= 2, 3, 1)]
+
+
+def pack_weights_kernel(place_ref, wq_ref, wk_ref, wv_ref, *refs):
+    own_ref, core_ref, side_ref, wk, wv, sems = refs
+    plane, lane = place_ref[2], place_ref[3]
+    feats = wk.shape[0]
+    block = wq_ref.shape[0] // 16
+    half = own_ref.shape[0]
+    parts = []
+    for r, out_ref in enumerate((own_ref, core_ref, side_ref, side_ref)):
+        for k, offset in enumerate(plane_order(plane)):
+            start = (((plane + offset) & 3) * 4 + (lane ^ r)) * block
+            base = half if r == 3 else 0
+            parts.append((out_ref, base, k, pl.multiple_of(start, block)))
+    copies = [
+        pltpu.make_async_copy(
+            wq_ref.at[pl.ds(start, block)],
+            out_ref.at[pl.ds(base + k * block, block)],
+            sems.at[n],
+        )
+        for n, (out_ref, base, k, start) in enumerate(parts)
+    ]
+    copies.append(pltpu.make_async_copy(wk_ref, wk, sems.at[16]))
+    copies.append(pltpu.make_async_copy(wv_ref, wv, sems.at[17]))
+    for copy in copies[16:] + copies[:16]:
+        copy.start()
+    for copy in copies[16:]:
+        copy.wait()
+    for out_ref, base, k, start in parts:
+        for j in range(block // 128):
+            at = base + 4 * block + (k * (block // 128) + j) * 2 * feats
+            columns = pl.ds(pl.multiple_of(start + j * 128, 128), 128)
+            out_ref[at : at + feats, :] = wk[:, columns]
+            out_ref[at + feats : at + 2 * feats, :] = wv[:, columns]
+    for copy in copies[:16]:
+        copy.wait()
+
+
+def pack_weights(place, wq, wk_t, wv_t):
+    rows = wq.shape[0] // 4 + 2 * wk_t.shape[0] * wk_t.shape[1] // 4 // 128
+    block = jax.ShapeDtypeStruct((rows, 128), jnp.bfloat16)
+    return pl.pallas_call(
+        pack_weights_kernel,
+        out_shape=(block, block, jax.ShapeDtypeStruct((2 * rows, 128), jnp.bfloat16)),
+        in_specs=in_smem(1) + [pl.BlockSpec(memory_space=pl.ANY)] * 3,
+        out_specs=tuple(in_vmem(3)),
+        scratch_shapes=[
+            pltpu.VMEM(wk_t.shape, jnp.bfloat16),
+            pltpu.VMEM(wv_t.shape, jnp.bfloat16),
+            pltpu.SemaphoreType.DMA((18,)),
+        ],
+        compiler_params=params(),
+        cost_estimate=cost(0, 2 * wq.size),
+        name="pack_weights",
+    )(place, wq, wk_t, wv_t)
+
+
+def project_block(k, raw, inv, gain_ref, weights, block):
+    chunks = block // 128
+    normed = (raw.astype(jnp.float32) * inv * gain_ref[k : k + 1, :]).astype(jnp.bfloat16)
+    wide = jnp.concatenate([ref[k * block : (k + 1) * block, :] for ref in weights], axis=1)
+    kv_rows = []
+    for ref in weights:
+        pieces = []
+        for j in range(chunks):
+            at = 4 * block + (k * chunks + j) * 32
+            pieces.append(ref[at : at + 32, :])
+        kv_rows.append(jnp.concatenate(pieces, axis=1))
+    parts = jnp.dot(normed, wide, preferred_element_type=jnp.float32)
+    return parts, nt_dot(jnp.concatenate(kv_rows, axis=0), normed)
+
+
+def add_sums_kernel(hidden_ref, squares_ref, out_ref):
+    toks = hidden_ref.shape[0]
+    out_ref[:toks, :] = hidden_ref[...]
+    left = squares_ref[...]
+    rows = []
+    for _ in range(3):
+        rows.append(left.astype(jnp.bfloat16).astype(jnp.float32))
+        left = left - rows[-1]
+    rows.append(jnp.zeros((SUM_ROWS - 3, toks), jnp.float32))
+    out_ref[toks:, :] = jnp.concatenate(rows, axis=0).astype(jnp.bfloat16)
+
+
+def add_sums(hidden, squares):
+    toks, block = hidden.shape
+    return pl.pallas_call(
+        add_sums_kernel,
+        out_shape=jax.ShapeDtypeStruct((toks + SUM_ROWS, block), jnp.bfloat16),
+        in_specs=in_vmem(2),
+        out_specs=in_vmem(1)[0],
+        compiler_params=params(),
+        cost_estimate=cost(0, 1 << 20),
+        name="add_sums",
+    )(hidden, squares.reshape(1, toks))
+
+
+def project_kernel(place_ref, gain_ref, own_ref, *refs):
+    downs, ups, weights, out_refs = refs[0:3], refs[3:6], refs[6:10], refs[10:]
+    plane = place_ref[2]
+    block = own_ref.shape[1]
+    toks = own_ref.shape[0] - SUM_ROWS
+    sources = (
+        lambda at: own_ref[at],
+        lambda at: jnp.where(plane <= 2, downs[0][at], ups[0][at]),
+        lambda at: jnp.where(plane <= 1, downs[1][at], ups[1][at]),
+        lambda at: jnp.where(
+            plane == 0, downs[2][at], jnp.where(plane == 3, ups[2][at], ups[0][at])
+        ),
+    )
+    squares = sum(
+        jnp.sum(source(slice(toks, toks + SUM_ROWS)).astype(jnp.float32), axis=0, keepdims=True)
+        for source in sources
+    )
+    inv = lax.rsqrt(squares / (block * 16) + EPS)
+    inv = jnp.concatenate(
+        [row_to_column(inv[:, t : t + 128]) for t in range(0, toks, 128)], axis=0
+    )
+    query, kv_total = None, None
+    for k, source in enumerate(sources):
+        parts, kv_part = project_block(k, source(slice(0, toks)), inv, gain_ref, weights, block)
+        query = parts if k == 0 else query + parts
+        kv_total = kv_part if k == 0 else kv_total + kv_part
+    half = toks // 2
+    for n, out_ref in enumerate(out_refs):
+        r, rows = n // 2, slice(n % 2 * half, (n % 2 + 1) * half)
+        out_ref[:half, :] = query[rows, r * 128 : (r + 1) * 128]
+        for t in range(half // 128):
+            chunk = slice(rows.start + t * 128, rows.start + (t + 1) * 128)
+            out_ref[half + t * 32 : half + (t + 1) * 32, :] = kv_total[r * 32 : (r + 1) * 32, chunk]
+
+
+def project(place, gain, downs, ups, weights):
+    toks = downs[0].shape[0] - SUM_ROWS
+    out = jax.ShapeDtypeStruct(((toks + 128) // 2, 128), jnp.float32)
+    return pl.pallas_call(
+        project_kernel,
+        out_shape=(out,) * 8,
+        in_specs=in_smem(1) + in_vmem(12),
+        out_specs=tuple(in_vmem(8)),
+        compiler_params=params(),
+        cost_estimate=cost(2 * toks * 512 * 640, 6 << 20),
+        name="project",
+    )(place, gain, *downs, *ups[1:], *weights)
+
+
+def finish_kernel(*refs):
+    cos_ref, sin_ref, out_ref = refs[6:]
+    toks = cos_ref.shape[0]
+    half, kv_rows = toks // 2, 64
+    for n in range(2):
+        rows = slice(n * half, (n + 1) * half)
+        total = refs[n][...] + refs[2 + n][...] + refs[4 + n][...]
+        query = total[:half]
+        swapped = jnp.concatenate([query[:, 64:], query[:, :64]], axis=1)
+        rotated = query * cos_ref[rows, :] + swapped * sin_ref[rows, :]
+        out_ref[rows, :] = rotated.astype(jnp.bfloat16)
+        at = toks + n * kv_rows
+        out_ref[at : at + kv_rows, :] = total[half:].astype(jnp.bfloat16)
+
+
+def finish(own, got, far_sum, cos_wide, sin_wide):
+    toks = cos_wide.shape[0]
+    return pl.pallas_call(
+        finish_kernel,
+        out_shape=jax.ShapeDtypeStruct((toks + 128, 128), jnp.bfloat16),
+        in_specs=in_vmem(8),
+        out_specs=in_vmem(1)[0],
+        compiler_params=params(),
+        cost_estimate=cost(0, 2 << 20),
+        name="finish_projection",
+    )(*own, *got, *far_sum, cos_wide, sin_wide)
+
+
+def lane_tiles(values, join):
+    joined = values[:, :128]
+    for start in range(128, values.shape[1], 128):
+        joined = join(joined, values[:, start : start + 128])
+    return joined
+
+
+def put_state(out_ref, toks, first, acc, top, total):
+    out_ref[first : first + acc.shape[0], :] = acc
+    for b in range(acc.shape[0] // 128):
+        row, part = toks + first // 128 + b, slice(b * 128, (b + 1) * 128)
+        out_ref[row : row + 1, :] = column_to_row(top[part])
+        out_ref[row + 4 : row + 5, :] = column_to_row(total[part])
+
+
+def get_state(ref, toks, first, count):
+    rows = range(toks + first // 128, toks + (first + count) // 128)
+    top = [row_to_column(ref[row : row + 1, :]) for row in rows]
+    total = [row_to_column(ref[row + 4 : row + 5, :]) for row in rows]
+    return ref[first : first + count, :], jnp.concatenate(top), jnp.concatenate(total)
+
+
+def merge_states(states):
+    peak = functools.reduce(jnp.maximum, [top for _, top, _ in states])
+    base = jnp.where(peak == -jnp.inf, 0.0, peak)
+    fades = [jnp.exp(top - base) for _, top, _ in states]
+    acc = sum(acc * fade for (acc, _, _), fade in zip(states, fades))
+    total = sum(total * fade for (_, _, total), fade in zip(states, fades))
+    return acc, peak, total
+
+
+def attend_kernel(offset, page_len, earlier, table_ref, *refs):
+    blocks, (own_ref, far_ref), refs = refs[:4], refs[4:6], refs[6:]
+    before = refs[:2] if earlier else ()
+    outs, (held, keys, values, scores_ref, acc, lanes, sems) = refs[-9:-7], refs[-7:]
+    copies = [
+        pltpu.make_async_copy(block, held.at[n], sems.at[n]) for n, block in enumerate(blocks)
+    ]
+    for copy in copies:
+        copy.start()
+    me = table_ref[0] ^ offset
+    toks = outs[0].shape[0] - 8
+    new_len = toks // 2
+    chunk_pages = CHUNK // page_len
+    for copy in copies:
+        copy.wait()
+    for request in range(2):
+        last_holder = table_ref[1 + request]
+        has_last = (last_holder & 12) == (me & 12)
+        pages = jnp.int32(0)
+        for n in range(4):
+            holder = (me & 12) | ((last_holder + 1 + n) & 3)
+            count = table_ref[5 + request * 16 + holder]
+            first = table_ref[5 + holder] if request else jnp.int32(0)
+            which = (holder ^ me) & 3
+
+            def move(p, carry, which=which, first=first, pages=pages):
+                source = pl.multiple_of((first + p) * 2 * page_len, 2 * page_len)
+                target = pl.multiple_of((pages + p) * page_len, page_len)
+                keys[pl.ds(target, page_len), :] = held[which, pl.ds(source, page_len), :]
+                values[pl.ds(target, page_len), :] = held[
+                    which, pl.ds(source + page_len, page_len), :
+                ]
+                return carry
+
+            lax.fori_loop(0, count, move, 0)
+            pages = pages + count
+        trips = (pages + chunk_pages - 1) // chunk_pages
+
+        def clear(p, carry):
+            target = pl.multiple_of(p * page_len, page_len)
+            values[pl.ds(target, page_len), :] = jnp.zeros((page_len, 128), jnp.bfloat16)
+            return carry
+
+        lax.fori_loop(pages, trips * chunk_pages, clear, 0)
+        keys_here = pages * page_len - jnp.where(has_last, table_ref[3 + request], 0)
+        rows = slice(request * new_len, (request + 1) * new_len)
+        query = jnp.concatenate([far_ref[rows, :], own_ref[rows, :]], axis=0)
+        lanes[...] = jnp.full_like(lanes, -jnp.inf)
+
+        def score(n, carry, query=query, keys_here=keys_here):
+            at = pl.ds(pl.multiple_of(n * CHUNK, CHUNK), CHUNK)
+            scores = nt_dot(query, keys[at, :]) * 128**-0.5
+            column = lax.broadcasted_iota(jnp.int32, scores.shape, 1)
+            scores = jnp.where(column < keys_here - n * CHUNK, scores, -jnp.inf)
+            scores_ref[:, at] = scores
+            lanes[...] = jnp.maximum(lanes[...], lane_tiles(scores, jnp.maximum))
+            return carry
+
+        lax.fori_loop(0, trips, score, 0)
+        top = jnp.max(lanes[...], axis=1, keepdims=True)
+        lanes[...] = jnp.zeros_like(lanes)
+        acc[...] = jnp.zeros_like(acc)
+
+        def mix(n, carry, top=top):
+            at = pl.ds(pl.multiple_of(n * CHUNK, CHUNK), CHUNK)
+            exps = jnp.exp(scores_ref[:, at] - top)
+            lanes[...] += lane_tiles(exps, jnp.add)
+            acc[...] += jnp.dot(
+                exps.astype(jnp.bfloat16), values[at, :], preferred_element_type=jnp.float32
+            )
+            return carry
+
+        lax.fori_loop(0, trips, mix, 0)
+        total = jnp.sum(lanes[...], axis=1, keepdims=True)
+        for n, out_ref in enumerate(outs):
+            part = slice(n * new_len, (n + 1) * new_len)
+            state = (acc[part, :], top[part], total[part])
+            if earlier:
+                past = get_state(before[n], toks, request * new_len, new_len)
+                state = merge_states([past, state])
+            put_state(out_ref, toks, request * new_len, *state)
+
+
+def attend(offset, table, blocks, own_query, far_query, earlier, toks, span, page_len):
+    new_len = toks // 2
+    state = jax.ShapeDtypeStruct((toks + 8, 128), jnp.float32)
+    return pl.pallas_call(
+        functools.partial(attend_kernel, offset, page_len, bool(earlier)),
+        out_shape=(state, state),
+        in_specs=in_smem(1)
+        + [pl.BlockSpec(memory_space=pl.ANY)] * 4
+        + in_vmem(2 + len(earlier)),
+        out_specs=tuple(in_vmem(2)),
+        scratch_shapes=[
+            pltpu.VMEM((4,) + blocks[0].shape, jnp.bfloat16),
+            pltpu.VMEM((span, 128), jnp.bfloat16),
+            pltpu.VMEM((span, 128), jnp.bfloat16),
+            pltpu.VMEM((toks, span), jnp.float32),
+            pltpu.VMEM((toks, 128), jnp.float32),
+            pltpu.VMEM((toks, 128), jnp.float32),
+            pltpu.SemaphoreType.DMA((4,)),
+        ],
+        compiler_params=params(),
+        cost_estimate=cost(1, 20 << 20),
+        name="attend_far_plane" if offset else "attend_own_plane",
+    )(table, *blocks, own_query, far_query, *earlier)
+
+
+def new_tokens_kernel(
+    place_ref, near_ref, side_ref, core_ref, cos_ref, sin_ref, query_ref, state_ref, page_ref, held, kt, vt
+):
+    me, head = place_ref[0], place_ref[1]
+    toks = cos_ref.shape[1]
+    for n in range(4):
+        held[n] = near_ref[n]
+        held[4 + n] = side_ref[n]
+    for n in range(8):
+        held[8 + n] = core_ref[n]
+    for device in range(16):
+        rel = device ^ me
+        block = held[(rel & 1) * 8 + ((rel >> 1) & 1) * 4 + (rel >> 2)]
+        rows = slice((device % 8) * 16, (device % 8) * 16 + 16)
+        for t in range(toks // 128):
+            columns = slice(t * 128, (t + 1) * 128)
+            kt[device // 8, rows, columns] = block[t * 32 : t * 32 + 16]
+            vt[device // 8, rows, columns] = block[t * 32 + 16 : t * 32 + 32]
+    cos, sin = cos_ref[...], sin_ref[...]
+    for g in range(2):
+        first = kt[g, :64, :].astype(jnp.float32)
+        second = kt[g, 64:, :].astype(jnp.float32)
+        kt[g, :64, :] = (first * cos - second * sin).astype(jnp.bfloat16)
+        kt[g, 64:, :] = (second * cos + first * sin).astype(jnp.bfloat16)
+    new_len = toks // 2
+    query_at = lax.broadcasted_iota(jnp.int32, (new_len, new_len), 0)
+    key_at = lax.broadcasted_iota(jnp.int32, (new_len, new_len), 1)
+    for request in range(2):
+        part = slice(request * new_len, (request + 1) * new_len)
+        scores = jnp.dot(
+            query_ref[part, :], kt[head, :, part], preferred_element_type=jnp.float32
+        )
+        scores = jnp.where(key_at <= query_at, scores * 128**-0.5, -jnp.inf)
+        top = jnp.max(scores, axis=1, keepdims=True)
+        exps = jnp.exp(scores - top)
+        acc = nt_dot(exps.astype(jnp.bfloat16), vt[head, :, part])
+        total = jnp.sum(exps, axis=1, keepdims=True)
+        put_state(state_ref, toks, request * new_len, acc, top, total)
+    page_len = page_ref.shape[1]
+    out_row = lax.broadcasted_iota(jnp.int32, (2 * page_len, 128), 0)
+    token = lax.broadcasted_iota(jnp.int32, (2 * page_len, 128), 1)
+    for slot in range(page_ref.shape[0]):
+        row, has = place_ref[4 + 2 * slot], place_ref[5 + 2 * slot]
+        start = (row // 8) * (toks // 2) + ((row // 2) % 4) * page_len
+        columns = pl.ds(pl.multiple_of(start // 128 * 128, 128), 128)
+        inside = token - start % 128
+        inside = jnp.where(has > 0, inside, -1)
+        take_k = ((out_row % 2 == 0) & (inside == out_row // 2)).astype(jnp.bfloat16)
+        take_v = ((out_row % 2 == 1) & (inside == out_row // 2)).astype(jnp.bfloat16)
+        woven = nt_dot(take_k, kt[row % 2, :, columns]) + nt_dot(take_v, vt[row % 2, :, columns])
+        page_ref[slot] = woven.astype(jnp.bfloat16).reshape(page_len, 2, 128)
+
+
+def new_tokens(place, near, side, core, cos_t, sin_t, query_kv, page_len):
+    toks = cos_t.shape[1]
+    return pl.pallas_call(
+        new_tokens_kernel,
+        out_shape=(
+            jax.ShapeDtypeStruct((toks + 8, 128), jnp.float32),
+            jax.ShapeDtypeStruct((OWN, page_len, 2, 128), jnp.bfloat16),
+        ),
+        in_specs=in_smem(1) + in_vmem(6),
+        out_specs=tuple(in_vmem(2)),
+        scratch_shapes=[
+            pltpu.VMEM((16, 128, 128), jnp.bfloat16),
+            pltpu.VMEM((2, 128, toks), jnp.bfloat16),
+            pltpu.VMEM((2, 128, toks), jnp.bfloat16),
+        ],
+        compiler_params=params(),
+        cost_estimate=cost(0, 2 << 20),
+        name="new_tokens",
+    )(place, near, side, core, cos_t, sin_t, query_kv)
+
+
+def combine_kernel(own_ref, far_ref, new_ref, out_ref):
+    toks = out_ref.shape[0]
+    for first in range(0, toks, 128):
+        states = [get_state(ref, toks, first, 128) for ref in (own_ref, far_ref, new_ref)]
+        acc, _, total = merge_states(states)
+        out_ref[first : first + 128, :] = (acc / total).astype(jnp.bfloat16)
+
+
+def combine(own, far, new):
+    toks = own.shape[0] - 8
+    return pl.pallas_call(
+        combine_kernel,
+        out_shape=jax.ShapeDtypeStruct((toks, 128), jnp.bfloat16),
+        in_specs=in_vmem(3),
+        out_specs=in_vmem(1)[0],
+        compiler_params=params(),
+        cost_estimate=cost(0, 1 << 20),
+        name="combine",
+    )(own, far, new)
+
+
+def swap(values, bits):
+    return lax.ppermute(values, "inst", [(i, i ^ bits) for i in range(16)])
+
+
+def after(values, *others):
+    return lax.optimization_barrier((values, others))[0]
+
+
+def hop(values, step, step_count):
+    pairs = []
+    for i in range(16):
+        plane = i // 4
+        sends = plane >= step_count - 1 if step > 0 else plane <= 4 - step_count
+        if sends and 0 <= plane + step <= 3:
+            pairs.append((i, i + 4 * step))
+    return lax.ppermute(values, "inst", pairs)
+
+
+def on_16_devices(
+    hidden, gain, w_query, w_key, w_value, cache_pool, prefix_len, hit_page, decode_owner
+):
+    me = lax.axis_index("inst")
+    plane, lane = me // 4, me % 4
+    toks, block = hidden.shape
+    pool_dev, page_len = cache_pool.shape[0], cache_pool.shape[1]
+    requests = prefix_len.shape[0]
+    new_len = toks // requests
+    slots = pool_dev // 2
+    head = me // 8
+    rows_new = decode_owner.shape[0]
+    row_ids = jnp.arange(rows_new, dtype=jnp.int32)
+    before_rows = (decode_owner[None, :] == decode_owner[:, None]) & (
+        row_ids[None, :] < row_ids[:, None]
+    )
+    slot_num = jnp.sum(before_rows.astype(jnp.int32), axis=1)
+    owned = (decode_owner[None, :] == me) & (
+        slot_num[None, :] == jnp.arange(OWN, dtype=jnp.int32)[:, None]
+    )
+    pick_row = jnp.sum(jnp.where(owned, row_ids[None, :], 0), axis=1)
+    has_row = jnp.any(owned, axis=1).astype(jnp.int32)
+    place = jnp.stack([me, head, plane, lane]).astype(jnp.int32)
+    page_place = jnp.concatenate([place, jnp.stack([pick_row, has_row], 1).reshape(-1)])
+    hits = hit_page.reshape(-1)
+
+    holders = jnp.where(hit_page >= 0, hit_page // pool_dev, -1)
+    counts = jnp.sum(
+        (holders[:, :, None] == jnp.arange(16, dtype=jnp.int32)).astype(jnp.int32), axis=1
+    )
+    last_page = (prefix_len - 1) // page_len
+    is_last = jnp.arange(hit_page.shape[1], dtype=jnp.int32)[None, :] == last_page[:, None]
+    last_holder = jnp.sum(jnp.where(is_last, holders, 0), axis=1)
+    missing = (last_page + 1) * page_len - prefix_len
+    table = jnp.concatenate([me[None], last_holder, missing, counts.reshape(-1)]).astype(jnp.int32)
+
+    wide = hidden.astype(jnp.float32)
+    squares = jnp.sum(wide * wide, axis=1)
+    for bit in (1, 2):
+        squares = squares + swap(squares, bit)
+
+    w_own, w_core, w_side = pack_weights(place, w_query, w_key.T, w_value.T)
+    w_side = swap(after(w_side, squares), 2)
+    rows = w_own.shape[0]
+    weights = [w_own, swap(w_core, 1), w_side, swap(w_side[rows:], 1)]
+
+    mine, other = pick_pages(place, hits, cache_pool, slots)
+    first = add_sums(hidden, squares)
+    downs, ups = [first], [first]
+    for k in (1, 2, 3):
+        down, up = downs[-1], ups[-1]
+        if k == 2:
+            down, up = after((down, up), mine)
+        downs.append(hop(down, -1, k))
+        ups.append(hop(up, 1, k))
+
+    mine_side = swap(after(mine, w_side), 2)
+    far_pages = swap(after(other, downs[2], ups[2]), 8)
+
+    positions = (
+        jnp.repeat(prefix_len, new_len) + jnp.tile(jnp.arange(new_len, dtype=jnp.int32), requests)
+    ).astype(jnp.float32)
+    cos_table, sin_table = rotary_tables(positions, 128)
+    cos_wide = jnp.concatenate([cos_table, cos_table], axis=1)
+    sin_wide = jnp.concatenate([-sin_table, sin_table], axis=1)
+
+    gain_blocks = lax.dynamic_index_in_dim(gain.reshape(4, 4, block), lane, 1, keepdims=False)
+    gain_blocks = gain_blocks[(plane + jnp.stack(plane_order(plane))) & 3]
+    sums = project(place, gain_blocks, downs, ups, weights)
+    got = [swap(part, 1) for part in sums[2:4] + sums[6:8]]
+    far_sum = [swap(sums[4 + n] + got[2 + n], 2) for n in range(2)]
+    far_sum = after(far_sum, far_pages)
+    query_kv = finish(sums[:2], got[:2], far_sum, cos_wide, sin_wide)
+
+    far_side = swap(after(far_pages, far_sum), 2)
+    near_pages = [mine, swap(mine, 1), mine_side, swap(mine_side, 1)]
+    away_pages = [far_pages, swap(far_pages, 1), far_side, swap(far_side, 1)]
+
+    from_plane = swap(query_kv, 4)
+    kv = query_kv[toks:]
+    far_kv = (swap(kv, 8), swap(kv, 12))
+
+    span = hit_page.shape[1] * page_len
+    sizes = (toks, span, page_len)
+    part = attend(0, table, near_pages, query_kv, from_plane, (), *sizes)
+    far_kv = after(far_kv, part)
+    near_kv = jnp.stack([kv, from_plane[toks:], *far_kv])
+    side_kv = swap(near_kv, 2)
+    core_kv = swap(jnp.concatenate([near_kv, side_kv], axis=0), 1)
+    partner_part, own_part = attend(8, table, away_pages, query_kv, from_plane, part, *sizes)
+    partner_part = swap(partner_part, 4)
+    new_part, decode_pages = new_tokens(
+        page_place, near_kv, side_kv, core_kv, cos_table.T, sin_table.T, query_kv, page_len
+    )
+    attn_out = combine(own_part, partner_part, new_part)
+    return (attn_out, decode_pages)
+
+
 def solution(mesh):
     return jax.shard_map(
-        on_device,
+        on_16_devices if mesh.shape["inst"] == 16 else on_device,
         mesh=mesh,
         in_specs=(
             P("groups", "inst"),

time: 310 us -> 126 us (0.41)
  waiting for transfers between devices: 173 us -> 45.6 us
  blocking collectives: 44.3 us -> 0 us
  Pallas kernels: 0 us -> 29.9 us
  starting transfers between devices: 7.62 us -> 36 us
  local copies, waits for them, and re-layouts: 27.3 us -> 7.92 us
  matrix products: 19.3 us -> 0 us
  other arithmetic: 23.5 us -> 5.03 us
  between operations: 14.3 us -> 1.09 us
    all_gather x1 -> x0, waiting for transfers between devices: 172 us -> none  [on_device(): gathered = lax.all_gather(hidden, 'inst', axis=1, tiled=True)]
    ppermute x0 -> x30, waiting for transfers between devices: none -> 45.6 us  [the longest x24 37.8 us: swap(): return lax.ppermute(values, 'inst', [(i, i ^ bits) for i in range(16)])]
    all_gather x1 -> x0, blocking collectives: 44.3 us -> none  [on_device(): all_kv = lax.all_gather(new_kv, 'inst', axis=1, tiled=True)]
    ppermute x0 -> x30, starting transfers between devices: none -> 36 us  [the longest x24 24.6 us: swap(): return lax.ppermute(values, 'inst', [(i, i ^ bits) for i in range(16)])]
    pallas_call x0 -> x9, Pallas kernels: none -> 29.9 us  [the longest x2 11.1 us: attend(): pl.pallas_call(functools.partial(attend_kernel, offset, page_len, bool(ea...]
    dot_general x11 -> x0, matrix products: 19.3 us -> none  [the longest x2 8.05 us: contract_first(): lax.dot_general(weights, rows, (((0,), (1,)), ((), ())), preferred_elemen...]
    gather x5 -> x1, local copies, waits for them, and re-layouts: 14.7 us -> 0.56 us  [on_16_devices(): gain_blocks = gain_blocks[plane + jnp.stack(plane_order(plane)) & 3]]
    convert_element_type x2 -> x1, other arithmetic: 9.92 us -> 0.01 us  [on_16_devices(): has_row = jnp.any(owned, axis=1).astype(jnp.int32)]
  transfers between devices with their start and end apart: 2 -> 30, of which waited for: 1 -> 13; matrix products, arithmetic and copies ran while one was open for 17% -> 5% of each run, Pallas kernels for 0% -> 23%
where the time goes in v2:
time: 126 us
  waiting for transfers between devices  45.6 us (36%)
  starting transfers between devices  36 us (29%)
  Pallas kernels  29.9 us (24%)
  local copies, waits for them, and re-layouts  7.92 us (6%)
  other arithmetic  5.03 us (4%)
    ppermute x24, waiting for transfers between devices, swap(): return lax.ppermute(values, 'inst', [(i, i ^ bits) for i in range(16)])  37.8 us
    ppermute x24, starting transfers between devices, swap(): return lax.ppermute(values, 'inst', [(i, i ^ bits) for i in range(16)])  24.6 us
    ppermute x6, starting transfers between devices, hop(): return lax.ppermute(values, 'inst', pairs)  11.4 us
    pallas_call x2, Pallas kernels, attend(): pl.pallas_call(functools.partial(attend_kernel, offset, page_len, bool(ea...  11.1 us
    ppermute x6, waiting for transfers between devices, hop(): return lax.ppermute(values, 'inst', pairs)  7.76 us
    pallas_call x1, Pallas kernels, pick_pages(): pl.pallas_call(pick_pages_kernel, out_shape=(block, block), in_specs=in_s...  5.19 us
    pallas_call x1, Pallas kernels, project(): pl.pallas_call(project_kernel, out_shape=(out,) * 8, in_specs=in_smem(1)...  4.97 us
    pallas_call x1, Pallas kernels, pack_weights(): pl.pallas_call(pack_weights_kernel, out_shape=(block, block, jax.ShapeDty...  4.94 us
  transfers between devices with their start and end apart: 30, of which 13 were waited for; matrix products, arithmetic and copies ran while one was open for 5% of the time, Pallas kernels for 23%

profile of v2, /device:TPU:0, one launch (start us, length us, event | category | flops | bytes accessed | tf_op | source)
XLA Modules:
  0.0 125.5 jit_solution(8210692452020464444)
XLA Ops:
  3.3 2.9 %collective-permute-start.1 = (f32[512]{0:T(512)S(1)}, f32[512]{0:T(512)S(1)}, u32[]{:S(2)}, u32[]{:S(2)}) collective-permute-start(f32[512]{0:T(512)S(1)} %add.61), channel_id=1, source_target_pairs={{0,2},{1,3},{2,0},{3,1},{4,6},{5,7},{6,4},{7,5},{8,10},{9,11},{10,... | collective-permute-start | bytes 6152 | tf_op jit(solution)/shard_map/ppermute | solution.py:700
  9.7 4.9 %pack_weights.1 = (bf16[2560,128]{1,0:T(8,128)(2,1)S(1)}, bf16[2560,128]{1,0:T(8,128)(2,1)}, bf16[5120,128]{1,0:T(8,128)(2,1)}) custom-call(s32[4]{0:T(128)S(1)} %pad_add_fusion.2.place_ref, bf16[8192,128]{1,0:T(8,128)(2,1)S(1)} %copy-done, bf16[16,8192]{1,0:T(8,128)(2,1)S(1)} %bitcast.31, bf16[16,8192]{1,0:T(8,128)(2,1)S(1)} %bitcast.32), custom_call_target="tpu_custom_call" | custom-call | bytes 2097152 | tf_op jit(solution)/shard_map/pack_weights/pallas_call | solution.py:332
  16.8 5.4 %collective-permute-start.3 = (bf16[528,512]{1,0:T(8,128)(2,1)S(1)}, bf16[528,512]{1,0:T(8,128)(2,1)}, u32[]{:S(2)}, u32[]{:S(2)}) collective-permute-start(bf16[528,512]{1,0:T(8,128)(2,1)S(1)} %add_sums.1.own_ref), channel_id=1, source_target_pairs={{0,4},{1,5},{2,6},{3,7},{4,8},{5,9},{6,10},{7,11},{8,12},{9,13},{1... | collective-permute-start | bytes 1622024 | tf_op jit(solution)/shard_map/ppermute | solution.py:714
  22.3 5.2 %pick_pages.1 = (bf16[2048,128]{1,0:T(8,128)(2,1)S(1)}, bf16[2048,128]{1,0:T(8,128)(2,1)}) custom-call(s32[4]{0:T(128)S(1)} %pad_add_fusion.2.place_ref, s32[128]{0:T(128)S(1)} %reshape.118.hits_ref, bf16[32,64,2,256]{3,2,1,0:T(2,128)(2,1)S(1)} %copy-done.1), custom_call_target="tpu_custom_call" | custom-call | bytes 4194304 | tf_op jit(solution)/shard_map/pick_pages/pallas_call | solution.py:266
  28.6 3.2 %collective-permute-done.2.refs_0_ = bf16[528,512]{1,0:T(8,128)(2,1)} collective-permute-done((bf16[528,512]{1,0:T(8,128)(2,1)S(1)}, bf16[528,512]{1,0:T(8,128)(2,1)}, u32[]{:S(2)}, u32[]{:S(2)}) %collective-permute-start.2) | collective-permute-done | bytes 540704 | tf_op jit(solution)/shard_map/ppermute | solution.py:714
  35.0 10.7 %collective-permute-done.11.refs_8_ = bf16[5120,128]{1,0:T(8,128)(2,1)} collective-permute-done((bf16[5120,128]{1,0:T(8,128)(2,1)}, bf16[5120,128]{1,0:T(8,128)(2,1)}, u32[]{:S(2)}, u32[]{:S(2)}) %collective-permute-start.11) | collective-permute-done | bytes 1310752 | tf_op jit(solution)/shard_map/ppermute | solution.py:700
  45.7 2.0 %slice.14 = bf16[2560,128]{1,0:T(8,128)(2,1)} slice(bf16[5120,128]{1,0:T(8,128)(2,1)} %collective-permute-done.11.refs_8_), slice={[2560:5120], [0:128]} | slice | bytes 1310720 | tf_op jit(solution)/shard_map/slice | solution.py:761
  52.1 1.9 %fusion = (f32[512,64]{1,0:T(8,128)}, f32[512,64]{1,0:T(8,128)}, f32[512,64]{1,0:T(8,128)}) fusion(f32[64]{0:T(128)S(1)} %negate_power_fusion, f32[512]{0:T(512)S(1)} %bitcast.37), kind=kLoop, calls=%fused_computation.9 | loop fusion | flops 65536 | bytes 395520 | tf_op jit(solution)/shard_map/neg | solution.py:781
  54.0 6.1 %collective-permute-start.6 = (bf16[2048,128]{1,0:T(8,128)(2,1)}, bf16[2048,128]{1,0:T(8,128)(2,1)}, u32[]{:S(2)}, u32[]{:S(2)}) collective-permute-start(bf16[2048,128]{1,0:T(8,128)(2,1)} %get-tuple-element.35), channel_id=1, source_target_pairs={{0,8},{1,9},{2,10},{3,11},{4,12},{5,13},{6,14},{7,15},{8,0},{9,1},... | collective-permute-start | bytes 1572872 | tf_op jit(solution)/shard_map/ppermute | solution.py:700
  60.7 1.7 %collective-permute-start.23 = (bf16[2048,128]{1,0:T(8,128)(2,1)}, bf16[2048,128]{1,0:T(8,128)(2,1)}, u32[]{:S(2)}, u32[]{:S(2)}) collective-permute-start(bf16[2048,128]{1,0:T(8,128)(2,1)} %copy-done.5), channel_id=1, source_target_pairs={{0,2},{1,3},{2,0},{3,1},{4,6},{5,7},{6,4},{7,5},{8,10},{9,11},{10,... | collective-permute-start | bytes 1572872 | tf_op jit(solution)/shard_map/ppermute | solution.py:700
  62.4 2.0 %collective-permute-done.8.refs_2_ = bf16[528,512]{1,0:T(8,128)(2,1)S(1)} collective-permute-done((bf16[528,512]{1,0:T(8,128)(2,1)S(1)}, bf16[528,512]{1,0:T(8,128)(2,1)S(1)}, u32[]{:S(2)}, u32[]{:S(2)}) %collective-permute-start.8) | collective-permute-done | bytes 540704 | tf_op jit(solution)/shard_map/ppermute | solution.py:714
  64.4 5.0 %project.1 = (f32[320,128]{1,0:T(8,128)S(1)}, f32[320,128]{1,0:T(8,128)S(1)}, f32[320,128]{1,0:T(8,128)}, f32[320,128]{1,0:T(8,128)S(1)}, f32[320,128]{1,0:T(8,1...) custom-call(s32[4]{0:T(128)S(1)} %pad_add_fusion.2.place_ref, ...), custom_call_target="tpu_custom_call" | custom-call | flops 335544320 | bytes 6291456 | tf_op jit(solution)/shard_map/project/pallas_call | solution.py:426
  70.8 1.8 %collective-permute-start.16 = (f32[320,128]{1,0:T(8,128)S(1)}, f32[320,128]{1,0:T(8,128)S(1)}, u32[]{:S(2)}, u32[]{:S(2)}) collective-permute-start(f32[320,128]{1,0:T(8,128)S(1)} %add.68), channel_id=1, source_target_pairs={{0,2},{1,3},{2,0},{3,1},{4,6},{5,7},{6,4},{7,5},{8,10},{9,11},{10,... | collective-permute-start | bytes 491528 | tf_op jit(solution)/shard_map/ppermute | solution.py:700
  73.3 7.8 %collective-permute-done.6.refs_0_ = bf16[2048,128]{1,0:T(8,128)(2,1)} collective-permute-done((bf16[2048,128]{1,0:T(8,128)(2,1)}, bf16[2048,128]{1,0:T(8,128)(2,1)}, u32[]{:S(2)}, u32[]{:S(2)}) %collective-permute-start.6) | collective-permute-done | bytes 524320 | tf_op jit(solution)/shard_map/ppermute | solution.py:700
  83.7 3.6 %collective-permute-done.14.refs_4_ = f32[320,128]{1,0:T(8,128)S(1)} collective-permute-done((f32[320,128]{1,0:T(8,128)S(1)}, f32[320,128]{1,0:T(8,128)S(1)}, u32[]{:S(2)}, u32[]{:S(2)}) %collective-permute-start.14) | collective-permute-done | bytes 163872 | tf_op jit(solution)/shard_map/ppermute | solution.py:700
  89.0 2.9 %collective-permute-start.27 = (bf16[128,128]{1,0:T(8,128)(2,1)S(1)}, bf16[128,128]{1,0:T(8,128)(2,1)S(1)}, u32[]{:S(2)}, u32[]{:S(2)}) collective-permute-start(bf16[128,128]{1,0:T(8,128)(2,1)S(1)} %get-tuple-element.65), channel_id=1, source_target_pairs={{0,12},{1,13},{2,14},{3,15},{4,8},{5,9},{6,10},{7,11},{8,4},{9,5},... | collective-permute-start | bytes 98312 | tf_op jit(solution)/shard_map/ppermute | solution.py:700
  91.9 1.8 %collective-permute-start.17 = (bf16[2048,128]{1,0:T(8,128)(2,1)}, bf16[2048,128]{1,0:T(8,128)(2,1)S(1)}, u32[]{:S(2)}, u32[]{:S(2)}) collective-permute-start(bf16[2048,128]{1,0:T(8,128)(2,1)} %collective-permute-done.6.refs_0_), channel_id=1, source_target_pairs={{0,2},{1,3},{2,0},{3,1},{4,6},{5,7},{6,4},{7,5},{8,10},{9,11},{10,... | collective-permute-start | bytes 1572872 | tf_op jit(solution)/shard_map/ppermute | solution.py:700
  93.8 5.3 %attend_own_plane.1 = (f32[520,128]{1,0:T(8,128)S(1)}, f32[520,128]{1,0:T(8,128)S(1)}) custom-call(s32[37]{0:T(128)S(1)} %pad_add_fusion.1.table_ref, bf16[2048,128]{1,0:T(8,128)(2,1)S(1)} %copy-done.6, bf16[2048,128]{1,0:T(8,128)(2,1)S(1)} %collective-permute-done.22.refs_1_, bf16[2048,128]{1,0:T(8,128)(2,1)} %collective-permute-done.23.refs_2_, ...), custom_call_target="tpu_custom_call" | custom-call | flops 1 | bytes 20971520 | tf_op jit(solution)/shard_map/attend_own_plane/pallas_call | solution.py:582
  99.2 1.8 %collective-permute-start.28 = (bf16[4,128,128]{2,1,0:T(8,128)(2,1)S(1)}, bf16[4,128,128]{2,1,0:T(8,128)(2,1)S(1)}, u32[]{:S(2)}, u32[]{:S(2)}) collective-permute-start(bf16[4,128,128]{2,1,0:T(8,128)(2,1)S(1)} %pad_maximum_fusion.2.near_ref), channel_id=1, source_target_pairs={{0,2},{1,3},{2,0},{3,1},{4,6},{5,7},{6,4},{7,5},{8,10},{9,11},{10,... | collective-permute-start | bytes 393224 | tf_op jit(solution)/shard_map/ppermute | solution.py:700
  101.0 5.9 %collective-permute-done.17.refs_2_ = bf16[2048,128]{1,0:T(8,128)(2,1)S(1)} collective-permute-done((bf16[2048,128]{1,0:T(8,128)(2,1)}, bf16[2048,128]{1,0:T(8,128)(2,1)S(1)}, u32[]{:S(2)}, u32[]{:S(2)}) %collective-permute-start.17) | collective-permute-done | bytes 524320 | tf_op jit(solution)/shard_map/ppermute | solution.py:700
  106.9 2.3 %collective-permute-done.28.side_ref = bf16[4,128,128]{2,1,0:T(8,128)(2,1)S(1)} collective-permute-done((bf16[4,128,128]{2,1,0:T(8,128)(2,1)S(1)}, bf16[4,128,128]{2,1,0:T(8,128)(2,1)S(1)}, u32[]{:S(2)}, u32[]{:S(2)}) %collective-permute-start.28) | collective-permute-done | bytes 131104 | tf_op jit(solution)/shard_map/ppermute | solution.py:700
  109.4 5.8 %attend_far_plane.1 = (f32[520,128]{1,0:T(8,128)S(1)}, f32[520,128]{1,0:T(8,128)S(1)}) custom-call(s32[37]{0:T(128)S(1)} %pad_add_fusion.1.table_ref, bf16[2048,128]{1,0:T(8,128)(2,1)} %collective-permute-done.6.refs_0_, bf16[2048,128]{1,0:T(8,128)(2,1)S(1)} %collective-permute-done.7.refs_1_, bf16[2048,128]{1,0:T(8,128)(2,1)S(1)} %collective-permute-done.17.refs_2_, ...), custom_call_target="tpu_custom_call" | custom-call | flops 1 | bytes 20971520 | tf_op jit(solution)/shard_map/attend_far_plane/pallas_call | solution.py:582
  116.1 2.0 %new_tokens.1 = (f32[520,128]{1,0:T(8,128)S(1)}, bf16[2,64,2,128]{3,2,1,0:T(2,128)(2,1)}) custom-call(s32[8]{0:T(128)S(1)} %concatenate.27.place_ref, bf16[4,128,128]{2,1,0:T(8,128)(2,1)S(1)} %pad_maximum_fusion.2.near_ref, bf16[4,128,128]{2,1,0:T(8,128)(2,1)S(1)} %collective-permute-done.28.side_ref, ...), custom_call_target="tpu_custom_call" | custom-call | bytes 2097152 | tf_op jit(solution)/shard_map/new_tokens/pallas_call | solution.py:659
  118.2 5.9 %collective-permute-done.25.far_ref = f32[520,128]{1,0:T(8,128)S(1)} collective-permute-done((f32[520,128]{1,0:T(8,128)S(1)}, f32[520,128]{1,0:T(8,128)S(1)}, u32[]{:S(2)}, u32[]{:S(2)}) %collective-permute-start.25) | collective-permute-done | bytes 266272 | tf_op jit(solution)/shard_map/ppermute | solution.py:700
  (119 shorter events, 26.6 us)
Async XLA Ops:
  3.3 11.4 %collective-permute-start.1 = (f32[512]{0:T(512)S(1)}, f32[512]{0:T(512)S(1)}, u32[]{:S(2)}, u32[]{:S(2)}) collective-permute-start(f32[512]{0:T(512)S(1)} %add.61), channel_id=1, source_target_pairs={{0,2},{1,3},{2,0},{3,1},{4,6},{5,7},{6,4},{7,5},{8,10},{9,11},{10,... | collective-permute-start | bytes 6152 | tf_op jit(solution)/shard_map/ppermute | solution.py:700
  14.7 31.0 %collective-permute-start.11 = (bf16[5120,128]{1,0:T(8,128)(2,1)}, bf16[5120,128]{1,0:T(8,128)(2,1)}, u32[]{:S(2)}, u32[]{:S(2)}) collective-permute-start(bf16[5120,128]{1,0:T(8,128)(2,1)} %get-tuple-element.39), channel_id=1, source_target_pairs={{0,2},{1,3},{2,0},{3,1},{4,6},{5,7},{6,4},{7,5},{8,10},{9,11},{10,... | collective-permute-start | bytes 3932168 | tf_op jit(solution)/shard_map/ppermute | solution.py:700
  14.8 45.9 %collective-permute-start.10 = (bf16[2560,128]{1,0:T(8,128)(2,1)}, bf16[2560,128]{1,0:T(8,128)(2,1)}, u32[]{:S(2)}, u32[]{:S(2)}) collective-permute-start(bf16[2560,128]{1,0:T(8,128)(2,1)} %get-tuple-element.37), channel_id=1, source_target_pairs={{0,1},{1,0},{2,3},{3,2},{4,5},{5,4},{6,7},{7,6},{8,9},{9,8},{10,11... | collective-permute-start | bytes 1966088 | tf_op jit(solution)/shard_map/ppermute | solution.py:700
  15.5 16.4 %collective-permute-start.2 = (bf16[528,512]{1,0:T(8,128)(2,1)S(1)}, bf16[528,512]{1,0:T(8,128)(2,1)}, u32[]{:S(2)}, u32[]{:S(2)}) collective-permute-start(bf16[528,512]{1,0:T(8,128)(2,1)S(1)} %add_sums.1.own_ref), channel_id=1, source_target_pairs={{4,0},{5,1},{6,2},{7,3},{8,4},{9,5},{10,6},{11,7},{12,8},{13,9},{1... | collective-permute-start | bytes 1622024 | tf_op jit(solution)/shard_map/ppermute | solution.py:714
  16.8 16.2 %collective-permute-start.3 = (bf16[528,512]{1,0:T(8,128)(2,1)S(1)}, bf16[528,512]{1,0:T(8,128)(2,1)}, u32[]{:S(2)}, u32[]{:S(2)}) collective-permute-start(bf16[528,512]{1,0:T(8,128)(2,1)S(1)} %add_sums.1.own_ref), channel_id=1, source_target_pairs={{0,4},{1,5},{2,6},{3,7},{4,8},{5,9},{6,10},{7,11},{8,12},{9,13},{1... | collective-permute-start | bytes 1622024 | tf_op jit(solution)/shard_map/ppermute | solution.py:714
  33.0 16.2 %collective-permute-start.4 = (bf16[528,512]{1,0:T(8,128)(2,1)}, bf16[528,512]{1,0:T(8,128)(2,1)S(1)}, u32[]{:S(2)}, u32[]{:S(2)}) collective-permute-start(bf16[528,512]{1,0:T(8,128)(2,1)} %collective-permute-done.2.refs_0_), channel_id=1, source_target_pairs={{4,0},{5,1},{6,2},{7,3},{8,4},{9,5},{10,6},{11,7},{20,16},{21,17},... | collective-permute-start | bytes 1622024 | tf_op jit(solution)/shard_map/ppermute | solution.py:714
  34.2 16.2 %collective-permute-start.5 = (bf16[528,512]{1,0:T(8,128)(2,1)}, bf16[528,512]{1,0:T(8,128)(2,1)S(1)}, u32[]{:S(2)}, u32[]{:S(2)}) collective-permute-start(bf16[528,512]{1,0:T(8,128)(2,1)} %collective-permute-done.3.refs_3_), channel_id=1, source_target_pairs={{4,8},{5,9},{6,10},{7,11},{8,12},{9,13},{10,14},{11,15},{20,24},{2... | collective-permute-start | bytes 1622024 | tf_op jit(solution)/shard_map/ppermute | solution.py:714
  47.6 16.8 %collective-permute-start.12 = (bf16[2560,128]{1,0:T(8,128)(2,1)}, bf16[2560,128]{1,0:T(8,128)(2,1)}, u32[]{:S(2)}, u32[]{:S(2)}) collective-permute-start(bf16[2560,128]{1,0:T(8,128)(2,1)} %slice.14), channel_id=1, source_target_pairs={{0,1},{1,0},{2,3},{3,2},{4,5},{5,4},{6,7},{7,6},{8,9},{9,8},{10,11... | collective-permute-start | bytes 1966088 | tf_op jit(solution)/shard_map/ppermute | solution.py:700
  49.2 15.2 %collective-permute-start.8 = (bf16[528,512]{1,0:T(8,128)(2,1)S(1)}, bf16[528,512]{1,0:T(8,128)(2,1)S(1)}, u32[]{:S(2)}, u32[]{:S(2)}) collective-permute-start(bf16[528,512]{1,0:T(8,128)(2,1)S(1)} %collective-permute-done.4.refs_1_), channel_id=1, source_target_pairs={{4,0},{5,1},{6,2},{7,3},{20,16},{21,17},{22,18},{23,19}} | collective-permute-start | bytes 1622024 | tf_op jit(solution)/shard_map/ppermute | solution.py:714
  50.5 13.9 %collective-permute-start.9 = (bf16[528,512]{1,0:T(8,128)(2,1)S(1)}, bf16[528,512]{1,0:T(8,128)(2,1)}, u32[]{:S(2)}, u32[]{:S(2)}) collective-permute-start(bf16[528,512]{1,0:T(8,128)(2,1)S(1)} %collective-permute-done.5.refs_4_), channel_id=1, source_target_pairs={{8,12},{9,13},{10,14},{11,15},{24,28},{25,29},{26,30},{27,31}} | collective-permute-start | bytes 1622024 | tf_op jit(solution)/shard_map/ppermute | solution.py:714
  54.0 27.2 %collective-permute-start.6 = (bf16[2048,128]{1,0:T(8,128)(2,1)}, bf16[2048,128]{1,0:T(8,128)(2,1)}, u32[]{:S(2)}, u32[]{:S(2)}) collective-permute-start(bf16[2048,128]{1,0:T(8,128)(2,1)} %get-tuple-element.35), channel_id=1, source_target_pairs={{0,8},{1,9},{2,10},{3,11},{4,12},{5,13},{6,14},{7,15},{8,0},{9,1},... | collective-permute-start | bytes 1572872 | tf_op jit(solution)/shard_map/ppermute | solution.py:700
  60.7 22.4 %collective-permute-start.23 = (bf16[2048,128]{1,0:T(8,128)(2,1)}, bf16[2048,128]{1,0:T(8,128)(2,1)}, u32[]{:S(2)}, u32[]{:S(2)}) collective-permute-start(bf16[2048,128]{1,0:T(8,128)(2,1)} %copy-done.5), channel_id=1, source_target_pairs={{0,2},{1,3},{2,0},{3,1},{4,6},{5,7},{6,4},{7,5},{8,10},{9,11},{10,... | collective-permute-start | bytes 1572872 | tf_op jit(solution)/shard_map/ppermute | solution.py:700
  70.8 12.3 %collective-permute-start.16 = (f32[320,128]{1,0:T(8,128)S(1)}, f32[320,128]{1,0:T(8,128)S(1)}, u32[]{:S(2)}, u32[]{:S(2)}) collective-permute-start(f32[320,128]{1,0:T(8,128)S(1)} %add.68), channel_id=1, source_target_pairs={{0,2},{1,3},{2,0},{3,1},{4,6},{5,7},{6,4},{7,5},{8,10},{9,11},{10,... | collective-permute-start | bytes 491528 | tf_op jit(solution)/shard_map/ppermute | solution.py:700
  72.7 14.5 %collective-permute-start.19 = (f32[320,128]{1,0:T(8,128)}, f32[320,128]{1,0:T(8,128)S(1)}, u32[]{:S(2)}, u32[]{:S(2)}) collective-permute-start(f32[320,128]{1,0:T(8,128)} %get-tuple-element.49), channel_id=1, source_target_pairs={{0,1},{1,0},{2,3},{3,2},{4,5},{5,4},{6,7},{7,6},{8,9},{9,8},{10,11... | collective-permute-start | bytes 491528 | tf_op jit(solution)/shard_map/ppermute | solution.py:700
  72.8 14.5 %collective-permute-start.20 = (f32[320,128]{1,0:T(8,128)S(1)}, f32[320,128]{1,0:T(8,128)S(1)}, u32[]{:S(2)}, u32[]{:S(2)}) collective-permute-start(f32[320,128]{1,0:T(8,128)S(1)} %get-tuple-element.50), channel_id=1, source_target_pairs={{0,1},{1,0},{2,3},{3,2},{4,5},{5,4},{6,7},{7,6},{8,9},{9,8},{10,11... | collective-permute-start | bytes 491528 | tf_op jit(solution)/shard_map/ppermute | solution.py:700
  83.1 8.8 %collective-permute-start.22 = (bf16[2048,128]{1,0:T(8,128)(2,1)S(1)}, bf16[2048,128]{1,0:T(8,128)(2,1)S(1)}, u32[]{:S(2)}, u32[]{:S(2)}) collective-permute-start(bf16[2048,128]{1,0:T(8,128)(2,1)S(1)} %copy-done.6), channel_id=1, source_target_pairs={{0,1},{1,0},{2,3},{3,2},{4,5},{5,4},{6,7},{7,6},{8,9},{9,8},{10,11... | collective-permute-start | bytes 1572872 | tf_op jit(solution)/shard_map/ppermute | solution.py:700
  83.1 8.8 %collective-permute-start.24 = (bf16[2048,128]{1,0:T(8,128)(2,1)}, bf16[2048,128]{1,0:T(8,128)(2,1)S(1)}, u32[]{:S(2)}, u32[]{:S(2)}) collective-permute-start(bf16[2048,128]{1,0:T(8,128)(2,1)} %collective-permute-done.23.refs_2_), channel_id=1, source_target_pairs={{0,1},{1,0},{2,3},{3,2},{4,5},{5,4},{6,7},{7,6},{8,9},{9,8},{10,11... | collective-permute-start | bytes 1572872 | tf_op jit(solution)/shard_map/ppermute | solution.py:700
  87.5 11.7 %collective-permute-start.26 = (bf16[128,128]{1,0:T(8,128)(2,1)S(1)}, bf16[128,128]{1,0:T(8,128)(2,1)S(1)}, u32[]{:S(2)}, u32[]{:S(2)}) collective-permute-start(bf16[128,128]{1,0:T(8,128)(2,1)S(1)} %get-tuple-element.65), channel_id=1, source_target_pairs={{0,8},{1,9},{2,10},{3,11},{4,12},{5,13},{6,14},{7,15},{8,0},{9,1},... | collective-permute-start | bytes 98312 | tf_op jit(solution)/shard_map/ppermute | solution.py:700
  89.0 10.2 %collective-permute-start.27 = (bf16[128,128]{1,0:T(8,128)(2,1)S(1)}, bf16[128,128]{1,0:T(8,128)(2,1)S(1)}, u32[]{:S(2)}, u32[]{:S(2)}) collective-permute-start(bf16[128,128]{1,0:T(8,128)(2,1)S(1)} %get-tuple-element.65), channel_id=1, source_target_pairs={{0,12},{1,13},{2,14},{3,15},{4,8},{5,9},{6,10},{7,11},{8,4},{9,5},... | collective-permute-start | bytes 98312 | tf_op jit(solution)/shard_map/ppermute | solution.py:700
  91.9 17.5 %collective-permute-start.7 = (bf16[2048,128]{1,0:T(8,128)(2,1)}, bf16[2048,128]{1,0:T(8,128)(2,1)S(1)}, u32[]{:S(2)}, u32[]{:S(2)}) collective-permute-start(bf16[2048,128]{1,0:T(8,128)(2,1)} %collective-permute-done.6.refs_0_), channel_id=1, source_target_pairs={{0,1},{1,0},{2,3},{3,2},{4,5},{5,4},{6,7},{7,6},{8,9},{9,8},{10,11... | collective-permute-start | bytes 1572872 | tf_op jit(solution)/shard_map/ppermute | solution.py:700
  91.9 15.0 %collective-permute-start.17 = (bf16[2048,128]{1,0:T(8,128)(2,1)}, bf16[2048,128]{1,0:T(8,128)(2,1)S(1)}, u32[]{:S(2)}, u32[]{:S(2)}) collective-permute-start(bf16[2048,128]{1,0:T(8,128)(2,1)} %collective-permute-done.6.refs_0_), channel_id=1, source_target_pairs={{0,2},{1,3},{2,0},{3,1},{4,6},{5,7},{6,4},{7,5},{8,10},{9,11},{10,... | collective-permute-start | bytes 1572872 | tf_op jit(solution)/shard_map/ppermute | solution.py:700
  99.2 10.0 %collective-permute-start.28 = (bf16[4,128,128]{2,1,0:T(8,128)(2,1)S(1)}, bf16[4,128,128]{2,1,0:T(8,128)(2,1)S(1)}, u32[]{:S(2)}, u32[]{:S(2)}) collective-permute-start(bf16[4,128,128]{2,1,0:T(8,128)(2,1)S(1)} %pad_maximum_fusion.2.near_ref), channel_id=1, source_target_pairs={{0,2},{1,3},{2,0},{3,1},{4,6},{5,7},{6,4},{7,5},{8,10},{9,11},{10,... | collective-permute-start | bytes 393224 | tf_op jit(solution)/shard_map/ppermute | solution.py:700
  109.3 6.8 %collective-permute-start.29 = (bf16[8,128,128]{2,1,0:T(8,128)(2,1)S(1)}, bf16[8,128,128]{2,1,0:T(8,128)(2,1)S(1)}, u32[]{:S(2)}, u32[]{:S(2)}) collective-permute-start(bf16[8,128,128]{2,1,0:T(8,128)(2,1)S(1)} %constant_dynamic-update-slice_fusion), channel_id=1, source_target_pairs={{0,1},{1,0},{2,3},{3,2},{4,5},{5,4},{6,7},{7,6},{8,9},{9,8},{10,11... | collective-permute-start | bytes 786440 | tf_op jit(solution)/shard_map/ppermute | solution.py:700
  115.2 8.9 %collective-permute-start.25 = (f32[520,128]{1,0:T(8,128)S(1)}, f32[520,128]{1,0:T(8,128)S(1)}, u32[]{:S(2)}, u32[]{:S(2)}) collective-permute-start(f32[520,128]{1,0:T(8,128)S(1)} %get-tuple-element.55), channel_id=1, source_target_pairs={{0,4},{1,5},{2,6},{3,7},{4,0},{5,1},{6,2},{7,3},{8,12},{9,13},{10,... | collective-permute-start | bytes 798728 | tf_op jit(solution)/shard_map/ppermute | solution.py:700
  (22 other events, 203.7 us)

commit v3 on v2

--- a/solution.py
+++ b/solution.py
@@ -290,40 +290,22 @@
     return [0, jnp.where(plane <= 2, 1, 3), 2, jnp.where(plane <= 2, 3, 1)]
 
 
-def pack_weights_kernel(place_ref, wq_ref, wk_ref, wv_ref, *refs):
-    own_ref, core_ref, side_ref, wk, wv, sems = refs
+def pack_weights_kernel(place_ref, wq_ref, wk_ref, wv_ref, own_ref, core_ref, side_ref):
     plane, lane = place_ref[2], place_ref[3]
-    feats = wk.shape[0]
+    feats = wk_ref.shape[0]
     block = wq_ref.shape[0] // 16
     half = own_ref.shape[0]
-    parts = []
     for r, out_ref in enumerate((own_ref, core_ref, side_ref, side_ref)):
+        base = half if r == 3 else 0
         for k, offset in enumerate(plane_order(plane)):
             start = (((plane + offset) & 3) * 4 + (lane ^ r)) * block
-            base = half if r == 3 else 0
-            parts.append((out_ref, base, k, pl.multiple_of(start, block)))
-    copies = [
-        pltpu.make_async_copy(
-            wq_ref.at[pl.ds(start, block)],
-            out_ref.at[pl.ds(base + k * block, block)],
-            sems.at[n],
-        )
-        for n, (out_ref, base, k, start) in enumerate(parts)
-    ]
-    copies.append(pltpu.make_async_copy(wk_ref, wk, sems.at[16]))
-    copies.append(pltpu.make_async_copy(wv_ref, wv, sems.at[17]))
-    for copy in copies[16:] + copies[:16]:
-        copy.start()
-    for copy in copies[16:]:
-        copy.wait()
-    for out_ref, base, k, start in parts:
-        for j in range(block // 128):
-            at = base + 4 * block + (k * (block // 128) + j) * 2 * feats
-            columns = pl.ds(pl.multiple_of(start + j * 128, 128), 128)
-            out_ref[at : at + feats, :] = wk[:, columns]
-            out_ref[at + feats : at + 2 * feats, :] = wv[:, columns]
-    for copy in copies[:16]:
-        copy.wait()
+            start = pl.multiple_of(start, block)
+            out_ref[base + k * block : base + (k + 1) * block, :] = wq_ref[pl.ds(start, block), :]
+            for j in range(block // 128):
+                at = base + 4 * block + (k * (block // 128) + j) * 2 * feats
+                columns = pl.ds(pl.multiple_of(start + j * 128, 128), 128)
+                out_ref[at : at + feats, :] = wk_ref[:, columns]
+                out_ref[at + feats : at + 2 * feats, :] = wv_ref[:, columns]
 
 
 def pack_weights(place, wq, wk_t, wv_t):
@@ -332,15 +314,10 @@
     return pl.pallas_call(
         pack_weights_kernel,
         out_shape=(block, block, jax.ShapeDtypeStruct((2 * rows, 128), jnp.bfloat16)),
-        in_specs=in_smem(1) + [pl.BlockSpec(memory_space=pl.ANY)] * 3,
+        in_specs=in_smem(1) + in_vmem(3),
         out_specs=tuple(in_vmem(3)),
-        scratch_shapes=[
-            pltpu.VMEM(wk_t.shape, jnp.bfloat16),
-            pltpu.VMEM(wv_t.shape, jnp.bfloat16),
-            pltpu.SemaphoreType.DMA((18,)),
-        ],
         compiler_params=params(),
-        cost_estimate=cost(0, 2 * wq.size),
+        cost_estimate=cost(1, 1),
         name="pack_weights",
     )(place, wq, wk_t, wv_t)
 
@@ -498,7 +475,8 @@
     before = refs[:2] if earlier else ()
     outs, (held, keys, values, scores_ref, acc, lanes, sems) = refs[-9:-7], refs[-7:]
     copies = [
-        pltpu.make_async_copy(block, held.at[n], sems.at[n]) for n, block in enumerate(blocks)
+        pltpu.make_async_copy(block, held.at[n, pl.ds(0, block.shape[0])], sems.at[n])
+        for n, block in enumerate(blocks)
     ]
     for copy in copies:
         copy.start()
@@ -519,24 +497,21 @@
             which = (holder ^ me) & 3
 
             def move(p, carry, which=which, first=first, pages=pages):
-                source = pl.multiple_of((first + p) * 2 * page_len, 2 * page_len)
-                target = pl.multiple_of((pages + p) * page_len, page_len)
-                keys[pl.ds(target, page_len), :] = held[which, pl.ds(source, page_len), :]
-                values[pl.ds(target, page_len), :] = held[
-                    which, pl.ds(source + page_len, page_len), :
-                ]
+                source = pl.multiple_of((first + 4 * p) * 2 * page_len, 2 * page_len)
+                target = pl.multiple_of((pages + 4 * p) * page_len, page_len)
+                slab = held[which, pl.ds(source, 8 * page_len), :]
+                slab = slab.reshape(4, 2 * page_len, 128)
+                four = pl.ds(target, 4 * page_len)
+                keys[four, :] = slab[:, :page_len].reshape(4 * page_len, 128)
+                values[four, :] = slab[:, page_len:].reshape(4 * page_len, 128)
                 return carry
 
-            lax.fori_loop(0, count, move, 0)
+            lax.fori_loop(0, (count + 3) // 4, move, 0)
             pages = pages + count
         trips = (pages + chunk_pages - 1) // chunk_pages
 
-        def clear(p, carry):
-            target = pl.multiple_of(p * page_len, page_len)
-            values[pl.ds(target, page_len), :] = jnp.zeros((page_len, 128), jnp.bfloat16)
-            return carry
-
-        lax.fori_loop(pages, trips * chunk_pages, clear, 0)
+        rest = pl.ds(pl.multiple_of(pages * page_len, page_len), CHUNK)
+        values[rest, :] = jnp.zeros((CHUNK, 128), jnp.bfloat16)
         keys_here = pages * page_len - jnp.where(has_last, table_ref[3 + request], 0)
         rows = slice(request * new_len, (request + 1) * new_len)
         query = jnp.concatenate([far_ref[rows, :], own_ref[rows, :]], axis=0)
@@ -587,9 +562,9 @@
         + in_vmem(2 + len(earlier)),
         out_specs=tuple(in_vmem(2)),
         scratch_shapes=[
-            pltpu.VMEM((4,) + blocks[0].shape, jnp.bfloat16),
-            pltpu.VMEM((span, 128), jnp.bfloat16),
-            pltpu.VMEM((span, 128), jnp.bfloat16),
+            pltpu.VMEM((4, blocks[0].shape[0] + 8 * page_len, 128), jnp.bfloat16),
+            pltpu.VMEM((span + CHUNK, 128), jnp.bfloat16),
+            pltpu.VMEM((span + CHUNK, 128), jnp.bfloat16),
             pltpu.VMEM((toks, span), jnp.float32),
             pltpu.VMEM((toks, 128), jnp.float32),
             pltpu.VMEM((toks, 128), jnp.float32),
@@ -788,19 +763,21 @@
     far_sum = after(far_sum, far_pages)
     query_kv = finish(sums[:2], got[:2], far_sum, cos_wide, sin_wide)
 
-    far_side = swap(after(far_pages, far_sum), 2)
+    far_pages = after(far_pages, far_sum)
+    far_side = swap(far_pages, 2)
     near_pages = [mine, swap(mine, 1), mine_side, swap(mine_side, 1)]
     away_pages = [far_pages, swap(far_pages, 1), far_side, swap(far_side, 1)]
 
     from_plane = swap(query_kv, 4)
     kv = query_kv[toks:]
-    far_kv = (swap(kv, 8), swap(kv, 12))
+    pair_kv = jnp.stack([kv, from_plane[toks:]])
+    far_kv = swap(pair_kv, 8)
 
     span = hit_page.shape[1] * page_len
     sizes = (toks, span, page_len)
     part = attend(0, table, near_pages, query_kv, from_plane, (), *sizes)
     far_kv = after(far_kv, part)
-    near_kv = jnp.stack([kv, from_plane[toks:], *far_kv])
+    near_kv = jnp.concatenate([pair_kv, far_kv], axis=0)
     side_kv = swap(near_kv, 2)
     core_kv = swap(jnp.concatenate([near_kv, side_kv], axis=0), 1)
     partner_part, own_part = attend(8, table, away_pages, query_kv, from_plane, part, *sizes)

time: 126 us -> 120 us (0.952)
  starting transfers between devices: 36 us -> 27.8 us
  waiting for transfers between devices: 45.6 us -> 49.8 us
  Pallas kernels: 29.9 us -> 27.4 us
    ppermute x24 -> x23, starting transfers between devices: 24.6 us -> 16.4 us  [swap(): return lax.ppermute(values, 'inst', [(i, i ^ bits) for i in range(16)])]
    ppermute x6, waiting for transfers between devices: 7.76 us -> 12.5 us  [hop(): return lax.ppermute(values, 'inst', pairs)]
    pallas_call x1, Pallas kernels: 4.94 us -> 2.14 us  [pack_weights(): pl.pallas_call(pack_weights_kernel, out_shape=(block, block, jax.ShapeDty...]
    unnamed x38 -> x30, local copies, waits for them, and re-layouts: 4.9 us -> 4.21 us
    ppermute x24 -> x23, waiting for transfers between devices: 37.8 us -> 37.4 us  [swap(): return lax.ppermute(values, 'inst', [(i, i ^ bits) for i in range(16)])]
  transfers between devices with their start and end apart: 30 -> 29, of which waited for: 13 -> 14; matrix products, arithmetic and copies ran while one was open for 5% -> 7% of each run, Pallas kernels for 23% -> 22%
where the time goes in v3:
time: 120 us; the launch traced here: 119 us
  waiting for transfers between devices  49.8 us (42%)
  starting transfers between devices  27.8 us (23%)
  Pallas kernels  27.4 us (23%)
  local copies, waits for them, and re-layouts  7.21 us (6%)
  other arithmetic  6.24 us (5%)
    ppermute x23, waiting for transfers between devices, swap(): return lax.ppermute(values, 'inst', [(i, i ^ bits) for i in range(16)])  37.4 us
    ppermute x23, starting transfers between devices, swap(): return lax.ppermute(values, 'inst', [(i, i ^ bits) for i in range(16)])  16.4 us
    ppermute x6, waiting for transfers between devices, hop(): return lax.ppermute(values, 'inst', pairs)  12.5 us
    pallas_call x2, Pallas kernels, attend(): pl.pallas_call(functools.partial(attend_kernel, offset, page_len, bool(ea...  12.3 us
    ppermute x6, starting transfers between devices, hop(): return lax.ppermute(values, 'inst', pairs)  11.4 us
    pallas_call x1, Pallas kernels, project(): pl.pallas_call(project_kernel, out_shape=(out,) * 8, in_specs=in_smem(1)...  4.9 us
    pallas_call x1, Pallas kernels, pick_pages(): pl.pallas_call(pick_pages_kernel, out_shape=(block, block), in_specs=in_s...  4.38 us
    unnamed x30, local copies, waits for them, and re-layouts  4.21 us
  transfers between devices with their start and end apart: 29, of which 14 were waited for; matrix products, arithmetic and copies ran while one was open for 7% of the time, Pallas kernels for 22%

profile of v3, /device:TPU:0, one launch (start us, length us, event | category | flops | bytes accessed | tf_op | source)
XLA Modules:
  0.0 119.5 jit_solution(16226564265373628031)
XLA Ops:
  3.3 2.9 %collective-permute-start.1 = (f32[512]{0:T(512)S(1)}, f32[512]{0:T(512)S(1)}, u32[]{:S(2)}, u32[]{:S(2)}) collective-permute-start(f32[512]{0:T(512)S(1)} %add.61), channel_id=1, source_target_pairs={{0,2},{1,3},{2,0},{3,1},{4,6},{5,7},{6,4},{7,5},{8,10},{9,11},{10,... | collective-permute-start | bytes 6152 | tf_op jit(solution)/shard_map/ppermute | solution.py:675
  6.2 1.6 %copy-done = bf16[8192,128]{1,0:T(8,128)(2,1)S(1)} copy-done((bf16[8192,128]{1,0:T(8,128)(2,1)S(1)}, bf16[8192,128]{1,0:T(8,128)(2,1)}, u32[]{:S(2)}) %copy-start) | copy-done | bytes 2097176
  9.7 2.1 %pack_weights.1 = (bf16[2560,128]{1,0:T(8,128)(2,1)S(1)}, bf16[2560,128]{1,0:T(8,128)(2,1)}, bf16[5120,128]{1,0:T(8,128)(2,1)}) custom-call(s32[4]{0:T(128)S(1)} %pad_add_fusion.2.place_ref, bf16[8192,128]{1,0:T(8,128)(2,1)S(1)} %copy-done, bf16[16,8192]{1,0:T(8,128)(2,1)S(1)} %bitcast.24, bf16[16,8192]{1,0:T(8,128)(2,1)S(1)} %bitcast.25), custom_call_target="tpu_custom_call" | custom-call | flops 1 | bytes 1 | tf_op jit(solution)/shard_map/pack_weights/pallas_call | solution.py:314
  14.0 5.4 %collective-permute-start.3 = (bf16[528,512]{1,0:T(8,128)(2,1)S(1)}, bf16[528,512]{1,0:T(8,128)(2,1)}, u32[]{:S(2)}, u32[]{:S(2)}) collective-permute-start(bf16[528,512]{1,0:T(8,128)(2,1)S(1)} %add_sums.1.own_ref), channel_id=1, source_target_pairs={{0,4},{1,5},{2,6},{3,7},{4,8},{5,9},{6,10},{7,11},{8,12},{9,13},{1... | collective-permute-start | bytes 1622024 | tf_op jit(solution)/shard_map/ppermute | solution.py:689
  19.5 4.4 %pick_pages.1 = (bf16[2048,128]{1,0:T(8,128)(2,1)S(1)}, bf16[2048,128]{1,0:T(8,128)(2,1)S(1)}) custom-call(s32[4]{0:T(128)S(1)} %pad_add_fusion.2.place_ref, s32[128]{0:T(128)S(1)} %reshape.118.hits_ref, bf16[32,64,2,256]{3,2,1,0:T(2,128)(2,1)S(1)} %copy-done.1), custom_call_target="tpu_custom_call" | custom-call | bytes 4194304 | tf_op jit(solution)/shard_map/pick_pages/pallas_call | solution.py:266
  23.9 4.8 %collective-permute-done.2.refs_0_ = bf16[528,512]{1,0:T(8,128)(2,1)} collective-permute-done((bf16[528,512]{1,0:T(8,128)(2,1)S(1)}, bf16[528,512]{1,0:T(8,128)(2,1)}, u32[]{:S(2)}, u32[]{:S(2)}) %collective-permute-start.2) | collective-permute-done | bytes 540704 | tf_op jit(solution)/shard_map/ppermute | solution.py:689
  31.8 1.9 %fusion = (f32[512,64]{1,0:T(8,128)}, f32[512,64]{1,0:T(8,128)}, f32[512,64]{1,0:T(8,128)}) fusion(f32[64]{0:T(128)S(1)} %negate_power_fusion, f32[512]{0:T(512)S(1)} %bitcast.28), kind=kLoop, calls=%fused_computation.10 | loop fusion | flops 65536 | bytes 395520 | tf_op jit(solution)/shard_map/neg | solution.py:756
  33.7 9.1 %collective-permute-done.10.refs_8_ = bf16[5120,128]{1,0:T(8,128)(2,1)} collective-permute-done((bf16[5120,128]{1,0:T(8,128)(2,1)}, bf16[5120,128]{1,0:T(8,128)(2,1)}, u32[]{:S(2)}, u32[]{:S(2)}) %collective-permute-start.10) | collective-permute-done | bytes 1310752 | tf_op jit(solution)/shard_map/ppermute | solution.py:675
  42.8 2.0 %slice.14 = bf16[2560,128]{1,0:T(8,128)(2,1)} slice(bf16[5120,128]{1,0:T(8,128)(2,1)} %collective-permute-done.10.refs_8_), slice={[2560:5120], [0:128]} | slice | bytes 1310720 | tf_op jit(solution)/shard_map/slice | solution.py:736
  46.9 1.5 %collective-permute-start.8 = (bf16[528,512]{1,0:T(8,128)(2,1)S(1)}, bf16[528,512]{1,0:T(8,128)(2,1)}, u32[]{:S(2)}, u32[]{:S(2)}) collective-permute-start(bf16[528,512]{1,0:T(8,128)(2,1)S(1)} %collective-permute-done.5.refs_4_), channel_id=1, source_target_pairs={{8,12},{9,13},{10,14},{11,15},{24,28},{25,29},{26,30},{27,31}} | collective-permute-start | bytes 1622024 | tf_op jit(solution)/shard_map/ppermute | solution.py:689
  48.4 5.8 %collective-permute-start.6 = (bf16[2048,128]{1,0:T(8,128)(2,1)}, bf16[2048,128]{1,0:T(8,128)(2,1)}, u32[]{:S(2)}, u32[]{:S(2)}) collective-permute-start(bf16[2048,128]{1,0:T(8,128)(2,1)} %copy-done.9), channel_id=1, source_target_pairs={{0,8},{1,9},{2,10},{3,11},{4,12},{5,13},{6,14},{7,15},{8,0},{9,1},... | collective-permute-start | bytes 1572872 | tf_op jit(solution)/shard_map/ppermute | solution.py:675
  55.8 5.9 %collective-permute-done.7.refs_2_ = bf16[528,512]{1,0:T(8,128)(2,1)S(1)} collective-permute-done((bf16[528,512]{1,0:T(8,128)(2,1)S(1)}, bf16[528,512]{1,0:T(8,128)(2,1)S(1)}, u32[]{:S(2)}, u32[]{:S(2)}) %collective-permute-start.7) | collective-permute-done | bytes 540704 | tf_op jit(solution)/shard_map/ppermute | solution.py:689
  61.7 4.9 %project.1 = (f32[320,128]{1,0:T(8,128)S(1)}, f32[320,128]{1,0:T(8,128)S(1)}, f32[320,128]{1,0:T(8,128)}, f32[320,128]{1,0:T(8,128)S(1)}, f32[320,128]{1,0:T(8,1...) custom-call(s32[4]{0:T(128)S(1)} %pad_add_fusion.2.place_ref, ...), custom_call_target="tpu_custom_call" | custom-call | flops 335544320 | bytes 6291456 | tf_op jit(solution)/shard_map/project/pallas_call | solution.py:403
  68.5 7.9 %collective-permute-done.6.refs_0_ = bf16[2048,128]{1,0:T(8,128)(2,1)} collective-permute-done((bf16[2048,128]{1,0:T(8,128)(2,1)}, bf16[2048,128]{1,0:T(8,128)(2,1)}, u32[]{:S(2)}, u32[]{:S(2)}) %collective-permute-start.6) | collective-permute-done | bytes 524320 | tf_op jit(solution)/shard_map/ppermute | solution.py:675
  78.9 3.6 %collective-permute-done.13.refs_4_ = f32[320,128]{1,0:T(8,128)S(1)} collective-permute-done((f32[320,128]{1,0:T(8,128)S(1)}, f32[320,128]{1,0:T(8,128)S(1)}, u32[]{:S(2)}, u32[]{:S(2)}) %collective-permute-start.13) | collective-permute-done | bytes 163872 | tf_op jit(solution)/shard_map/ppermute | solution.py:675
  83.1 4.9 %collective-permute-done.21.refs_5_ = bf16[640,128]{1,0:T(8,128)(2,1)S(1)} collective-permute-done((bf16[640,128]{1,0:T(8,128)(2,1)S(1)}, bf16[640,128]{1,0:T(8,128)(2,1)S(1)}, u32[]{:S(2)}, u32[]{:S(2)}) %collective-permute-start.21) | collective-permute-done | bytes 163872 | tf_op jit(solution)/shard_map/ppermute | solution.py:675
  88.1 1.8 %collective-permute-start.26 = (bf16[2,128,128]{2,1,0:T(8,128)(2,1)S(1)}, bf16[2,128,128]{2,1,0:T(8,128)(2,1)S(1)}, u32[]{:S(2)}, u32[]{:S(2)}) collective-permute-start(bf16[2,128,128]{2,1,0:T(8,128)(2,1)S(1)} %pad_maximum_fusion.4), channel_id=1, source_target_pairs={{0,8},{1,9},{2,10},{3,11},{4,12},{5,13},{6,14},{7,15},{8,0},{9,1},... | collective-permute-start | bytes 196616 | tf_op jit(solution)/shard_map/ppermute | solution.py:675
  90.0 5.3 %attend_own_plane.1 = (f32[520,128]{1,0:T(8,128)S(1)}, f32[520,128]{1,0:T(8,128)S(1)}) custom-call(s32[37]{0:T(128)S(1)} %pad_add_fusion.1.table_ref, bf16[2048,128]{1,0:T(8,128)(2,1)S(1)} %copy-done.6, bf16[2048,128]{1,0:T(8,128)(2,1)S(1)} %collective-permute-done.22.refs_1_, bf16[2048,128]{1,0:T(8,128)(2,1)} %collective-permute-done.23.refs_2_, ...), custom_call_target="tpu_custom_call" | custom-call | flops 1 | bytes 20971520 | tf_op jit(solution)/shard_map/attend_own_plane/pallas_call | solution.py:557
  96.5 5.5 %collective-permute-done.27.side_ref = bf16[4,128,128]{2,1,0:T(8,128)(2,1)S(1)} collective-permute-done((bf16[4,128,128]{2,1,0:T(8,128)(2,1)S(1)}, bf16[4,128,128]{2,1,0:T(8,128)(2,1)S(1)}, u32[]{:S(2)}, u32[]{:S(2)}) %collective-permute-start.27) | collective-permute-done | bytes 131104 | tf_op jit(solution)/shard_map/ppermute | solution.py:675
  102.1 7.1 %attend_far_plane.1 = (f32[520,128]{1,0:T(8,128)S(1)}, f32[520,128]{1,0:T(8,128)S(1)}) custom-call(s32[37]{0:T(128)S(1)} %pad_add_fusion.1.table_ref, bf16[2048,128]{1,0:T(8,128)(2,1)} %collective-permute-done.6.refs_0_, bf16[2048,128]{1,0:T(8,128)(2,1)S(1)} %collective-permute-done.16.refs_1_, bf16[2048,128]{1,0:T(8,128)(2,1)S(1)} %collective-permute-done.17.refs_2_, ...), custom_call_target="tpu_custom_call" | custom-call | flops 1 | bytes 20971520 | tf_op jit(solution)/shard_map/attend_far_plane/pallas_call | solution.py:557
  109.2 1.8 %collective-permute-start.25 = (f32[520,128]{1,0:T(8,128)S(1)}, f32[520,128]{1,0:T(8,128)S(1)}, u32[]{:S(2)}, u32[]{:S(2)}) collective-permute-start(f32[520,128]{1,0:T(8,128)S(1)} %get-tuple-element.54), channel_id=1, source_target_pairs={{0,4},{1,5},{2,6},{3,7},{4,0},{5,1},{6,2},{7,3},{8,12},{9,13},{10,... | collective-permute-start | bytes 798728 | tf_op jit(solution)/shard_map/ppermute | solution.py:675
  111.8 2.0 %new_tokens.1 = (f32[520,128]{1,0:T(8,128)S(1)}, bf16[2,64,2,128]{3,2,1,0:T(2,128)(2,1)}) custom-call(s32[8]{0:T(128)S(1)} %concatenate.31.place_ref, bf16[4,128,128]{2,1,0:T(8,128)(2,1)S(1)} %pad_maximum_fusion.3.near_ref, bf16[4,128,128]{2,1,0:T(8,128)(2,1)S(1)} %collective-permute-done.27.side_ref, ...), custom_call_target="tpu_custom_call" | custom-call | bytes 2097152 | tf_op jit(solution)/shard_map/new_tokens/pallas_call | solution.py:634
  113.9 4.2 %collective-permute-done.25.far_ref = f32[520,128]{1,0:T(8,128)S(1)} collective-permute-done((f32[520,128]{1,0:T(8,128)S(1)}, f32[520,128]{1,0:T(8,128)S(1)}, u32[]{:S(2)}, u32[]{:S(2)}) %collective-permute-start.25) | collective-permute-done | bytes 266272 | tf_op jit(solution)/shard_map/ppermute | solution.py:675
  118.1 1.4 %combine.1 = bf16[512,128]{1,0:T(8,128)(2,1)} custom-call(f32[520,128]{1,0:T(8,128)S(1)} %get-tuple-element.53.own_ref, f32[520,128]{1,0:T(8,128)S(1)} %collective-permute-done.25.far_ref, f32[520,128]{1,0:T(8,128)S(1)} %get-tuple-element.56.new_ref), custom_call_target="tpu_custom_call" | custom-call | bytes 1048576 | tf_op jit(solution)/shard_map/combine/pallas_call | solution.py:663
  (110 shorter events, 20.9 us)
Async XLA Ops:
  3.3 8.6 %collective-permute-start.1 = (f32[512]{0:T(512)S(1)}, f32[512]{0:T(512)S(1)}, u32[]{:S(2)}, u32[]{:S(2)}) collective-permute-start(f32[512]{0:T(512)S(1)} %add.61), channel_id=1, source_target_pairs={{0,2},{1,3},{2,0},{3,1},{4,6},{5,7},{6,4},{7,5},{8,10},{9,11},{10,... | collective-permute-start | bytes 6152 | tf_op jit(solution)/shard_map/ppermute | solution.py:675
  11.8 31.0 %collective-permute-start.10 = (bf16[5120,128]{1,0:T(8,128)(2,1)}, bf16[5120,128]{1,0:T(8,128)(2,1)}, u32[]{:S(2)}, u32[]{:S(2)}) collective-permute-start(bf16[5120,128]{1,0:T(8,128)(2,1)} %get-tuple-element.38), channel_id=1, source_target_pairs={{0,2},{1,3},{2,0},{3,1},{4,6},{5,7},{6,4},{7,5},{8,10},{9,11},{10,... | collective-permute-start | bytes 3932168 | tf_op jit(solution)/shard_map/ppermute | solution.py:675
  12.7 16.1 %collective-permute-start.2 = (bf16[528,512]{1,0:T(8,128)(2,1)S(1)}, bf16[528,512]{1,0:T(8,128)(2,1)}, u32[]{:S(2)}, u32[]{:S(2)}) collective-permute-start(bf16[528,512]{1,0:T(8,128)(2,1)S(1)} %add_sums.1.own_ref), channel_id=1, source_target_pairs={{4,0},{5,1},{6,2},{7,3},{8,4},{9,5},{10,6},{11,7},{12,8},{13,9},{1... | collective-permute-start | bytes 1622024 | tf_op jit(solution)/shard_map/ppermute | solution.py:689
  14.0 15.8 %collective-permute-start.3 = (bf16[528,512]{1,0:T(8,128)(2,1)S(1)}, bf16[528,512]{1,0:T(8,128)(2,1)}, u32[]{:S(2)}, u32[]{:S(2)}) collective-permute-start(bf16[528,512]{1,0:T(8,128)(2,1)S(1)} %add_sums.1.own_ref), channel_id=1, source_target_pairs={{0,4},{1,5},{2,6},{3,7},{4,8},{5,9},{6,10},{7,11},{8,12},{9,13},{1... | collective-permute-start | bytes 1622024 | tf_op jit(solution)/shard_map/ppermute | solution.py:689
  19.3 35.0 %collective-permute-start.9 = (bf16[2560,128]{1,0:T(8,128)(2,1)}, bf16[2560,128]{1,0:T(8,128)(2,1)}, u32[]{:S(2)}, u32[]{:S(2)}) collective-permute-start(bf16[2560,128]{1,0:T(8,128)(2,1)} %get-tuple-element.36), channel_id=1, source_target_pairs={{0,1},{1,0},{2,3},{3,2},{4,5},{5,4},{6,7},{7,6},{8,9},{9,8},{10,11... | collective-permute-start | bytes 1966088 | tf_op jit(solution)/shard_map/ppermute | solution.py:675
  29.8 15.8 %collective-permute-start.4 = (bf16[528,512]{1,0:T(8,128)(2,1)}, bf16[528,512]{1,0:T(8,128)(2,1)S(1)}, u32[]{:S(2)}, u32[]{:S(2)}) collective-permute-start(bf16[528,512]{1,0:T(8,128)(2,1)} %collective-permute-done.2.refs_0_), channel_id=1, source_target_pairs={{4,0},{5,1},{6,2},{7,3},{8,4},{9,5},{10,6},{11,7},{20,16},{21,17},... | collective-permute-start | bytes 1622024 | tf_op jit(solution)/shard_map/ppermute | solution.py:689
  31.1 15.8 %collective-permute-start.5 = (bf16[528,512]{1,0:T(8,128)(2,1)}, bf16[528,512]{1,0:T(8,128)(2,1)S(1)}, u32[]{:S(2)}, u32[]{:S(2)}) collective-permute-start(bf16[528,512]{1,0:T(8,128)(2,1)} %collective-permute-done.3.refs_3_), channel_id=1, source_target_pairs={{4,8},{5,9},{6,10},{7,11},{8,12},{9,13},{10,14},{11,15},{20,24},{2... | collective-permute-start | bytes 1622024 | tf_op jit(solution)/shard_map/ppermute | solution.py:689
  44.8 16.9 %collective-permute-start.11 = (bf16[2560,128]{1,0:T(8,128)(2,1)}, bf16[2560,128]{1,0:T(8,128)(2,1)}, u32[]{:S(2)}, u32[]{:S(2)}) collective-permute-start(bf16[2560,128]{1,0:T(8,128)(2,1)} %slice.14), channel_id=1, source_target_pairs={{0,1},{1,0},{2,3},{3,2},{4,5},{5,4},{6,7},{7,6},{8,9},{9,8},{10,11... | collective-permute-start | bytes 1966088 | tf_op jit(solution)/shard_map/ppermute | solution.py:675
  45.6 16.0 %collective-permute-start.7 = (bf16[528,512]{1,0:T(8,128)(2,1)S(1)}, bf16[528,512]{1,0:T(8,128)(2,1)S(1)}, u32[]{:S(2)}, u32[]{:S(2)}) collective-permute-start(bf16[528,512]{1,0:T(8,128)(2,1)S(1)} %collective-permute-done.4.refs_1_), channel_id=1, source_target_pairs={{4,0},{5,1},{6,2},{7,3},{20,16},{21,17},{22,18},{23,19}} | collective-permute-start | bytes 1622024 | tf_op jit(solution)/shard_map/ppermute | solution.py:689
  46.9 14.7 %collective-permute-start.8 = (bf16[528,512]{1,0:T(8,128)(2,1)S(1)}, bf16[528,512]{1,0:T(8,128)(2,1)}, u32[]{:S(2)}, u32[]{:S(2)}) collective-permute-start(bf16[528,512]{1,0:T(8,128)(2,1)S(1)} %collective-permute-done.5.refs_4_), channel_id=1, source_target_pairs={{8,12},{9,13},{10,14},{11,15},{24,28},{25,29},{26,30},{27,31}} | collective-permute-start | bytes 1622024 | tf_op jit(solution)/shard_map/ppermute | solution.py:689
  48.4 28.0 %collective-permute-start.6 = (bf16[2048,128]{1,0:T(8,128)(2,1)}, bf16[2048,128]{1,0:T(8,128)(2,1)}, u32[]{:S(2)}, u32[]{:S(2)}) collective-permute-start(bf16[2048,128]{1,0:T(8,128)(2,1)} %copy-done.9), channel_id=1, source_target_pairs={{0,8},{1,9},{2,10},{3,11},{4,12},{5,13},{6,14},{7,15},{8,0},{9,1},... | collective-permute-start | bytes 1572872 | tf_op jit(solution)/shard_map/ppermute | solution.py:675
  54.3 23.9 %collective-permute-start.23 = (bf16[2048,128]{1,0:T(8,128)(2,1)}, bf16[2048,128]{1,0:T(8,128)(2,1)}, u32[]{:S(2)}, u32[]{:S(2)}) collective-permute-start(bf16[2048,128]{1,0:T(8,128)(2,1)} %copy-done.5), channel_id=1, source_target_pairs={{0,2},{1,3},{2,0},{3,1},{4,6},{5,7},{6,4},{7,5},{8,10},{9,11},{10,... | collective-permute-start | bytes 1572872 | tf_op jit(solution)/shard_map/ppermute | solution.py:675
  67.4 15.1 %collective-permute-start.19 = (f32[320,128]{1,0:T(8,128)}, f32[320,128]{1,0:T(8,128)S(1)}, u32[]{:S(2)}, u32[]{:S(2)}) collective-permute-start(f32[320,128]{1,0:T(8,128)} %get-tuple-element.48), channel_id=1, source_target_pairs={{0,1},{1,0},{2,3},{3,2},{4,5},{5,4},{6,7},{7,6},{8,9},{9,8},{10,11... | collective-permute-start | bytes 491528 | tf_op jit(solution)/shard_map/ppermute | solution.py:675
  68.0 14.6 %collective-permute-start.20 = (f32[320,128]{1,0:T(8,128)S(1)}, f32[320,128]{1,0:T(8,128)S(1)}, u32[]{:S(2)}, u32[]{:S(2)}) collective-permute-start(f32[320,128]{1,0:T(8,128)S(1)} %get-tuple-element.49), channel_id=1, source_target_pairs={{0,1},{1,0},{2,3},{3,2},{4,5},{5,4},{6,7},{7,6},{8,9},{9,8},{10,11... | collective-permute-start | bytes 491528 | tf_op jit(solution)/shard_map/ppermute | solution.py:675
  68.2 10.2 %collective-permute-start.15 = (f32[320,128]{1,0:T(8,128)S(1)}, f32[320,128]{1,0:T(8,128)S(1)}, u32[]{:S(2)}, u32[]{:S(2)}) collective-permute-start(f32[320,128]{1,0:T(8,128)S(1)} %add.68), channel_id=1, source_target_pairs={{0,2},{1,3},{2,0},{3,1},{4,6},{5,7},{6,4},{7,5},{8,10},{9,11},{10,... | collective-permute-start | bytes 491528 | tf_op jit(solution)/shard_map/ppermute | solution.py:675
  76.4 6.1 %collective-permute-start.13 = (f32[320,128]{1,0:T(8,128)S(1)}, f32[320,128]{1,0:T(8,128)S(1)}, u32[]{:S(2)}, u32[]{:S(2)}) collective-permute-start(f32[320,128]{1,0:T(8,128)S(1)} %add.67), channel_id=1, source_target_pairs={{0,2},{1,3},{2,0},{3,1},{4,6},{5,7},{6,4},{7,5},{8,10},{9,11},{10,... | collective-permute-start | bytes 491528 | tf_op jit(solution)/shard_map/ppermute | solution.py:675
  78.3 11.6 %collective-permute-start.22 = (bf16[2048,128]{1,0:T(8,128)(2,1)S(1)}, bf16[2048,128]{1,0:T(8,128)(2,1)S(1)}, u32[]{:S(2)}, u32[]{:S(2)}) collective-permute-start(bf16[2048,128]{1,0:T(8,128)(2,1)S(1)} %copy-done.6), channel_id=1, source_target_pairs={{0,1},{1,0},{2,3},{3,2},{4,5},{5,4},{6,7},{7,6},{8,9},{9,8},{10,11... | collective-permute-start | bytes 1572872 | tf_op jit(solution)/shard_map/ppermute | solution.py:675
  78.4 11.6 %collective-permute-start.24 = (bf16[2048,128]{1,0:T(8,128)(2,1)}, bf16[2048,128]{1,0:T(8,128)(2,1)S(1)}, u32[]{:S(2)}, u32[]{:S(2)}) collective-permute-start(bf16[2048,128]{1,0:T(8,128)(2,1)} %collective-permute-done.23.refs_2_), channel_id=1, source_target_pairs={{0,1},{1,0},{2,3},{3,2},{4,5},{5,4},{6,7},{7,6},{8,9},{9,8},{10,11... | collective-permute-start | bytes 1572872 | tf_op jit(solution)/shard_map/ppermute | solution.py:675
  82.7 13.3 %collective-permute-start.17 = (bf16[2048,128]{1,0:T(8,128)(2,1)}, bf16[2048,128]{1,0:T(8,128)(2,1)S(1)}, u32[]{:S(2)}, u32[]{:S(2)}) collective-permute-start(bf16[2048,128]{1,0:T(8,128)(2,1)} %collective-permute-done.6.refs_0_), channel_id=1, source_target_pairs={{0,2},{1,3},{2,0},{3,1},{4,6},{5,7},{6,4},{7,5},{8,10},{9,11},{10,... | collective-permute-start | bytes 1572872 | tf_op jit(solution)/shard_map/ppermute | solution.py:675
  88.1 7.2 %collective-permute-start.26 = (bf16[2,128,128]{2,1,0:T(8,128)(2,1)S(1)}, bf16[2,128,128]{2,1,0:T(8,128)(2,1)S(1)}, u32[]{:S(2)}, u32[]{:S(2)}) collective-permute-start(bf16[2,128,128]{2,1,0:T(8,128)(2,1)S(1)} %pad_maximum_fusion.4), channel_id=1, source_target_pairs={{0,8},{1,9},{2,10},{3,11},{4,12},{5,13},{6,14},{7,15},{8,0},{9,1},... | collective-permute-start | bytes 196616 | tf_op jit(solution)/shard_map/ppermute | solution.py:675
  89.9 12.2 %collective-permute-start.16 = (bf16[2048,128]{1,0:T(8,128)(2,1)}, bf16[2048,128]{1,0:T(8,128)(2,1)S(1)}, u32[]{:S(2)}, u32[]{:S(2)}) collective-permute-start(bf16[2048,128]{1,0:T(8,128)(2,1)} %collective-permute-done.6.refs_0_), channel_id=1, source_target_pairs={{0,1},{1,0},{2,3},{3,2},{4,5},{5,4},{6,7},{7,6},{8,9},{9,8},{10,11... | collective-permute-start | bytes 1572872 | tf_op jit(solution)/shard_map/ppermute | solution.py:675
  96.0 6.1 %collective-permute-start.18 = (bf16[2048,128]{1,0:T(8,128)(2,1)S(1)}, bf16[2048,128]{1,0:T(8,128)(2,1)S(1)}, u32[]{:S(2)}, u32[]{:S(2)}) collective-permute-start(bf16[2048,128]{1,0:T(8,128)(2,1)S(1)} %collective-permute-done.17.refs_2_), channel_id=1, source_target_pairs={{0,1},{1,0},{2,3},{3,2},{4,5},{5,4},{6,7},{7,6},{8,9},{9,8},{10,11... | collective-permute-start | bytes 1572872 | tf_op jit(solution)/shard_map/ppermute | solution.py:675
  102.0 9.8 %collective-permute-start.28 = (bf16[8,128,128]{2,1,0:T(8,128)(2,1)S(1)}, bf16[8,128,128]{2,1,0:T(8,128)(2,1)S(1)}, u32[]{:S(2)}, u32[]{:S(2)}) collective-permute-start(bf16[8,128,128]{2,1,0:T(8,128)(2,1)S(1)} %pad_maximum_fusion.2), channel_id=1, source_target_pairs={{0,1},{1,0},{2,3},{3,2},{4,5},{5,4},{6,7},{7,6},{8,9},{9,8},{10,11... | collective-permute-start | bytes 786440 | tf_op jit(solution)/shard_map/ppermute | solution.py:675
  109.2 8.8 %collective-permute-start.25 = (f32[520,128]{1,0:T(8,128)S(1)}, f32[520,128]{1,0:T(8,128)S(1)}, u32[]{:S(2)}, u32[]{:S(2)}) collective-permute-start(f32[520,128]{1,0:T(8,128)S(1)} %get-tuple-element.54), channel_id=1, source_target_pairs={{0,4},{1,5},{2,6},{3,7},{4,0},{5,1},{6,2},{7,3},{8,12},{9,13},{10,... | collective-permute-start | bytes 798728 | tf_op jit(solution)/shard_map/ppermute | solution.py:675
  (19 other events, 209.3 us)

commit v4 on v3

--- a/solution.py
+++ b/solution.py
@@ -186,7 +186,7 @@
 
 
 VMEM_LIMIT = 48 * 1024 * 1024
-CHUNK = 512
+CHUNK = 1024
 SUM_ROWS = 16
 
 
@@ -577,15 +577,15 @@
 
 
 def new_tokens_kernel(
-    place_ref, near_ref, side_ref, core_ref, cos_ref, sin_ref, query_ref, state_ref, page_ref, held, kt, vt
+    place_ref, near_ref, side_ref, core_ref, across_ref, cos_ref, sin_ref, query_ref, state_ref, page_ref, held, kt, vt
 ):
     me, head = place_ref[0], place_ref[1]
     toks = cos_ref.shape[1]
     for n in range(4):
         held[n] = near_ref[n]
         held[4 + n] = side_ref[n]
-    for n in range(8):
         held[8 + n] = core_ref[n]
+        held[12 + n] = across_ref[n]
     for device in range(16):
         rel = device ^ me
         block = held[(rel & 1) * 8 + ((rel >> 1) & 1) * 4 + (rel >> 2)]
@@ -629,7 +629,7 @@
         page_ref[slot] = woven.astype(jnp.bfloat16).reshape(page_len, 2, 128)
 
 
-def new_tokens(place, near, side, core, cos_t, sin_t, query_kv, page_len):
+def new_tokens(place, near, side, core, across, cos_t, sin_t, query_kv, page_len):
     toks = cos_t.shape[1]
     return pl.pallas_call(
         new_tokens_kernel,
@@ -637,7 +637,7 @@
             jax.ShapeDtypeStruct((toks + 8, 128), jnp.float32),
             jax.ShapeDtypeStruct((OWN, page_len, 2, 128), jnp.bfloat16),
         ),
-        in_specs=in_smem(1) + in_vmem(6),
+        in_specs=in_smem(1) + in_vmem(7),
         out_specs=tuple(in_vmem(2)),
         scratch_shapes=[
             pltpu.VMEM((16, 128, 128), jnp.bfloat16),
@@ -647,7 +647,7 @@
         compiler_params=params(),
         cost_estimate=cost(0, 2 << 20),
         name="new_tokens",
-    )(place, near, side, core, cos_t, sin_t, query_kv)
+    )(place, near, side, core, across, cos_t, sin_t, query_kv)
 
 
 def combine_kernel(own_ref, far_ref, new_ref, out_ref):
@@ -759,6 +759,7 @@
     gain_blocks = gain_blocks[(plane + jnp.stack(plane_order(plane))) & 3]
     sums = project(place, gain_blocks, downs, ups, weights)
     got = [swap(part, 1) for part in sums[2:4] + sums[6:8]]
+    got = after(got, mine_side)
     far_sum = [swap(sums[4 + n] + got[2 + n], 2) for n in range(2)]
     far_sum = after(far_sum, far_pages)
     query_kv = finish(sums[:2], got[:2], far_sum, cos_wide, sin_wide)
@@ -766,7 +767,6 @@
     far_pages = after(far_pages, far_sum)
     far_side = swap(far_pages, 2)
     near_pages = [mine, swap(mine, 1), mine_side, swap(mine_side, 1)]
-    away_pages = [far_pages, swap(far_pages, 1), far_side, swap(far_side, 1)]
 
     from_plane = swap(query_kv, 4)
     kv = query_kv[toks:]
@@ -776,14 +776,14 @@
     span = hit_page.shape[1] * page_len
     sizes = (toks, span, page_len)
     part = attend(0, table, near_pages, query_kv, from_plane, (), *sizes)
-    far_kv = after(far_kv, part)
     near_kv = jnp.concatenate([pair_kv, far_kv], axis=0)
     side_kv = swap(near_kv, 2)
-    core_kv = swap(jnp.concatenate([near_kv, side_kv], axis=0), 1)
+    core_kv, across_kv = swap(near_kv, 1), swap(near_kv, 3)
+    away_pages = [far_pages, swap(far_pages, 1), far_side, swap(after(far_side, part), 1)]
     partner_part, own_part = attend(8, table, away_pages, query_kv, from_plane, part, *sizes)
     partner_part = swap(partner_part, 4)
     new_part, decode_pages = new_tokens(
-        page_place, near_kv, side_kv, core_kv, cos_table.T, sin_table.T, query_kv, page_len
+        page_place, near_kv, side_kv, core_kv, across_kv, cos_table.T, sin_table.T, query_kv, page_len
     )
     attn_out = combine(own_part, partner_part, new_part)
     return (attn_out, decode_pages)

time: 120 us -> 117 us (0.975)
  waiting for transfers between devices: 49.8 us -> 38.2 us
  starting transfers between devices: 27.8 us -> 36 us
    ppermute x23 -> x24, starting transfers between devices: 16.4 us -> 24.6 us  [swap(): return lax.ppermute(values, 'inst', [(i, i ^ bits) for i in range(16)])]
    ppermute x23 -> x24, waiting for transfers between devices: 37.4 us -> 29.9 us  [swap(): return lax.ppermute(values, 'inst', [(i, i ^ bits) for i in range(16)])]
    ppermute x6, waiting for transfers between devices: 12.5 us -> 8.26 us  [hop(): return lax.ppermute(values, 'inst', pairs)]
    pallas_call x1, Pallas kernels: 4.38 us -> 5.9 us  [pick_pages(): pl.pallas_call(pick_pages_kernel, out_shape=(block, block), in_specs=in_s...]
    unnamed x30 -> x26, local copies, waits for them, and re-layouts: 4.21 us -> 5 us
  transfers between devices with their start and end apart: 29 -> 30, of which waited for: 14 -> 15; matrix products, arithmetic and copies ran while one was open for 7% -> 7% of each run, Pallas kernels for 22% -> 22%
where the time goes in v4:
time: 117 us
  waiting for transfers between devices  38.2 us (33%)
  starting transfers between devices  36 us (31%)
  Pallas kernels  27.5 us (24%)
  local copies, waits for them, and re-layouts  8 us (7%)
  other arithmetic  6.26 us (5%)
    ppermute x24, waiting for transfers between devices, swap(): return lax.ppermute(values, 'inst', [(i, i ^ bits) for i in range(16)])  29.9 us
    ppermute x24, starting transfers between devices, swap(): return lax.ppermute(values, 'inst', [(i, i ^ bits) for i in range(16)])  24.6 us
    pallas_call x2, Pallas kernels, attend(): pl.pallas_call(functools.partial(attend_kernel, offset, page_len, bool(ea...  11.6 us
    ppermute x6, starting transfers between devices, hop(): return lax.ppermute(values, 'inst', pairs)  11.4 us
    ppermute x6, waiting for transfers between devices, hop(): return lax.ppermute(values, 'inst', pairs)  8.26 us
    pallas_call x1, Pallas kernels, pick_pages(): pl.pallas_call(pick_pages_kernel, out_shape=(block, block), in_specs=in_s...  5.9 us
    unnamed x26, local copies, waits for them, and re-layouts  5 us
    pallas_call x1, Pallas kernels, project(): pl.pallas_call(project_kernel, out_shape=(out,) * 8, in_specs=in_smem(1)...  4.25 us
  transfers between devices with their start and end apart: 30, of which 15 were waited for; matrix products, arithmetic and copies ran while one was open for 7% of the time, Pallas kernels for 22%

profile of v4, /device:TPU:0, one launch (start us, length us, event | category | flops | bytes accessed | tf_op | source)
XLA Modules:
  0.0 116.9 jit_solution(12654044046270056783)
XLA Ops:
  3.3 2.9 %collective-permute-start.1 = (f32[512]{0:T(512)S(1)}, f32[512]{0:T(512)S(1)}, u32[]{:S(2)}, u32[]{:S(2)}) collective-permute-start(f32[512]{0:T(512)S(1)} %add.61), channel_id=1, source_target_pairs={{0,2},{1,3},{2,0},{3,1},{4,6},{5,7},{6,4},{7,5},{8,10},{9,11},{10,... | collective-permute-start | bytes 6152 | tf_op jit(solution)/shard_map/ppermute | solution.py:675
  6.2 1.6 %copy-done = bf16[8192,128]{1,0:T(8,128)(2,1)S(1)} copy-done((bf16[8192,128]{1,0:T(8,128)(2,1)S(1)}, bf16[8192,128]{1,0:T(8,128)(2,1)}, u32[]{:S(2)}) %copy-start) | copy-done | bytes 2097176
  9.7 2.1 %pack_weights.1 = (bf16[2560,128]{1,0:T(8,128)(2,1)S(1)}, bf16[2560,128]{1,0:T(8,128)(2,1)}, bf16[5120,128]{1,0:T(8,128)(2,1)}) custom-call(s32[4]{0:T(128)S(1)} %pad_add_fusion.2.place_ref, bf16[8192,128]{1,0:T(8,128)(2,1)S(1)} %copy-done, bf16[16,8192]{1,0:T(8,128)(2,1)S(1)} %bitcast.24, bf16[16,8192]{1,0:T(8,128)(2,1)S(1)} %bitcast.25), custom_call_target="tpu_custom_call" | custom-call | flops 1 | bytes 1 | tf_op jit(solution)/shard_map/pack_weights/pallas_call | solution.py:314
  14.0 5.4 %collective-permute-start.3 = (bf16[528,512]{1,0:T(8,128)(2,1)S(1)}, bf16[528,512]{1,0:T(8,128)(2,1)}, u32[]{:S(2)}, u32[]{:S(2)}) collective-permute-start(bf16[528,512]{1,0:T(8,128)(2,1)S(1)} %add_sums.1.own_ref), channel_id=1, source_target_pairs={{0,4},{1,5},{2,6},{3,7},{4,8},{5,9},{6,10},{7,11},{8,12},{9,13},{1... | collective-permute-start | bytes 1622024 | tf_op jit(solution)/shard_map/ppermute | solution.py:689
  19.5 5.9 %pick_pages.1 = (bf16[2048,128]{1,0:T(8,128)(2,1)}, bf16[2048,128]{1,0:T(8,128)(2,1)S(1)}) custom-call(s32[4]{0:T(128)S(1)} %pad_add_fusion.2.place_ref, s32[128]{0:T(128)S(1)} %reshape.118.hits_ref, bf16[32,64,2,256]{3,2,1,0:T(2,128)(2,1)S(1)} %copy-done.1), custom_call_target="tpu_custom_call" | custom-call | bytes 4194304 | tf_op jit(solution)/shard_map/pick_pages/pallas_call | solution.py:266
  26.3 2.5 %collective-permute-done.2.refs_0_ = bf16[528,512]{1,0:T(8,128)(2,1)} collective-permute-done((bf16[528,512]{1,0:T(8,128)(2,1)S(1)}, bf16[528,512]{1,0:T(8,128)(2,1)}, u32[]{:S(2)}, u32[]{:S(2)}) %collective-permute-start.2) | collective-permute-done | bytes 540704 | tf_op jit(solution)/shard_map/ppermute | solution.py:689
  31.9 10.9 %collective-permute-done.10.refs_8_ = bf16[5120,128]{1,0:T(8,128)(2,1)} collective-permute-done((bf16[5120,128]{1,0:T(8,128)(2,1)}, bf16[5120,128]{1,0:T(8,128)(2,1)}, u32[]{:S(2)}, u32[]{:S(2)}) %collective-permute-start.10) | collective-permute-done | bytes 1310752 | tf_op jit(solution)/shard_map/ppermute | solution.py:675
  42.8 2.0 %slice.14 = bf16[2560,128]{1,0:T(8,128)(2,1)} slice(bf16[5120,128]{1,0:T(8,128)(2,1)} %collective-permute-done.10.refs_8_), slice={[2560:5120], [0:128]} | slice | bytes 1310720 | tf_op jit(solution)/shard_map/slice | solution.py:736
  47.0 1.5 %collective-permute-start.8 = (bf16[528,512]{1,0:T(8,128)(2,1)S(1)}, bf16[528,512]{1,0:T(8,128)(2,1)}, u32[]{:S(2)}, u32[]{:S(2)}) collective-permute-start(bf16[528,512]{1,0:T(8,128)(2,1)S(1)} %collective-permute-done.5.refs_4_), channel_id=1, source_target_pairs={{8,12},{9,13},{10,14},{11,15},{24,28},{25,29},{26,30},{27,31}} | collective-permute-start | bytes 1622024 | tf_op jit(solution)/shard_map/ppermute | solution.py:689
  50.0 1.9 %fusion = (f32[512,64]{1,0:T(8,128)}, f32[512,64]{1,0:T(8,128)}, f32[512,64]{1,0:T(8,128)}) fusion(f32[64]{0:T(128)S(1)} %negate_power_fusion, f32[512]{0:T(512)S(1)} %bitcast.28), kind=kLoop, calls=%fused_computation.9 | loop fusion | flops 65536 | bytes 395520 | tf_op jit(solution)/shard_map/neg | solution.py:756
  51.9 5.7 %collective-permute-start.6 = (bf16[2048,128]{1,0:T(8,128)(2,1)}, bf16[2048,128]{1,0:T(8,128)(2,1)}, u32[]{:S(2)}, u32[]{:S(2)}) collective-permute-start(bf16[2048,128]{1,0:T(8,128)(2,1)} %copy-done.7), channel_id=1, source_target_pairs={{0,8},{1,9},{2,10},{3,11},{4,12},{5,13},{6,14},{7,15},{8,0},{9,1},... | collective-permute-start | bytes 1572872 | tf_op jit(solution)/shard_map/ppermute | solution.py:675
  57.6 3.9 %collective-permute-done.7.refs_2_ = bf16[528,512]{1,0:T(8,128)(2,1)S(1)} collective-permute-done((bf16[528,512]{1,0:T(8,128)(2,1)S(1)}, bf16[528,512]{1,0:T(8,128)(2,1)S(1)}, u32[]{:S(2)}, u32[]{:S(2)}) %collective-permute-start.7) | collective-permute-done | bytes 540704 | tf_op jit(solution)/shard_map/ppermute | solution.py:689
  61.5 4.3 %project.1 = (f32[320,128]{1,0:T(8,128)S(1)}, f32[320,128]{1,0:T(8,128)S(1)}, f32[320,128]{1,0:T(8,128)S(1)}, f32[320,128]{1,0:T(8,128)S(1)}, f32[320,128]{1,0:T...) custom-call(s32[4]{0:T(128)S(1)} %pad_add_fusion.2.place_ref, ...), custom_call_target="tpu_custom_call" | custom-call | flops 335544320 | bytes 6291456 | tf_op jit(solution)/shard_map/project/pallas_call | solution.py:403
  68.4 1.8 %collective-permute-start.17 = (f32[320,128]{1,0:T(8,128)S(1)}, f32[320,128]{1,0:T(8,128)S(1)}, u32[]{:S(2)}, u32[]{:S(2)}) collective-permute-start(f32[320,128]{1,0:T(8,128)S(1)} %add.67), channel_id=1, source_target_pairs={{0,2},{1,3},{2,0},{3,1},{4,6},{5,7},{6,4},{7,5},{8,10},{9,11},{10,... | collective-permute-start | bytes 491528 | tf_op jit(solution)/shard_map/ppermute | solution.py:675
  71.9 7.0 %collective-permute-done.6.refs_0_ = bf16[2048,128]{1,0:T(8,128)(2,1)} collective-permute-done((bf16[2048,128]{1,0:T(8,128)(2,1)}, bf16[2048,128]{1,0:T(8,128)(2,1)}, u32[]{:S(2)}, u32[]{:S(2)}) %collective-permute-start.6) | collective-permute-done | bytes 524320 | tf_op jit(solution)/shard_map/ppermute | solution.py:675
  78.9 1.7 %collective-permute-start.20 = (bf16[2048,128]{1,0:T(8,128)(2,1)}, bf16[2048,128]{1,0:T(8,128)(2,1)S(1)}, u32[]{:S(2)}, u32[]{:S(2)}) collective-permute-start(bf16[2048,128]{1,0:T(8,128)(2,1)} %collective-permute-done.6.refs_0_), channel_id=1, source_target_pairs={{0,2},{1,3},{2,0},{3,1},{4,6},{5,7},{6,4},{7,5},{8,10},{9,11},{10,... | collective-permute-start | bytes 1572872 | tf_op jit(solution)/shard_map/ppermute | solution.py:675
  81.3 5.5 %collective-permute-done.23.refs_5_ = bf16[640,128]{1,0:T(8,128)(2,1)S(1)} collective-permute-done((bf16[640,128]{1,0:T(8,128)(2,1)S(1)}, bf16[640,128]{1,0:T(8,128)(2,1)S(1)}, u32[]{:S(2)}, u32[]{:S(2)}) %collective-permute-start.23) | collective-permute-done | bytes 163872 | tf_op jit(solution)/shard_map/ppermute | solution.py:675
  86.8 5.7 %attend_own_plane.1 = (f32[520,128]{1,0:T(8,128)S(1)}, f32[520,128]{1,0:T(8,128)S(1)}) custom-call(s32[37]{0:T(128)S(1)} %pad_add_fusion.1.table_ref, bf16[2048,128]{1,0:T(8,128)(2,1)} %get-tuple-element.48.refs_0_, bf16[2048,128]{1,0:T(8,128)(2,1)S(1)} %collective-permute-done.21.refs_1_, bf16[2048,128]{1,0:T(8,128)(2,1)} %collective-permute-done.16.refs_2_, ...), custom_call_target="tpu_custom_call" | custom-call | flops 1 | bytes 20971520 | tf_op jit(solution)/shard_map/attend_own_plane/pallas_call | solution.py:557
  93.0 3.5 %collective-permute-start.26 = (bf16[2,128,128]{2,1,0:T(8,128)(2,1)S(1)}, bf16[2,128,128]{2,1,0:T(8,128)(2,1)S(1)}, u32[]{:S(2)}, u32[]{:S(2)}) collective-permute-start(bf16[2,128,128]{2,1,0:T(8,128)(2,1)S(1)} %pad_maximum_fusion.3), channel_id=1, source_target_pairs={{0,8},{1,9},{2,10},{3,11},{4,12},{5,13},{6,14},{7,15},{8,0},{9,1},... | collective-permute-start | bytes 196616 | tf_op jit(solution)/shard_map/ppermute | solution.py:675
  96.7 5.8 %attend_far_plane.1 = (f32[520,128]{1,0:T(8,128)S(1)}, f32[520,128]{1,0:T(8,128)S(1)}) custom-call(s32[37]{0:T(128)S(1)} %pad_add_fusion.1.table_ref, bf16[2048,128]{1,0:T(8,128)(2,1)} %collective-permute-done.6.refs_0_, bf16[2048,128]{1,0:T(8,128)(2,1)S(1)} %collective-permute-done.19.refs_1_, bf16[2048,128]{1,0:T(8,128)(2,1)S(1)} %collective-permute-done.20.refs_2_, ...), custom_call_target="tpu_custom_call" | custom-call | flops 1 | bytes 20971520 | tf_op jit(solution)/shard_map/attend_far_plane/pallas_call | solution.py:557
  102.6 3.6 %collective-permute-start.25 = (f32[520,128]{1,0:T(8,128)S(1)}, f32[520,128]{1,0:T(8,128)S(1)}, u32[]{:S(2)}, u32[]{:S(2)}) collective-permute-start(f32[520,128]{1,0:T(8,128)S(1)} %get-tuple-element.63), channel_id=1, source_target_pairs={{0,4},{1,5},{2,6},{3,7},{4,0},{5,1},{6,2},{7,3},{8,12},{9,13},{10,... | collective-permute-start | bytes 798728 | tf_op jit(solution)/shard_map/ppermute | solution.py:675
  106.8 1.6 %collective-permute-start.29 = (bf16[4,128,128]{2,1,0:T(8,128)(2,1)S(1)}, bf16[4,128,128]{2,1,0:T(8,128)(2,1)S(1)}, u32[]{:S(2)}, u32[]{:S(2)}) collective-permute-start(bf16[4,128,128]{2,1,0:T(8,128)(2,1)S(1)} %pad_maximum_fusion.2.near_ref), channel_id=1, source_target_pairs={{0,3},{1,2},{2,1},{3,0},{4,7},{5,6},{6,5},{7,4},{8,11},{9,10},{10,... | collective-permute-start | bytes 393224 | tf_op jit(solution)/shard_map/ppermute | solution.py:675
  109.0 3.7 %collective-permute-done.27.side_ref = bf16[4,128,128]{2,1,0:T(8,128)(2,1)S(1)} collective-permute-done((bf16[4,128,128]{2,1,0:T(8,128)(2,1)S(1)}, bf16[4,128,128]{2,1,0:T(8,128)(2,1)S(1)}, u32[]{:S(2)}, u32[]{:S(2)}) %collective-permute-start.27) | collective-permute-done | bytes 131104 | tf_op jit(solution)/shard_map/ppermute | solution.py:675
  113.4 2.0 %new_tokens.1 = (f32[520,128]{1,0:T(8,128)S(1)}, bf16[2,64,2,128]{3,2,1,0:T(2,128)(2,1)}) custom-call(s32[8]{0:T(128)S(1)} %concatenate.27.place_ref, bf16[4,128,128]{2,1,0:T(8,128)(2,1)S(1)} %pad_maximum_fusion.2.near_ref, bf16[4,128,128]{2,1,0:T(8,128)(2,1)S(1)} %collective-permute-done.27.side_ref, ...), custom_call_target="tpu_custom_call" | custom-call | bytes 2097152 | tf_op jit(solution)/shard_map/new_tokens/pallas_call | solution.py:634
  (107 shorter events, 23.4 us)
Async XLA Ops:
  3.3 8.6 %collective-permute-start.1 = (f32[512]{0:T(512)S(1)}, f32[512]{0:T(512)S(1)}, u32[]{:S(2)}, u32[]{:S(2)}) collective-permute-start(f32[512]{0:T(512)S(1)} %add.61), channel_id=1, source_target_pairs={{0,2},{1,3},{2,0},{3,1},{4,6},{5,7},{6,4},{7,5},{8,10},{9,11},{10,... | collective-permute-start | bytes 6152 | tf_op jit(solution)/shard_map/ppermute | solution.py:675
  11.8 31.0 %collective-permute-start.10 = (bf16[5120,128]{1,0:T(8,128)(2,1)}, bf16[5120,128]{1,0:T(8,128)(2,1)}, u32[]{:S(2)}, u32[]{:S(2)}) collective-permute-start(bf16[5120,128]{1,0:T(8,128)(2,1)} %get-tuple-element.42), channel_id=1, source_target_pairs={{0,2},{1,3},{2,0},{3,1},{4,6},{5,7},{6,4},{7,5},{8,10},{9,11},{10,... | collective-permute-start | bytes 3932168 | tf_op jit(solution)/shard_map/ppermute | solution.py:675
  12.7 16.1 %collective-permute-start.2 = (bf16[528,512]{1,0:T(8,128)(2,1)S(1)}, bf16[528,512]{1,0:T(8,128)(2,1)}, u32[]{:S(2)}, u32[]{:S(2)}) collective-permute-start(bf16[528,512]{1,0:T(8,128)(2,1)S(1)} %add_sums.1.own_ref), channel_id=1, source_target_pairs={{4,0},{5,1},{6,2},{7,3},{8,4},{9,5},{10,6},{11,7},{12,8},{13,9},{1... | collective-permute-start | bytes 1622024 | tf_op jit(solution)/shard_map/ppermute | solution.py:689
  14.0 15.8 %collective-permute-start.3 = (bf16[528,512]{1,0:T(8,128)(2,1)S(1)}, bf16[528,512]{1,0:T(8,128)(2,1)}, u32[]{:S(2)}, u32[]{:S(2)}) collective-permute-start(bf16[528,512]{1,0:T(8,128)(2,1)S(1)} %add_sums.1.own_ref), channel_id=1, source_target_pairs={{0,4},{1,5},{2,6},{3,7},{4,8},{5,9},{6,10},{7,11},{8,12},{9,13},{1... | collective-permute-start | bytes 1622024 | tf_op jit(solution)/shard_map/ppermute | solution.py:689
  19.3 32.5 %collective-permute-start.9 = (bf16[2560,128]{1,0:T(8,128)(2,1)}, bf16[2560,128]{1,0:T(8,128)(2,1)}, u32[]{:S(2)}, u32[]{:S(2)}) collective-permute-start(bf16[2560,128]{1,0:T(8,128)(2,1)} %get-tuple-element.40), channel_id=1, source_target_pairs={{0,1},{1,0},{2,3},{3,2},{4,5},{5,4},{6,7},{7,6},{8,9},{9,8},{10,11... | collective-permute-start | bytes 1966088 | tf_op jit(solution)/shard_map/ppermute | solution.py:675
  29.8 15.8 %collective-permute-start.4 = (bf16[528,512]{1,0:T(8,128)(2,1)}, bf16[528,512]{1,0:T(8,128)(2,1)S(1)}, u32[]{:S(2)}, u32[]{:S(2)}) collective-permute-start(bf16[528,512]{1,0:T(8,128)(2,1)} %collective-permute-done.2.refs_0_), channel_id=1, source_target_pairs={{4,0},{5,1},{6,2},{7,3},{8,4},{9,5},{10,6},{11,7},{20,16},{21,17},... | collective-permute-start | bytes 1622024 | tf_op jit(solution)/shard_map/ppermute | solution.py:689
  31.1 15.8 %collective-permute-start.5 = (bf16[528,512]{1,0:T(8,128)(2,1)}, bf16[528,512]{1,0:T(8,128)(2,1)S(1)}, u32[]{:S(2)}, u32[]{:S(2)}) collective-permute-start(bf16[528,512]{1,0:T(8,128)(2,1)} %collective-permute-done.3.refs_3_), channel_id=1, source_target_pairs={{4,8},{5,9},{6,10},{7,11},{8,12},{9,13},{10,14},{11,15},{20,24},{2... | collective-permute-start | bytes 1622024 | tf_op jit(solution)/shard_map/ppermute | solution.py:689
  44.8 16.7 %collective-permute-start.11 = (bf16[2560,128]{1,0:T(8,128)(2,1)}, bf16[2560,128]{1,0:T(8,128)(2,1)}, u32[]{:S(2)}, u32[]{:S(2)}) collective-permute-start(bf16[2560,128]{1,0:T(8,128)(2,1)} %slice.14), channel_id=1, source_target_pairs={{0,1},{1,0},{2,3},{3,2},{4,5},{5,4},{6,7},{7,6},{8,9},{9,8},{10,11... | collective-permute-start | bytes 1966088 | tf_op jit(solution)/shard_map/ppermute | solution.py:675
  45.7 15.8 %collective-permute-start.7 = (bf16[528,512]{1,0:T(8,128)(2,1)S(1)}, bf16[528,512]{1,0:T(8,128)(2,1)S(1)}, u32[]{:S(2)}, u32[]{:S(2)}) collective-permute-start(bf16[528,512]{1,0:T(8,128)(2,1)S(1)} %collective-permute-done.4.refs_1_), channel_id=1, source_target_pairs={{4,0},{5,1},{6,2},{7,3},{20,16},{21,17},{22,18},{23,19}} | collective-permute-start | bytes 1622024 | tf_op jit(solution)/shard_map/ppermute | solution.py:689
  47.0 14.5 %collective-permute-start.8 = (bf16[528,512]{1,0:T(8,128)(2,1)S(1)}, bf16[528,512]{1,0:T(8,128)(2,1)}, u32[]{:S(2)}, u32[]{:S(2)}) collective-permute-start(bf16[528,512]{1,0:T(8,128)(2,1)S(1)} %collective-permute-done.5.refs_4_), channel_id=1, source_target_pairs={{8,12},{9,13},{10,14},{11,15},{24,28},{25,29},{26,30},{27,31}} | collective-permute-start | bytes 1622024 | tf_op jit(solution)/shard_map/ppermute | solution.py:689
  48.4 18.0 %collective-permute-start.16 = (bf16[2048,128]{1,0:T(8,128)(2,1)}, bf16[2048,128]{1,0:T(8,128)(2,1)}, u32[]{:S(2)}, u32[]{:S(2)}) collective-permute-start(bf16[2048,128]{1,0:T(8,128)(2,1)} %get-tuple-element.48.refs_0_), channel_id=1, source_target_pairs={{0,2},{1,3},{2,0},{3,1},{4,6},{5,7},{6,4},{7,5},{8,10},{9,11},{10,... | collective-permute-start | bytes 1572872 | tf_op jit(solution)/shard_map/ppermute | solution.py:675
  51.9 27.0 %collective-permute-start.6 = (bf16[2048,128]{1,0:T(8,128)(2,1)}, bf16[2048,128]{1,0:T(8,128)(2,1)}, u32[]{:S(2)}, u32[]{:S(2)}) collective-permute-start(bf16[2048,128]{1,0:T(8,128)(2,1)} %copy-done.7), channel_id=1, source_target_pairs={{0,8},{1,9},{2,10},{3,11},{4,12},{5,13},{6,14},{7,15},{8,0},{9,1},... | collective-permute-start | bytes 1572872 | tf_op jit(solution)/shard_map/ppermute | solution.py:675
  67.2 14.0 %collective-permute-start.21 = (bf16[2048,128]{1,0:T(8,128)(2,1)}, bf16[2048,128]{1,0:T(8,128)(2,1)S(1)}, u32[]{:S(2)}, u32[]{:S(2)}) collective-permute-start(bf16[2048,128]{1,0:T(8,128)(2,1)} %get-tuple-element.48.refs_0_), channel_id=1, source_target_pairs={{0,1},{1,0},{2,3},{3,2},{4,5},{5,4},{6,7},{7,6},{8,9},{9,8},{10,11... | collective-permute-start | bytes 1572872 | tf_op jit(solution)/shard_map/ppermute | solution.py:675
  68.0 10.9 %collective-permute-start.18 = (f32[320,128]{1,0:T(8,128)S(1)}, f32[320,128]{1,0:T(8,128)S(1)}, u32[]{:S(2)}, u32[]{:S(2)}) collective-permute-start(f32[320,128]{1,0:T(8,128)S(1)} %add.68), channel_id=1, source_target_pairs={{0,2},{1,3},{2,0},{3,1},{4,6},{5,7},{6,4},{7,5},{8,10},{9,11},{10,... | collective-permute-start | bytes 491528 | tf_op jit(solution)/shard_map/ppermute | solution.py:675
  68.4 10.5 %collective-permute-start.17 = (f32[320,128]{1,0:T(8,128)S(1)}, f32[320,128]{1,0:T(8,128)S(1)}, u32[]{:S(2)}, u32[]{:S(2)}) collective-permute-start(f32[320,128]{1,0:T(8,128)S(1)} %add.67), channel_id=1, source_target_pairs={{0,2},{1,3},{2,0},{3,1},{4,6},{5,7},{6,4},{7,5},{8,10},{9,11},{10,... | collective-permute-start | bytes 491528 | tf_op jit(solution)/shard_map/ppermute | solution.py:675
  71.8 9.5 %collective-permute-start.22 = (bf16[2048,128]{1,0:T(8,128)(2,1)}, bf16[2048,128]{1,0:T(8,128)(2,1)S(1)}, u32[]{:S(2)}, u32[]{:S(2)}) collective-permute-start(bf16[2048,128]{1,0:T(8,128)(2,1)} %collective-permute-done.16.refs_2_), channel_id=1, source_target_pairs={{0,1},{1,0},{2,3},{3,2},{4,5},{5,4},{6,7},{7,6},{8,9},{9,8},{10,11... | collective-permute-start | bytes 1572872 | tf_op jit(solution)/shard_map/ppermute | solution.py:675
  78.9 14.1 %collective-permute-start.20 = (bf16[2048,128]{1,0:T(8,128)(2,1)}, bf16[2048,128]{1,0:T(8,128)(2,1)S(1)}, u32[]{:S(2)}, u32[]{:S(2)}) collective-permute-start(bf16[2048,128]{1,0:T(8,128)(2,1)} %collective-permute-done.6.refs_0_), channel_id=1, source_target_pairs={{0,2},{1,3},{2,0},{3,1},{4,6},{5,7},{6,4},{7,5},{8,10},{9,11},{10,... | collective-permute-start | bytes 1572872 | tf_op jit(solution)/shard_map/ppermute | solution.py:675
  80.9 5.9 %collective-permute-start.23 = (bf16[640,128]{1,0:T(8,128)(2,1)S(1)}, bf16[640,128]{1,0:T(8,128)(2,1)S(1)}, u32[]{:S(2)}, u32[]{:S(2)}) collective-permute-start(bf16[640,128]{1,0:T(8,128)(2,1)S(1)} %finish_projection.1.refs_4_.query_ref), channel_id=1, source_target_pairs={{0,4},{1,5},{2,6},{3,7},{4,0},{5,1},{6,2},{7,3},{8,12},{9,13},{10,... | collective-permute-start | bytes 491528 | tf_op jit(solution)/shard_map/ppermute | solution.py:675
  81.2 15.5 %collective-permute-start.19 = (bf16[2048,128]{1,0:T(8,128)(2,1)}, bf16[2048,128]{1,0:T(8,128)(2,1)S(1)}, u32[]{:S(2)}, u32[]{:S(2)}) collective-permute-start(bf16[2048,128]{1,0:T(8,128)(2,1)} %collective-permute-done.6.refs_0_), channel_id=1, source_target_pairs={{0,1},{1,0},{2,3},{3,2},{4,5},{5,4},{6,7},{7,6},{8,9},{9,8},{10,11... | collective-permute-start | bytes 1572872 | tf_op jit(solution)/shard_map/ppermute | solution.py:675
  93.0 13.2 %collective-permute-start.26 = (bf16[2,128,128]{2,1,0:T(8,128)(2,1)S(1)}, bf16[2,128,128]{2,1,0:T(8,128)(2,1)S(1)}, u32[]{:S(2)}, u32[]{:S(2)}) collective-permute-start(bf16[2,128,128]{2,1,0:T(8,128)(2,1)S(1)} %pad_maximum_fusion.3), channel_id=1, source_target_pairs={{0,8},{1,9},{2,10},{3,11},{4,12},{5,13},{6,14},{7,15},{8,0},{9,1},... | collective-permute-start | bytes 196616 | tf_op jit(solution)/shard_map/ppermute | solution.py:675
  102.6 12.9 %collective-permute-start.25 = (f32[520,128]{1,0:T(8,128)S(1)}, f32[520,128]{1,0:T(8,128)S(1)}, u32[]{:S(2)}, u32[]{:S(2)}) collective-permute-start(f32[520,128]{1,0:T(8,128)S(1)} %get-tuple-element.63), channel_id=1, source_target_pairs={{0,4},{1,5},{2,6},{3,7},{4,0},{5,1},{6,2},{7,3},{8,12},{9,13},{10,... | collective-permute-start | bytes 798728 | tf_op jit(solution)/shard_map/ppermute | solution.py:675
  106.2 6.4 %collective-permute-start.27 = (bf16[4,128,128]{2,1,0:T(8,128)(2,1)S(1)}, bf16[4,128,128]{2,1,0:T(8,128)(2,1)S(1)}, u32[]{:S(2)}, u32[]{:S(2)}) collective-permute-start(bf16[4,128,128]{2,1,0:T(8,128)(2,1)S(1)} %pad_maximum_fusion.2.near_ref), channel_id=1, source_target_pairs={{0,2},{1,3},{2,0},{3,1},{4,6},{5,7},{6,4},{7,5},{8,10},{9,11},{10,... | collective-permute-start | bytes 393224 | tf_op jit(solution)/shard_map/ppermute | solution.py:675
  106.8 5.9 %collective-permute-start.28 = (bf16[4,128,128]{2,1,0:T(8,128)(2,1)S(1)}, bf16[4,128,128]{2,1,0:T(8,128)(2,1)S(1)}, u32[]{:S(2)}, u32[]{:S(2)}) collective-permute-start(bf16[4,128,128]{2,1,0:T(8,128)(2,1)S(1)} %pad_maximum_fusion.2.near_ref), channel_id=1, source_target_pairs={{0,1},{1,0},{2,3},{3,2},{4,5},{5,4},{6,7},{7,6},{8,9},{9,8},{10,11... | collective-permute-start | bytes 393224 | tf_op jit(solution)/shard_map/ppermute | solution.py:675
  106.8 6.6 %collective-permute-start.29 = (bf16[4,128,128]{2,1,0:T(8,128)(2,1)S(1)}, bf16[4,128,128]{2,1,0:T(8,128)(2,1)S(1)}, u32[]{:S(2)}, u32[]{:S(2)}) collective-permute-start(bf16[4,128,128]{2,1,0:T(8,128)(2,1)S(1)} %pad_maximum_fusion.2.near_ref), channel_id=1, source_target_pairs={{0,3},{1,2},{2,1},{3,0},{4,7},{5,6},{6,5},{7,4},{8,11},{9,10},{10,... | collective-permute-start | bytes 393224 | tf_op jit(solution)/shard_map/ppermute | solution.py:675
  (18 other events, 142.2 us)

commit v5 on v4

--- a/solution.py
+++ b/solution.py
@@ -761,7 +761,6 @@
     got = [swap(part, 1) for part in sums[2:4] + sums[6:8]]
     got = after(got, mine_side)
     far_sum = [swap(sums[4 + n] + got[2 + n], 2) for n in range(2)]
-    far_sum = after(far_sum, far_pages)
     query_kv = finish(sums[:2], got[:2], far_sum, cos_wide, sin_wide)
 
     far_pages = after(far_pages, far_sum)

time: 117 us -> 117 us (level)
  Pallas kernels: 27.5 us -> 25.6 us
  waiting for transfers between devices: 38.2 us -> 40.1 us
  transfers between devices with their start and end apart: 30 -> 30, of which waited for: 15 -> 15; matrix products, arithmetic and copies ran while one was open for 7% -> 7% of each run, Pallas kernels for 22% -> 21%
where the time goes in v5:
time: 117 us; the launch traced here: 116 us
  waiting for transfers between devices  40.1 us (34%)
  starting transfers between devices  35 us (30%)
  Pallas kernels  25.6 us (22%)
  local copies, waits for them, and re-layouts  8 us (7%)
  other arithmetic  6.26 us (5%)
    ppermute x24, waiting for transfers between devices, swap(): return lax.ppermute(values, 'inst', [(i, i ^ bits) for i in range(16)])  30.8 us
    ppermute x24, starting transfers between devices, swap(): return lax.ppermute(values, 'inst', [(i, i ^ bits) for i in range(16)])  23.6 us
    ppermute x6, starting transfers between devices, hop(): return lax.ppermute(values, 'inst', pairs)  11.4 us
    pallas_call x2, Pallas kernels, attend(): pl.pallas_call(functools.partial(attend_kernel, offset, page_len, bool(ea...  10.6 us
    ppermute x6, waiting for transfers between devices, hop(): return lax.ppermute(values, 'inst', pairs)  9.24 us
    unnamed x26, local copies, waits for them, and re-layouts  5 us
    pallas_call x1, Pallas kernels, pick_pages(): pl.pallas_call(pick_pages_kernel, out_shape=(block, block), in_specs=in_s...  4.92 us
    pallas_call x1, Pallas kernels, project(): pl.pallas_call(project_kernel, out_shape=(out,) * 8, in_specs=in_smem(1)...  4.25 us
  transfers between devices with their start and end apart: 30, of which 15 were waited for; matrix products, arithmetic and copies ran while one was open for 7% of the time, Pallas kernels for 21%

profile of v5, /device:TPU:0, one launch (start us, length us, event | category | flops | bytes accessed | tf_op | source)
XLA Modules:
  0.0 115.9 jit_solution(12654044046270056783)
XLA Ops:
  3.3 2.9 %collective-permute-start.1 = (f32[512]{0:T(512)S(1)}, f32[512]{0:T(512)S(1)}, u32[]{:S(2)}, u32[]{:S(2)}) collective-permute-start(f32[512]{0:T(512)S(1)} %add.61), channel_id=1, source_target_pairs={{0,2},{1,3},{2,0},{3,1},{4,6},{5,7},{6,4},{7,5},{8,10},{9,11},{10,... | collective-permute-start | bytes 6152 | tf_op jit(solution)/shard_map/ppermute | solution.py:675
  6.2 1.6 %copy-done = bf16[8192,128]{1,0:T(8,128)(2,1)S(1)} copy-done((bf16[8192,128]{1,0:T(8,128)(2,1)S(1)}, bf16[8192,128]{1,0:T(8,128)(2,1)}, u32[]{:S(2)}) %copy-start) | copy-done | bytes 2097176
  9.7 2.1 %pack_weights.1 = (bf16[2560,128]{1,0:T(8,128)(2,1)S(1)}, bf16[2560,128]{1,0:T(8,128)(2,1)}, bf16[5120,128]{1,0:T(8,128)(2,1)}) custom-call(s32[4]{0:T(128)S(1)} %pad_add_fusion.2.place_ref, bf16[8192,128]{1,0:T(8,128)(2,1)S(1)} %copy-done, bf16[16,8192]{1,0:T(8,128)(2,1)S(1)} %bitcast.24, bf16[16,8192]{1,0:T(8,128)(2,1)S(1)} %bitcast.25), custom_call_target="tpu_custom_call" | custom-call | flops 1 | bytes 1 | tf_op jit(solution)/shard_map/pack_weights/pallas_call | solution.py:314
  14.0 5.4 %collective-permute-start.3 = (bf16[528,512]{1,0:T(8,128)(2,1)S(1)}, bf16[528,512]{1,0:T(8,128)(2,1)}, u32[]{:S(2)}, u32[]{:S(2)}) collective-permute-start(bf16[528,512]{1,0:T(8,128)(2,1)S(1)} %add_sums.1.own_ref), channel_id=1, source_target_pairs={{0,4},{1,5},{2,6},{3,7},{4,8},{5,9},{6,10},{7,11},{8,12},{9,13},{1... | collective-permute-start | bytes 1622024 | tf_op jit(solution)/shard_map/ppermute | solution.py:689
  19.5 4.9 %pick_pages.1 = (bf16[2048,128]{1,0:T(8,128)(2,1)}, bf16[2048,128]{1,0:T(8,128)(2,1)S(1)}) custom-call(s32[4]{0:T(128)S(1)} %pad_add_fusion.2.place_ref, s32[128]{0:T(128)S(1)} %reshape.118.hits_ref, bf16[32,64,2,256]{3,2,1,0:T(2,128)(2,1)S(1)} %copy-done.1), custom_call_target="tpu_custom_call" | custom-call | bytes 4194304 | tf_op jit(solution)/shard_map/pick_pages/pallas_call | solution.py:266
  25.3 3.5 %collective-permute-done.2.refs_0_ = bf16[528,512]{1,0:T(8,128)(2,1)} collective-permute-done((bf16[528,512]{1,0:T(8,128)(2,1)S(1)}, bf16[528,512]{1,0:T(8,128)(2,1)}, u32[]{:S(2)}, u32[]{:S(2)}) %collective-permute-start.2) | collective-permute-done | bytes 540704 | tf_op jit(solution)/shard_map/ppermute | solution.py:689
  31.9 10.9 %collective-permute-done.10.refs_8_ = bf16[5120,128]{1,0:T(8,128)(2,1)} collective-permute-done((bf16[5120,128]{1,0:T(8,128)(2,1)}, bf16[5120,128]{1,0:T(8,128)(2,1)}, u32[]{:S(2)}, u32[]{:S(2)}) %collective-permute-start.10) | collective-permute-done | bytes 1310752 | tf_op jit(solution)/shard_map/ppermute | solution.py:675
  42.8 2.0 %slice.14 = bf16[2560,128]{1,0:T(8,128)(2,1)} slice(bf16[5120,128]{1,0:T(8,128)(2,1)} %collective-permute-done.10.refs_8_), slice={[2560:5120], [0:128]} | slice | bytes 1310720 | tf_op jit(solution)/shard_map/slice | solution.py:736
  47.0 1.5 %collective-permute-start.8 = (bf16[528,512]{1,0:T(8,128)(2,1)S(1)}, bf16[528,512]{1,0:T(8,128)(2,1)}, u32[]{:S(2)}, u32[]{:S(2)}) collective-permute-start(bf16[528,512]{1,0:T(8,128)(2,1)S(1)} %collective-permute-done.5.refs_4_), channel_id=1, source_target_pairs={{8,12},{9,13},{10,14},{11,15},{24,28},{25,29},{26,30},{27,31}} | collective-permute-start | bytes 1622024 | tf_op jit(solution)/shard_map/ppermute | solution.py:689
  50.0 1.9 %fusion = (f32[512,64]{1,0:T(8,128)}, f32[512,64]{1,0:T(8,128)}, f32[512,64]{1,0:T(8,128)}) fusion(f32[64]{0:T(128)S(1)} %negate_power_fusion, f32[512]{0:T(512)S(1)} %bitcast.28), kind=kLoop, calls=%fused_computation.9 | loop fusion | flops 65536 | bytes 395520 | tf_op jit(solution)/shard_map/neg | solution.py:756
  51.9 5.7 %collective-permute-start.6 = (bf16[2048,128]{1,0:T(8,128)(2,1)}, bf16[2048,128]{1,0:T(8,128)(2,1)}, u32[]{:S(2)}, u32[]{:S(2)}) collective-permute-start(bf16[2048,128]{1,0:T(8,128)(2,1)} %copy-done.7), channel_id=1, source_target_pairs={{0,8},{1,9},{2,10},{3,11},{4,12},{5,13},{6,14},{7,15},{8,0},{9,1},... | collective-permute-start | bytes 1572872 | tf_op jit(solution)/shard_map/ppermute | solution.py:675
  57.6 3.9 %collective-permute-done.7.refs_2_ = bf16[528,512]{1,0:T(8,128)(2,1)S(1)} collective-permute-done((bf16[528,512]{1,0:T(8,128)(2,1)S(1)}, bf16[528,512]{1,0:T(8,128)(2,1)S(1)}, u32[]{:S(2)}, u32[]{:S(2)}) %collective-permute-start.7) | collective-permute-done | bytes 540704 | tf_op jit(solution)/shard_map/ppermute | solution.py:689
  61.5 4.3 %project.1 = (f32[320,128]{1,0:T(8,128)S(1)}, f32[320,128]{1,0:T(8,128)S(1)}, f32[320,128]{1,0:T(8,128)S(1)}, f32[320,128]{1,0:T(8,128)S(1)}, f32[320,128]{1,0:T...) custom-call(s32[4]{0:T(128)S(1)} %pad_add_fusion.2.place_ref, ...), custom_call_target="tpu_custom_call" | custom-call | flops 335544320 | bytes 6291456 | tf_op jit(solution)/shard_map/project/pallas_call | solution.py:403
  68.4 1.8 %collective-permute-start.17 = (f32[320,128]{1,0:T(8,128)S(1)}, f32[320,128]{1,0:T(8,128)S(1)}, u32[]{:S(2)}, u32[]{:S(2)}) collective-permute-start(f32[320,128]{1,0:T(8,128)S(1)} %add.67), channel_id=1, source_target_pairs={{0,2},{1,3},{2,0},{3,1},{4,6},{5,7},{6,4},{7,5},{8,10},{9,11},{10,... | collective-permute-start | bytes 491528 | tf_op jit(solution)/shard_map/ppermute | solution.py:675
  71.9 7.0 %collective-permute-done.6.refs_0_ = bf16[2048,128]{1,0:T(8,128)(2,1)} collective-permute-done((bf16[2048,128]{1,0:T(8,128)(2,1)}, bf16[2048,128]{1,0:T(8,128)(2,1)}, u32[]{:S(2)}, u32[]{:S(2)}) %collective-permute-start.6) | collective-permute-done | bytes 524320 | tf_op jit(solution)/shard_map/ppermute | solution.py:675
  78.9 1.7 %collective-permute-start.20 = (bf16[2048,128]{1,0:T(8,128)(2,1)}, bf16[2048,128]{1,0:T(8,128)(2,1)S(1)}, u32[]{:S(2)}, u32[]{:S(2)}) collective-permute-start(bf16[2048,128]{1,0:T(8,128)(2,1)} %collective-permute-done.6.refs_0_), channel_id=1, source_target_pairs={{0,2},{1,3},{2,0},{3,1},{4,6},{5,7},{6,4},{7,5},{8,10},{9,11},{10,... | collective-permute-start | bytes 1572872 | tf_op jit(solution)/shard_map/ppermute | solution.py:675
  81.3 5.5 %collective-permute-done.23.refs_5_ = bf16[640,128]{1,0:T(8,128)(2,1)S(1)} collective-permute-done((bf16[640,128]{1,0:T(8,128)(2,1)S(1)}, bf16[640,128]{1,0:T(8,128)(2,1)S(1)}, u32[]{:S(2)}, u32[]{:S(2)}) %collective-permute-start.23) | collective-permute-done | bytes 163872 | tf_op jit(solution)/shard_map/ppermute | solution.py:675
  86.8 4.8 %attend_own_plane.1 = (f32[520,128]{1,0:T(8,128)S(1)}, f32[520,128]{1,0:T(8,128)S(1)}) custom-call(s32[37]{0:T(128)S(1)} %pad_add_fusion.1.table_ref, bf16[2048,128]{1,0:T(8,128)(2,1)} %get-tuple-element.46.refs_0_, bf16[2048,128]{1,0:T(8,128)(2,1)S(1)} %collective-permute-done.21.refs_1_, bf16[2048,128]{1,0:T(8,128)(2,1)} %collective-permute-done.16.refs_2_, ...), custom_call_target="tpu_custom_call" | custom-call | flops 1 | bytes 20971520 | tf_op jit(solution)/shard_map/attend_own_plane/pallas_call | solution.py:557
  93.0 3.5 %collective-permute-start.26 = (bf16[2,128,128]{2,1,0:T(8,128)(2,1)S(1)}, bf16[2,128,128]{2,1,0:T(8,128)(2,1)S(1)}, u32[]{:S(2)}, u32[]{:S(2)}) collective-permute-start(bf16[2,128,128]{2,1,0:T(8,128)(2,1)S(1)} %pad_maximum_fusion.3), channel_id=1, source_target_pairs={{0,8},{1,9},{2,10},{3,11},{4,12},{5,13},{6,14},{7,15},{8,0},{9,1},... | collective-permute-start | bytes 196616 | tf_op jit(solution)/shard_map/ppermute | solution.py:675
  96.7 5.8 %attend_far_plane.1 = (f32[520,128]{1,0:T(8,128)S(1)}, f32[520,128]{1,0:T(8,128)S(1)}) custom-call(s32[37]{0:T(128)S(1)} %pad_add_fusion.1.table_ref, bf16[2048,128]{1,0:T(8,128)(2,1)} %collective-permute-done.6.refs_0_, bf16[2048,128]{1,0:T(8,128)(2,1)S(1)} %collective-permute-done.19.refs_1_, bf16[2048,128]{1,0:T(8,128)(2,1)S(1)} %collective-permute-done.20.refs_2_, ...), custom_call_target="tpu_custom_call" | custom-call | flops 1 | bytes 20971520 | tf_op jit(solution)/shard_map/attend_far_plane/pallas_call | solution.py:557
  102.6 2.7 %collective-permute-start.25 = (f32[520,128]{1,0:T(8,128)S(1)}, f32[520,128]{1,0:T(8,128)S(1)}, u32[]{:S(2)}, u32[]{:S(2)}) collective-permute-start(f32[520,128]{1,0:T(8,128)S(1)} %get-tuple-element.59), channel_id=1, source_target_pairs={{0,4},{1,5},{2,6},{3,7},{4,0},{5,1},{6,2},{7,3},{8,12},{9,13},{10,... | collective-permute-start | bytes 798728 | tf_op jit(solution)/shard_map/ppermute | solution.py:675
  105.8 1.6 %collective-permute-start.29 = (bf16[4,128,128]{2,1,0:T(8,128)(2,1)S(1)}, bf16[4,128,128]{2,1,0:T(8,128)(2,1)S(1)}, u32[]{:S(2)}, u32[]{:S(2)}) collective-permute-start(bf16[4,128,128]{2,1,0:T(8,128)(2,1)S(1)} %pad_maximum_fusion.2.near_ref), channel_id=1, source_target_pairs={{0,3},{1,2},{2,1},{3,0},{4,7},{5,6},{6,5},{7,4},{8,11},{9,10},{10,... | collective-permute-start | bytes 393224 | tf_op jit(solution)/shard_map/ppermute | solution.py:675
  108.0 3.7 %collective-permute-done.27.side_ref = bf16[4,128,128]{2,1,0:T(8,128)(2,1)S(1)} collective-permute-done((bf16[4,128,128]{2,1,0:T(8,128)(2,1)S(1)}, bf16[4,128,128]{2,1,0:T(8,128)(2,1)S(1)}, u32[]{:S(2)}, u32[]{:S(2)}) %collective-permute-start.27) | collective-permute-done | bytes 131104 | tf_op jit(solution)/shard_map/ppermute | solution.py:675
  112.4 2.0 %new_tokens.1 = (f32[520,128]{1,0:T(8,128)S(1)}, bf16[2,64,2,128]{3,2,1,0:T(2,128)(2,1)}) custom-call(s32[8]{0:T(128)S(1)} %concatenate.27.place_ref, bf16[4,128,128]{2,1,0:T(8,128)(2,1)S(1)} %pad_maximum_fusion.2.near_ref, bf16[4,128,128]{2,1,0:T(8,128)(2,1)S(1)} %collective-permute-done.27.side_ref, ...), custom_call_target="tpu_custom_call" | custom-call | bytes 2097152 | tf_op jit(solution)/shard_map/new_tokens/pallas_call | solution.py:634
  (107 shorter events, 24.3 us)
Async XLA Ops:
  3.3 8.6 %collective-permute-start.1 = (f32[512]{0:T(512)S(1)}, f32[512]{0:T(512)S(1)}, u32[]{:S(2)}, u32[]{:S(2)}) collective-permute-start(f32[512]{0:T(512)S(1)} %add.61), channel_id=1, source_target_pairs={{0,2},{1,3},{2,0},{3,1},{4,6},{5,7},{6,4},{7,5},{8,10},{9,11},{10,... | collective-permute-start | bytes 6152 | tf_op jit(solution)/shard_map/ppermute | solution.py:675
  11.8 31.0 %collective-permute-start.10 = (bf16[5120,128]{1,0:T(8,128)(2,1)}, bf16[5120,128]{1,0:T(8,128)(2,1)}, u32[]{:S(2)}, u32[]{:S(2)}) collective-permute-start(bf16[5120,128]{1,0:T(8,128)(2,1)} %get-tuple-element.40), channel_id=1, source_target_pairs={{0,2},{1,3},{2,0},{3,1},{4,6},{5,7},{6,4},{7,5},{8,10},{9,11},{10,... | collective-permute-start | bytes 3932168 | tf_op jit(solution)/shard_map/ppermute | solution.py:675
  12.7 16.1 %collective-permute-start.2 = (bf16[528,512]{1,0:T(8,128)(2,1)S(1)}, bf16[528,512]{1,0:T(8,128)(2,1)}, u32[]{:S(2)}, u32[]{:S(2)}) collective-permute-start(bf16[528,512]{1,0:T(8,128)(2,1)S(1)} %add_sums.1.own_ref), channel_id=1, source_target_pairs={{4,0},{5,1},{6,2},{7,3},{8,4},{9,5},{10,6},{11,7},{12,8},{13,9},{1... | collective-permute-start | bytes 1622024 | tf_op jit(solution)/shard_map/ppermute | solution.py:689
  14.0 15.8 %collective-permute-start.3 = (bf16[528,512]{1,0:T(8,128)(2,1)S(1)}, bf16[528,512]{1,0:T(8,128)(2,1)}, u32[]{:S(2)}, u32[]{:S(2)}) collective-permute-start(bf16[528,512]{1,0:T(8,128)(2,1)S(1)} %add_sums.1.own_ref), channel_id=1, source_target_pairs={{0,4},{1,5},{2,6},{3,7},{4,8},{5,9},{6,10},{7,11},{8,12},{9,13},{1... | collective-permute-start | bytes 1622024 | tf_op jit(solution)/shard_map/ppermute | solution.py:689
  19.3 32.5 %collective-permute-start.9 = (bf16[2560,128]{1,0:T(8,128)(2,1)}, bf16[2560,128]{1,0:T(8,128)(2,1)}, u32[]{:S(2)}, u32[]{:S(2)}) collective-permute-start(bf16[2560,128]{1,0:T(8,128)(2,1)} %get-tuple-element.38), channel_id=1, source_target_pairs={{0,1},{1,0},{2,3},{3,2},{4,5},{5,4},{6,7},{7,6},{8,9},{9,8},{10,11... | collective-permute-start | bytes 1966088 | tf_op jit(solution)/shard_map/ppermute | solution.py:675
  29.8 15.8 %collective-permute-start.4 = (bf16[528,512]{1,0:T(8,128)(2,1)}, bf16[528,512]{1,0:T(8,128)(2,1)S(1)}, u32[]{:S(2)}, u32[]{:S(2)}) collective-permute-start(bf16[528,512]{1,0:T(8,128)(2,1)} %collective-permute-done.2.refs_0_), channel_id=1, source_target_pairs={{4,0},{5,1},{6,2},{7,3},{8,4},{9,5},{10,6},{11,7},{20,16},{21,17},... | collective-permute-start | bytes 1622024 | tf_op jit(solution)/shard_map/ppermute | solution.py:689
  31.1 15.8 %collective-permute-start.5 = (bf16[528,512]{1,0:T(8,128)(2,1)}, bf16[528,512]{1,0:T(8,128)(2,1)S(1)}, u32[]{:S(2)}, u32[]{:S(2)}) collective-permute-start(bf16[528,512]{1,0:T(8,128)(2,1)} %collective-permute-done.3.refs_3_), channel_id=1, source_target_pairs={{4,8},{5,9},{6,10},{7,11},{8,12},{9,13},{10,14},{11,15},{20,24},{2... | collective-permute-start | bytes 1622024 | tf_op jit(solution)/shard_map/ppermute | solution.py:689
  44.8 16.7 %collective-permute-start.11 = (bf16[2560,128]{1,0:T(8,128)(2,1)}, bf16[2560,128]{1,0:T(8,128)(2,1)}, u32[]{:S(2)}, u32[]{:S(2)}) collective-permute-start(bf16[2560,128]{1,0:T(8,128)(2,1)} %slice.14), channel_id=1, source_target_pairs={{0,1},{1,0},{2,3},{3,2},{4,5},{5,4},{6,7},{7,6},{8,9},{9,8},{10,11... | collective-permute-start | bytes 1966088 | tf_op jit(solution)/shard_map/ppermute | solution.py:675
  45.7 15.8 %collective-permute-start.7 = (bf16[528,512]{1,0:T(8,128)(2,1)S(1)}, bf16[528,512]{1,0:T(8,128)(2,1)S(1)}, u32[]{:S(2)}, u32[]{:S(2)}) collective-permute-start(bf16[528,512]{1,0:T(8,128)(2,1)S(1)} %collective-permute-done.4.refs_1_), channel_id=1, source_target_pairs={{4,0},{5,1},{6,2},{7,3},{20,16},{21,17},{22,18},{23,19}} | collective-permute-start | bytes 1622024 | tf_op jit(solution)/shard_map/ppermute | solution.py:689
  47.0 14.5 %collective-permute-start.8 = (bf16[528,512]{1,0:T(8,128)(2,1)S(1)}, bf16[528,512]{1,0:T(8,128)(2,1)}, u32[]{:S(2)}, u32[]{:S(2)}) collective-permute-start(bf16[528,512]{1,0:T(8,128)(2,1)S(1)} %collective-permute-done.5.refs_4_), channel_id=1, source_target_pairs={{8,12},{9,13},{10,14},{11,15},{24,28},{25,29},{26,30},{27,31}} | collective-permute-start | bytes 1622024 | tf_op jit(solution)/shard_map/ppermute | solution.py:689
  48.4 18.0 %collective-permute-start.16 = (bf16[2048,128]{1,0:T(8,128)(2,1)}, bf16[2048,128]{1,0:T(8,128)(2,1)}, u32[]{:S(2)}, u32[]{:S(2)}) collective-permute-start(bf16[2048,128]{1,0:T(8,128)(2,1)} %get-tuple-element.46.refs_0_), channel_id=1, source_target_pairs={{0,2},{1,3},{2,0},{3,1},{4,6},{5,7},{6,4},{7,5},{8,10},{9,11},{10,... | collective-permute-start | bytes 1572872 | tf_op jit(solution)/shard_map/ppermute | solution.py:675
  51.9 27.0 %collective-permute-start.6 = (bf16[2048,128]{1,0:T(8,128)(2,1)}, bf16[2048,128]{1,0:T(8,128)(2,1)}, u32[]{:S(2)}, u32[]{:S(2)}) collective-permute-start(bf16[2048,128]{1,0:T(8,128)(2,1)} %copy-done.7), channel_id=1, source_target_pairs={{0,8},{1,9},{2,10},{3,11},{4,12},{5,13},{6,14},{7,15},{8,0},{9,1},... | collective-permute-start | bytes 1572872 | tf_op jit(solution)/shard_map/ppermute | solution.py:675
  67.2 14.0 %collective-permute-start.21 = (bf16[2048,128]{1,0:T(8,128)(2,1)}, bf16[2048,128]{1,0:T(8,128)(2,1)S(1)}, u32[]{:S(2)}, u32[]{:S(2)}) collective-permute-start(bf16[2048,128]{1,0:T(8,128)(2,1)} %get-tuple-element.46.refs_0_), channel_id=1, source_target_pairs={{0,1},{1,0},{2,3},{3,2},{4,5},{5,4},{6,7},{7,6},{8,9},{9,8},{10,11... | collective-permute-start | bytes 1572872 | tf_op jit(solution)/shard_map/ppermute | solution.py:675
  68.0 10.9 %collective-permute-start.18 = (f32[320,128]{1,0:T(8,128)S(1)}, f32[320,128]{1,0:T(8,128)S(1)}, u32[]{:S(2)}, u32[]{:S(2)}) collective-permute-start(f32[320,128]{1,0:T(8,128)S(1)} %add.68), channel_id=1, source_target_pairs={{0,2},{1,3},{2,0},{3,1},{4,6},{5,7},{6,4},{7,5},{8,10},{9,11},{10,... | collective-permute-start | bytes 491528 | tf_op jit(solution)/shard_map/ppermute | solution.py:675
  68.4 10.5 %collective-permute-start.17 = (f32[320,128]{1,0:T(8,128)S(1)}, f32[320,128]{1,0:T(8,128)S(1)}, u32[]{:S(2)}, u32[]{:S(2)}) collective-permute-start(f32[320,128]{1,0:T(8,128)S(1)} %add.67), channel_id=1, source_target_pairs={{0,2},{1,3},{2,0},{3,1},{4,6},{5,7},{6,4},{7,5},{8,10},{9,11},{10,... | collective-permute-start | bytes 491528 | tf_op jit(solution)/shard_map/ppermute | solution.py:675
  71.8 9.5 %collective-permute-start.22 = (bf16[2048,128]{1,0:T(8,128)(2,1)}, bf16[2048,128]{1,0:T(8,128)(2,1)S(1)}, u32[]{:S(2)}, u32[]{:S(2)}) collective-permute-start(bf16[2048,128]{1,0:T(8,128)(2,1)} %collective-permute-done.16.refs_2_), channel_id=1, source_target_pairs={{0,1},{1,0},{2,3},{3,2},{4,5},{5,4},{6,7},{7,6},{8,9},{9,8},{10,11... | collective-permute-start | bytes 1572872 | tf_op jit(solution)/shard_map/ppermute | solution.py:675
  78.9 14.1 %collective-permute-start.20 = (bf16[2048,128]{1,0:T(8,128)(2,1)}, bf16[2048,128]{1,0:T(8,128)(2,1)S(1)}, u32[]{:S(2)}, u32[]{:S(2)}) collective-permute-start(bf16[2048,128]{1,0:T(8,128)(2,1)} %collective-permute-done.6.refs_0_), channel_id=1, source_target_pairs={{0,2},{1,3},{2,0},{3,1},{4,6},{5,7},{6,4},{7,5},{8,10},{9,11},{10,... | collective-permute-start | bytes 1572872 | tf_op jit(solution)/shard_map/ppermute | solution.py:675
  80.9 5.9 %collective-permute-start.23 = (bf16[640,128]{1,0:T(8,128)(2,1)S(1)}, bf16[640,128]{1,0:T(8,128)(2,1)S(1)}, u32[]{:S(2)}, u32[]{:S(2)}) collective-permute-start(bf16[640,128]{1,0:T(8,128)(2,1)S(1)} %finish_projection.1.refs_4_.query_ref), channel_id=1, source_target_pairs={{0,4},{1,5},{2,6},{3,7},{4,0},{5,1},{6,2},{7,3},{8,12},{9,13},{10,... | collective-permute-start | bytes 491528 | tf_op jit(solution)/shard_map/ppermute | solution.py:675
  81.2 15.5 %collective-permute-start.19 = (bf16[2048,128]{1,0:T(8,128)(2,1)}, bf16[2048,128]{1,0:T(8,128)(2,1)S(1)}, u32[]{:S(2)}, u32[]{:S(2)}) collective-permute-start(bf16[2048,128]{1,0:T(8,128)(2,1)} %collective-permute-done.6.refs_0_), channel_id=1, source_target_pairs={{0,1},{1,0},{2,3},{3,2},{4,5},{5,4},{6,7},{7,6},{8,9},{9,8},{10,11... | collective-permute-start | bytes 1572872 | tf_op jit(solution)/shard_map/ppermute | solution.py:675
  93.0 12.3 %collective-permute-start.26 = (bf16[2,128,128]{2,1,0:T(8,128)(2,1)S(1)}, bf16[2,128,128]{2,1,0:T(8,128)(2,1)S(1)}, u32[]{:S(2)}, u32[]{:S(2)}) collective-permute-start(bf16[2,128,128]{2,1,0:T(8,128)(2,1)S(1)} %pad_maximum_fusion.3), channel_id=1, source_target_pairs={{0,8},{1,9},{2,10},{3,11},{4,12},{5,13},{6,14},{7,15},{8,0},{9,1},... | collective-permute-start | bytes 196616 | tf_op jit(solution)/shard_map/ppermute | solution.py:675
  102.6 11.9 %collective-permute-start.25 = (f32[520,128]{1,0:T(8,128)S(1)}, f32[520,128]{1,0:T(8,128)S(1)}, u32[]{:S(2)}, u32[]{:S(2)}) collective-permute-start(f32[520,128]{1,0:T(8,128)S(1)} %get-tuple-element.59), channel_id=1, source_target_pairs={{0,4},{1,5},{2,6},{3,7},{4,0},{5,1},{6,2},{7,3},{8,12},{9,13},{10,... | collective-permute-start | bytes 798728 | tf_op jit(solution)/shard_map/ppermute | solution.py:675
  105.3 6.4 %collective-permute-start.27 = (bf16[4,128,128]{2,1,0:T(8,128)(2,1)S(1)}, bf16[4,128,128]{2,1,0:T(8,128)(2,1)S(1)}, u32[]{:S(2)}, u32[]{:S(2)}) collective-permute-start(bf16[4,128,128]{2,1,0:T(8,128)(2,1)S(1)} %pad_maximum_fusion.2.near_ref), channel_id=1, source_target_pairs={{0,2},{1,3},{2,0},{3,1},{4,6},{5,7},{6,4},{7,5},{8,10},{9,11},{10,... | collective-permute-start | bytes 393224 | tf_op jit(solution)/shard_map/ppermute | solution.py:675
  105.8 5.9 %collective-permute-start.28 = (bf16[4,128,128]{2,1,0:T(8,128)(2,1)S(1)}, bf16[4,128,128]{2,1,0:T(8,128)(2,1)S(1)}, u32[]{:S(2)}, u32[]{:S(2)}) collective-permute-start(bf16[4,128,128]{2,1,0:T(8,128)(2,1)S(1)} %pad_maximum_fusion.2.near_ref), channel_id=1, source_target_pairs={{0,1},{1,0},{2,3},{3,2},{4,5},{5,4},{6,7},{7,6},{8,9},{9,8},{10,11... | collective-permute-start | bytes 393224 | tf_op jit(solution)/shard_map/ppermute | solution.py:675
  105.8 6.6 %collective-permute-start.29 = (bf16[4,128,128]{2,1,0:T(8,128)(2,1)S(1)}, bf16[4,128,128]{2,1,0:T(8,128)(2,1)S(1)}, u32[]{:S(2)}, u32[]{:S(2)}) collective-permute-start(bf16[4,128,128]{2,1,0:T(8,128)(2,1)S(1)} %pad_maximum_fusion.2.near_ref), channel_id=1, source_target_pairs={{0,3},{1,2},{2,1},{3,0},{4,7},{5,6},{6,5},{7,4},{8,11},{9,10},{10,... | collective-permute-start | bytes 393224 | tf_op jit(solution)/shard_map/ppermute | solution.py:675
  (18 other events, 142.2 us)
